TPU v7x, 32 devices: a whole 2x2x4 slice. The times are simulated.
32 devices in a mesh: dom: 4 (over z), sub: 8 (over y, x, core).
Axes of the slice: x: 2, y: 2, z: 4, core: 2. Of those that a mesh axis runs over, the one named last changes fastest.
Arguments:
- coefficients: float32 [9, 56, 4096], P(None, None, ('dom', 'sub')), may hold values from -6 to 6
- stiffness: float32 [3, 56, 56], replicated, may hold values from -0.75 to 0.75
- jacobians: float32 [3, 9, 9, 4096], P(None, None, None, ('dom', 'sub')), may hold values from -1.25 to 1.25
- face_proj: float32 [4, 21, 56], replicated, may hold values from -0.75 to 0.75
- neigh_proj: float32 [12, 21, 56], replicated, may hold values from -0.75 to 0.75
- lifting: float32 [4, 56, 21], replicated, may hold values from -1.25 to 1.25
- flux_local: float32 [4, 9, 9, 4096], P(None, None, None, ('dom', 'sub')), may hold values from -2 to 2
- flux_neigh: float32 [4, 9, 9, 4096], P(None, None, None, ('dom', 'sub')), may hold values from -2 to 2
- clusters: int32 [4096], P(('dom', 'sub')), may hold values from 0 to 2
- face_slots: int32 [4, 4096], P(None, ('dom', 'sub')), may hold values from 0 to 192, as said below
- orientation: int32 [4, 4096], P(None, ('dom', 'sub')), may hold values from 0 to 11
- send_list: int32 [4, 512], P(None, ('dom', 'sub')), may hold values from 0 to 127, as said below
Outputs:
- increment: float32 [9, 56, 4096], P(None, None, ('dom', 'sub'))
Inputs may be any that keep to these rules, and one draw needn't show every extreme that they name: `face_slots`: A face refers to another local element (entry below 128, never the element itself), to a received element, or to the last entry (no neighbour). Every received entry of a neighbour that exists is referred to by exactly one face of the partition; entries of neighbours that do not exist are never referred to. `send_list`: the 16 entries of one row of one partition are distinct local element numbers.
All inputs are finite; a program needn't handle non-finite values.
Results may differ from a plain program's by a relative error of at most 0.0003.
Values sent between devices are 32-bit elements; how exact they have to be, the bound alone decides.
No kernel may reach another device: no remote copies, remote signals or barrier semaphores. Data moves between devices by JAX's collectives and lax.ppermute only.
A program may use at most 192 MiB of HBM per device.

v0:
```python
import functools
import math

import jax
import jax.numpy as jnp
from jax import lax
from jax.experimental import pallas as pl
from jax.experimental.pallas import tpu as pltpu
from jax.sharding import PartitionSpec as P

ORDER = 6
ORIENTS = 12
FACES = 4
SUBSTEPS = 4
STEP_LENGTH = 0.5
GROUPS = (5, 4)
AXES = ("dom", "sub")


def swaps(doms, subs, axis, phase):
    partner = {}
    for dom in range(doms):
        for sub in range(subs):
            place = sub if axis == "sub" else dom
            count = subs if axis == "sub" else doms
            other = place + 1 if (place - phase) % 2 == 0 else place - 1
            if 0 <= other < count:
                there = (dom, other) if axis == "sub" else (other, sub)
                partner[(dom, sub)] = there
    idle = [(d, s) for d in range(doms) for s in range(subs) if (d, s) not in partner]
    for dom, sub in idle:
        for there in ((dom, sub ^ 1), (dom ^ 1, sub)):
            if (dom, sub) not in partner and there in idle and there not in partner:
                partner[(dom, sub)] = there
                partner[there] = (dom, sub)
    return [
        (dom * subs + sub, there[0] * subs + there[1])
        for (dom, sub), there in sorted(partner.items())
    ]


def rounded(values):
    return values.astype(jnp.bfloat16).astype(jnp.float32)


def stacked(values):
    high = rounded(values)
    low = values - high
    pad = jnp.zeros((8, values.shape[1]), jnp.float32)
    return jnp.concatenate([high, low, high, pad], axis=0).astype(jnp.bfloat16)


def widened(weights):
    high = rounded(weights)
    low = weights - high
    pad = jnp.zeros((weights.shape[0], 8), jnp.float32)
    return jnp.concatenate([high, high, low, pad], axis=1).astype(jnp.bfloat16)


def product(left, right):
    return jnp.dot(left, right, preferred_element_type=jnp.float32)


def directions():
    sub_odd = lax.axis_index("sub") % 2
    dom_odd = lax.axis_index("dom") % 2
    return [1 - sub_odd, sub_odd, 3 - dom_odd, 2 + dom_odd]


def time_phase(clusters, substep):
    phases = [substep % 1, substep % 2, substep % 4]
    ends = [True, (substep + 1) % 2 == 0, (substep + 1) % 4 == 0]
    phase = jnp.where(
        clusters == 0, float(phases[0]), jnp.where(clusters == 1, float(phases[1]), float(phases[2]))
    )
    done = jnp.where(
        clusters == 0, float(ends[0]), jnp.where(clusters == 1, float(ends[1]), float(ends[2]))
    )
    return phase, done


def taylor_weights(clusters, substep):
    phase, _ = time_phase(clusters, substep)
    lower = phase * STEP_LENGTH
    upper = lower + STEP_LENGTH
    weights, low_power, high_power = [], lower, upper
    for degree in range(ORDER):
        weights.append((high_power - low_power) * (1.0 / math.factorial(degree + 1)))
        low_power, high_power = low_power * lower, high_power * upper
    return weights


def series(current, jac, stiff, weights, own, first, second):
    fields, basis, cells = own.shape

    def spatial(target, start, values):
        columns = jnp.concatenate([stacked(value) for value in values], axis=1)
        target[:, start * cells : (start + len(values)) * cells] = product(stiff[...], columns)

    start = 0
    for size in GROUPS:
        values = [current(start + i) for i in range(size)]
        for i in range(size):
            own[start + i] = values[i] * weights[0]
        spatial(first, start, values)
        start += size
    source, target = first, second
    for degree in range(1, ORDER):
        start = 0
        for size in GROUPS:
            total = [None] * size
            for direction in range(3):
                for inner in range(fields):
                    value = source[
                        direction * basis : (direction + 1) * basis,
                        inner * cells : (inner + 1) * cells,
                    ]
                    for i in range(size):
                        term = jac[direction, start + i, pl.ds(inner, 1), :] * value
                        total[i] = term if total[i] is None else total[i] + term
            for i in range(size):
                own[start + i] += total[i] * weights[degree]
            if degree < ORDER - 1:
                spatial(target, start, total)
            start += size
        source, target = target, source


def pack(own, picks, messages):
    fields, basis, cells = own.shape
    rows = own[...].reshape(fields * basis, cells)
    high = rows.astype(jnp.bfloat16)
    low = (rows - high.astype(jnp.float32)).astype(jnp.bfloat16)
    picked = product(jnp.concatenate([high, low], axis=1), picks[...])
    entries = cells // (fields - 1)
    lane = lax.broadcasted_iota(jnp.int32, (1, cells), 1) // entries
    for exchange, message in enumerate(messages):
        columns = slice(exchange * cells, (exchange + 1) * cells)
        main = picked[0:basis, columns]
        for field in range(1, fields - 1):
            main = jnp.where(lane == field, picked[field * basis : (field + 1) * basis, columns], main)
        message[0:basis, :] = main
        last = (fields - 1) * basis
        rest = picked[last : last + 8, columns]
        for tile in range(1, basis // 8):
            rest = jnp.where(
                lane == tile, picked[last + tile * 8 : last + tile * 8 + 8, columns], rest
            )
        message[basis : basis + 8, :] = rest


def start_kernel(
    coefficients, jac, stiffness, clusters, sends,
    own, message_0, message_1, message_2, message_3, stiff, picks,
    first, second,
):
    fields, basis, cells = own.shape
    stiff[...] = widened(-stiffness[...].reshape(3 * basis, basis))
    entries = sends.shape[1]
    rows = directions()
    places = []
    for row in rows:
        entry_row = sends[pl.ds(row, 1), :]
        places += [entry_row] * (cells // entries)
    place = jnp.concatenate(places, axis=1)
    element = lax.broadcasted_iota(jnp.int32, (cells, place.shape[1]), 0)
    hot = jnp.where(element == place, 1.0, 0.0).astype(jnp.bfloat16)
    picks[0:cells, :] = hot
    picks[cells : 2 * cells, :] = hot
    weights = taylor_weights(clusters[...], 0)
    series(lambda field: coefficients[field], jac, stiff, weights, own, first, second)
    pack(own, picks, (message_0, message_1, message_2, message_3))


def local_kernel(own, jac, flux_local, matrices, local_hot, volume, local_flux, traces, spatial):
    fields, basis, cells = own.shape
    wide = traces.shape[0] // fields
    columns = jnp.concatenate([stacked(own[field]) for field in range(fields)], axis=1)
    spatial[...] = product(matrices[...], columns)
    start = 0
    for size in GROUPS:
        total = [None] * size
        for direction in range(3):
            for inner in range(fields):
                value = spatial[
                    direction * basis : (direction + 1) * basis,
                    inner * cells : (inner + 1) * cells,
                ]
                for i in range(size):
                    term = jac[direction, start + i, pl.ds(inner, 1), :] * value
                    total[i] = term if total[i] is None else total[i] + term
        for i in range(size):
            volume[start + i] = total[i]
        start += size
    base = 3 * basis
    for face in range(FACES):
        total = [None] * fields
        for inner in range(fields):
            value = spatial[
                base + face * wide : base + (face + 1) * wide, inner * cells : (inner + 1) * cells
            ]
            for outer in range(fields):
                term = flux_local[face, outer, pl.ds(inner, 1), :] * value
                total[outer] = term if total[outer] is None else total[outer] + term
        for outer in range(fields):
            local_flux[face, outer] = total[outer]
    base += FACES * wide
    highs, lows = [], []
    for pair in range(ORIENTS):
        rows = slice(base + pair * wide, base + (pair + 1) * wide)
        values = jnp.concatenate(
            [spatial[rows, field * cells : (field + 1) * cells] for field in range(fields)], axis=0
        )
        high = rounded(values)
        highs.append(high)
        lows.append(values - high)
    left = jnp.concatenate(
        [jnp.concatenate(highs, axis=1), jnp.concatenate(lows, axis=1)], axis=0
    ).astype(jnp.bfloat16)
    both = product(left, local_hot[...])
    half = fields * wide
    traces[...] = both[:half] + both[half:]


def first_local_kernel(
    own, jac, flux_local, stiffness, face_proj, neigh_proj, lifting, slots, orientation,
    volume, local_flux, traces, matrices, local_hot, halo_hot, halo_pairs, lift,
    spatial, plain,
):
    fields, basis, cells = own.shape
    face_basis = face_proj.shape[1]
    wide = traces.shape[0] // fields
    plain[...] = jnp.zeros_like(plain)
    for direction in range(3):
        plain[direction * basis : (direction + 1) * basis, :] = stiffness[direction].T
    row = 3 * basis
    for face in range(FACES):
        plain[row : row + face_basis, :] = face_proj[face]
        row += wide
    for pair in range(ORIENTS):
        plain[row : row + face_basis, :] = neigh_proj[pair]
        row += wide
    matrices[...] = widened(plain[...])
    empty = jnp.zeros((basis, wide - face_basis), jnp.float32)
    parts = []
    for face in range(FACES):
        parts += [lifting[face], empty]
    lift_plain = jnp.concatenate(parts, axis=1)
    lift_high = rounded(lift_plain)
    lift[...] = jnp.concatenate([lift_high, lift_high, lift_plain - lift_high], axis=1).astype(
        jnp.bfloat16
    )
    slot_row = jnp.concatenate([slots[face : face + 1, :] for face in range(FACES)], axis=1)
    pair_row = jnp.concatenate([orientation[face : face + 1, :] for face in range(FACES)], axis=1)
    element = lax.broadcasted_iota(jnp.int32, (cells, FACES * cells), 0)
    hit = jnp.where(element == slot_row, pair_row, -1)
    for pair in range(ORIENTS):
        local_hot[pair * cells : (pair + 1) * cells, :] = jnp.where(hit == pair, 1.0, 0.0).astype(
            jnp.bfloat16
        )
    entries = cells // (fields - 1)
    rows = directions()
    keys = [cells + row * entries for row in rows]
    entry = lax.broadcasted_iota(jnp.int32, (cells, 1), 0)
    for exchange in range(4):
        key = keys[exchange] + entry % entries
        halo_hot[exchange * cells : (exchange + 1) * cells, :] = jnp.where(
            slot_row == key, 1.0, 0.0
        ).astype(jnp.bfloat16)
    key = jnp.full((cells, 1), -1, jnp.int32)
    for exchange in range(4):
        key = jnp.where(entry // entries == exchange, keys[exchange] + entry % entries, key)
    halo_hot[4 * cells : 5 * cells, :] = jnp.where(slot_row == key, 1.0, 0.0).astype(jnp.bfloat16)
    pair_rows = jnp.broadcast_to(pair_row.astype(jnp.float32), (8, FACES * cells))
    halo_pairs[...] = lax.dot_general(
        pair_rows.astype(jnp.bfloat16),
        halo_hot[...],
        (((1,), (1,)), ((), ())),
        preferred_element_type=jnp.float32,
    )
    local_kernel(own, jac, flux_local, matrices, local_hot, volume, local_flux, traces, spatial)


def remote_part(messages, matrices, halo_hot, halo_pairs, traces):
    cells = messages[0].shape[1]
    basis = messages[0].shape[0] - 8
    half = traces.shape[0]
    wide = (matrices.shape[0] - 3 * basis) // (FACES + ORIENTS)
    fields = half // wide
    entries = cells // (fields - 1)
    lane = lax.broadcasted_iota(jnp.int32, (1, cells), 1) // entries
    last = []
    for tile in range(basis // 8):
        total = jnp.zeros((8, cells), jnp.float32)
        for exchange in range(4):
            value = messages[exchange][basis : basis + 8, :]
            shift = ((exchange - tile) * entries) % cells
            if shift:
                value = pltpu.roll(value, shift, 1)
            total = jnp.where(lane == exchange, value, total)
        last.append(total)
    parts = [message[0:basis, :] for message in messages] + [jnp.concatenate(last, axis=0)]
    columns = jnp.concatenate([stacked(part) for part in parts], axis=1)
    base = 3 * basis + FACES * wide
    projected = product(matrices[base:, :], columns)
    pair_row = halo_pairs[0:1, :]
    chosen = projected[0:wide, :]
    for pair in range(1, ORIENTS):
        chosen = jnp.where(
            pair_row == float(pair), projected[pair * wide : (pair + 1) * wide, :], chosen
        )
    high = rounded(chosen)
    low = chosen - high
    left = []
    for part in (high, low):
        for field in range(fields - 1):
            left.append(
                jnp.concatenate(
                    [
                        jnp.where(lane == field, part[:, c * cells : (c + 1) * cells], 0.0)
                        for c in range(4)
                    ],
                    axis=1,
                )
            )
    most = (fields - 1) * wide
    both = product(jnp.concatenate(left, axis=0).astype(jnp.bfloat16), halo_hot[0 : 4 * cells, :])
    tail = jnp.concatenate([high[:, 4 * cells :], low[:, 4 * cells :]], axis=0)
    both_tail = product(tail.astype(jnp.bfloat16), halo_hot[4 * cells :, :])
    return (
        traces[0:most, :] + both[:most] + both[most:],
        traces[most:, :] + both_tail[:wide] + both_tail[wide:],
    )


def change(remote, volume, local_flux, flux_neigh, lift):
    main, tail = remote
    fields, _, cells = volume.shape
    wide = local_flux.shape[2]
    rows = []
    for face in range(FACES):
        total = [local_flux[face, outer] for outer in range(fields)]
        for inner in range(fields):
            source = main[inner * wide : (inner + 1) * wide] if inner < fields - 1 else tail
            value = source[:, face * cells : (face + 1) * cells]
            for outer in range(fields):
                total[outer] = total[outer] + flux_neigh[face, outer, pl.ds(inner, 1), :] * value
        rows.append(jnp.concatenate(total, axis=1))
    flux = jnp.concatenate(rows, axis=0)
    high = rounded(flux)
    right = jnp.concatenate([high, flux - high, high], axis=0).astype(jnp.bfloat16)
    lifted = product(lift[...], right)
    return [volume[p] - lifted[:, p * cells : (p + 1) * cells] for p in range(fields)]


def step_kernel(
    substep,
    coefficients, applied_in, pending_in, jac, stiff, clusters, picks,
    in_0, in_1, in_2, in_3,
    volume, local_flux, traces, flux_neigh, matrices, halo_hot, halo_pairs, lift,
    applied, pending, own, message_0, message_1, message_2, message_3,
    first, second,
):
    fields = volume.shape[0]
    remote = remote_part((in_0, in_1, in_2, in_3), matrices, halo_hot, halo_pairs, traces)
    updates = change(remote, volume, local_flux, flux_neigh, lift)
    _, done = time_phase(clusters[...], substep)
    finished = done > 0.5
    for field in range(fields):
        waiting = updates[field]
        if substep > 0:
            waiting = waiting + pending_in[field]
        passed = jnp.where(finished, waiting, 0.0)
        applied[field] = passed + applied_in[field] if substep > 0 else passed
        pending[field] = jnp.where(finished, 0.0, waiting)
    weights = taylor_weights(clusters[...], substep + 1)
    series(
        lambda field: coefficients[field] + applied[field], jac, stiff, weights, own, first, second
    )
    pack(own, picks, (message_0, message_1, message_2, message_3))


def last_kernel(
    applied_in, pending_in,
    in_0, in_1, in_2, in_3,
    volume, local_flux, traces, flux_neigh, matrices, halo_hot, halo_pairs, lift,
    increment,
):
    remote = remote_part((in_0, in_1, in_2, in_3), matrices, halo_hot, halo_pairs, traces)
    updates = change(remote, volume, local_flux, flux_neigh, lift)
    for field in range(volume.shape[0]):
        increment[field] = applied_in[field] + (pending_in[field] + updates[field])


def call(kernel, outs, scratch, flops, *operands):
    block = pl.BlockSpec(memory_space=pltpu.VMEM)
    return pl.pallas_call(
        kernel,
        out_shape=outs,
        in_specs=[block] * len(operands),
        out_specs=[block] * len(outs),
        scratch_shapes=[pltpu.VMEM(shape, jnp.float32) for shape in scratch],
        compiler_params=pltpu.CompilerParams(vmem_limit_bytes=40 << 20),
        cost_estimate=pl.CostEstimate(flops=flops, bytes_accessed=1 << 20, transcendentals=0),
    )(*operands)


def on_device(
    coefficients, stiffness, jacobians, face_proj, neigh_proj, lifting,
    flux_local, flux_neigh, clusters, face_slots, orientation, send_list, *, doms, subs,
):
    fields, basis, cells = coefficients.shape
    wide = -(-face_proj.shape[1] // 8) * 8
    clusters = clusters.reshape(1, cells)
    exchanges = [
        swaps(doms, subs, axis, phase) for axis in ("sub", "dom") for phase in (0, 1)
    ]

    def f32(*shape):
        return jax.ShapeDtypeStruct(shape, jnp.float32)

    def bf16(*shape):
        return jax.ShapeDtypeStruct(shape, jnp.bfloat16)

    state = f32(fields, basis, cells)
    message = f32(basis + 8, cells)
    depth = 3 * basis + 8
    rows = 3 * basis + (FACES + ORIENTS) * wide
    derived = (3 * basis, fields * cells)
    faces = FACES * cells

    def exchange(messages):
        return [lax.ppermute(m, AXES, pairs) for m, pairs in zip(messages, exchanges)]

    own, *messages, stiff, picks = call(
        start_kernel,
        [state] + [message] * 4 + [bf16(3 * basis, depth), bf16(2 * cells, 4 * cells)],
        [derived, derived], 1 << 27,
        coefficients, jacobians, stiffness, clusters, send_list,
    )
    local_outs = [state, f32(FACES, fields, wide, cells), f32(fields * wide, faces)]
    applied = pending = coefficients
    for substep in range(SUBSTEPS):
        received = exchange(messages)
        if substep == 0:
            volume, local_flux, traces, matrices, local_hot, halo_hot, halo_pairs, lift = call(
                first_local_kernel,
                local_outs
                + [
                    bf16(rows, depth), bf16(ORIENTS * cells, faces), bf16(5 * cells, faces),
                    f32(8, 5 * cells), bf16(basis, 3 * FACES * wide),
                ],
                [(rows, fields * cells), (rows, basis)], 1 << 27,
                own, jacobians, flux_local, stiffness, face_proj, neigh_proj, lifting,
                face_slots, orientation,
            )
        else:
            volume, local_flux, traces = call(
                local_kernel, local_outs, [(rows, fields * cells)], 1 << 27,
                own, jacobians, flux_local, matrices, local_hot,
            )
        rest = (
            *received, volume, local_flux, traces, flux_neigh, matrices, halo_hot, halo_pairs, lift,
        )
        if substep < SUBSTEPS - 1:
            applied, pending, own, *messages = call(
                functools.partial(step_kernel, substep),
                [state] * 3 + [message] * 4, [derived, derived], 1 << 27,
                coefficients, applied, pending, jacobians, stiff, clusters, picks, *rest,
            )
        else:
            (increment,) = call(last_kernel, [state], [], 1 << 27, applied, pending, *rest)
    return increment


def solution(mesh):
    split = ("dom", "sub")
    placed = (
        P(None, None, split), P(), P(None, None, None, split), P(), P(), P(),
        P(None, None, None, split), P(None, None, None, split), P(split),
        P(None, split), P(None, split), P(None, split),
    )
    return jax.shard_map(
        functools.partial(on_device, doms=mesh.shape["dom"], subs=mesh.shape["sub"]),
        mesh=mesh,
        in_specs=placed,
        out_specs=P(None, None, split),
        check_vma=False,
    )
```

profile of v0, /device:TPU:0, one launch (start us, length us, event | category | flops | bytes accessed | tf_op | source)
XLA Modules:
  0.0 52.8 jit_solution(16123637343585584997)
XLA Ops:
  0.0 1.0 %copy.18.jac = f32[3,9,9,128]{3,2,1,0:T(8,128)S(1)} copy(f32[3,9,9,128]{3,0,2,1:T(4,128)} %param.14) | data formatting | bytes 248832 | tf_op args[2]
  1.0 0.9 %copy-done = f32[9,56,128]{2,1,0:T(8,128)S(1)} copy-done((f32[9,56,128]{2,1,0:T(8,128)S(1)}, f32[9,56,128]{2,1,0:T(8,128)}, u32[]{:S(2)}) %copy-start) | copy-done | bytes 258072
  2.0 0.9 %copy-done.2 = f32[3,56,56]{2,1,0:T(8,128)S(1)} copy-done((f32[3,56,56]{2,1,0:T(8,128)S(1)}, f32[3,56,56]{2,1,0:T(8,128)}, u32[]{:S(2)}) %copy-start.2) | copy-done | bytes 37656
  2.9 0.7 %copy-done.5 = s32[128]{0:T(128)S(1)} copy-done((s32[128]{0:T(128)S(1)}, s32[128]{0:T(128)}, u32[]{:S(2)}) %copy-start.5) | copy-done | bytes 536
  3.5 0.7 %copy-done.9 = s32[4,16]{1,0:T(4,128)S(1)} copy-done((s32[4,16]{1,0:T(4,128)S(1)}, s32[4,16]{1,0:T(4,128)}, u32[]{:S(2)}) %copy-start.9) | copy-done | bytes 280
  4.2 3.7 %shard_map.118 = (f32[9,56,128]{2,1,0:T(8,128)S(1)}, f32[64,128]{1,0:T(8,128)S(1)}, f32[64,128]{1,0:T(8,128)S(1)}, f32[64,128]{1,0:T(8,128)S(1)}, f32[64,128]{1,...) custom-call(f32[9,56,128]{2,1,0:T(8,128)S(1)} %copy-done, f32[3,9,9,128]{3,2,1,0:T(8,128)S(1)} %copy.18.jac, ...), custom_call_target="tpu_custom_call" | custom-call | flops 134217728 | bytes 1048576 | tf_op jit(solution)/shard_map/pallas_call | solution.py:397
  7.9 0.5 %collective-permute-start = (f32[64,128]{1,0:T(8,128)S(1)}, f32[64,128]{1,0:T(8,128)S(1)}, u32[]{:S(2)}, u32[]{:S(2)}) collective-permute-start(f32[64,128]{1,0:T(8,128)S(1)} %get-tuple-element.52), channel_id=1, source_target_pairs={{0,1},{1,0},{2,3},{3,2},{4,5},{5,4},{6,7},{7,6},{8,9},{9,8},{10,11... | collective-permute-start | bytes 98312 | tf_op jit(solution)/shard_map/ppermute | solution.py:433
  8.4 2.7 %collective-permute-start.1 = (f32[64,128]{1,0:T(8,128)S(1)}, f32[64,128]{1,0:T(8,128)S(1)}, u32[]{:S(2)}, u32[]{:S(2)}) collective-permute-start(f32[64,128]{1,0:T(8,128)S(1)} %get-tuple-element.53), channel_id=1, source_target_pairs={{0,8},{1,2},{2,1},{3,4},{4,3},{5,6},{6,5},{7,15},{8,0},{9,10},{10,... | collective-permute-start | bytes 98312 | tf_op jit(solution)/shard_map/ppermute | solution.py:433
  11.1 0.1 collective-permute-start.2
  11.2 1.2 %collective-permute-start.3 = (f32[64,128]{1,0:T(8,128)S(1)}, f32[64,128]{1,0:T(8,128)S(1)}, u32[]{:S(2)}, u32[]{:S(2)}) collective-permute-start(f32[64,128]{1,0:T(8,128)S(1)} %get-tuple-element.55), channel_id=1, source_target_pairs={{0,1},{1,0},{2,3},{3,2},{4,5},{5,4},{6,7},{7,6},{8,16},{9,17},{10,... | collective-permute-start | bytes 98312 | tf_op jit(solution)/shard_map/ppermute | solution.py:433
  12.4 0.8 %copy.16.face_proj = f32[4,21,56]{2,1,0:T(8,128)S(1)} copy(f32[4,21,56]{2,0,1:T(4,128)} %param.15) | data formatting | bytes 37632 | tf_op args[3]
  13.2 0.9 %copy.17.lifting = f32[4,56,21]{2,1,0:T(8,128)S(1)} copy(f32[4,56,21]{1,0,2:T(4,128)} %param.17) | data formatting | bytes 37632 | tf_op args[5]
  14.1 0.9 %copy.15.flux_local = f32[4,9,9,128]{3,2,1,0:T(8,128)S(1)} copy(f32[4,9,9,128]{3,0,2,1:T(4,128)} %param.18) | data formatting | bytes 331776 | tf_op args[6]
  15.1 0.9 %copy.19.flux_neigh = f32[4,9,9,128]{3,2,1,0:T(8,128)S(1)} copy(f32[4,9,9,128]{3,0,2,1:T(4,128)} %param.19) | data formatting | bytes 331776 | tf_op args[7]
  16.0 2.2 %shard_map.119 = (f32[9,56,128]{2,1,0:T(8,128)S(1)}, f32[4,9,24,128]{3,2,1,0:T(8,128)S(1)}, f32[216,512]{1,0:T(8,128)S(1)}, bf16[552,176]{1,0:T(8,128)(2,1)S(1)}...) custom-call(f32[9,56,128]{2,1,0:T(8,128)S(1)} %get-tuple-element.56., ...), custom_call_target="tpu_custom_call" | custom-call | flops 134217728 | bytes 1048576 | tf_op jit(solution)/shard_map/pallas_call | solution.py:397
  18.3 4.5 %shard_map.120 = (f32[9,56,128]{2,1,0:T(8,128)S(1)}, f32[9,56,128]{2,1,0:T(8,128)S(1)}, f32[9,56,128]{2,1,0:T(8,128)S(1)}, f32[64,128]{1,0:T(8,128)S(1)}, f32[64...) custom-call(f32[9,56,128]{2,1,0:T(8,128)S(1)} %copy-done.1, f32[9,56,128]{2,1,0:T(8,128)S(1)} %copy-done.1, ...), custom_call_target="tpu_custom_call" | custom-call | flops 134217728 | bytes 1048576 | tf_op jit(solution)/shard_map/pallas_call | solution.py:397
  23.0 2.9 %collective-permute-start.5 = (f32[64,128]{1,0:T(8,128)S(1)}, f32[64,128]{1,0:T(8,128)S(1)}, u32[]{:S(2)}, u32[]{:S(2)}) collective-permute-start(f32[64,128]{1,0:T(8,128)S(1)} %get-tuple-element.67), channel_id=1, source_target_pairs={{0,8},{1,2},{2,1},{3,4},{4,3},{5,6},{6,5},{7,15},{8,0},{9,10},{10,... | collective-permute-start | bytes 98312 | tf_op jit(solution)/shard_map/ppermute | solution.py:433
  25.9 1.3 %collective-permute-start.7 = (f32[64,128]{1,0:T(8,128)S(1)}, f32[64,128]{1,0:T(8,128)S(1)}, u32[]{:S(2)}, u32[]{:S(2)}) collective-permute-start(f32[64,128]{1,0:T(8,128)S(1)} %get-tuple-element.69), channel_id=1, source_target_pairs={{0,1},{1,0},{2,3},{3,2},{4,5},{5,4},{6,7},{7,6},{8,16},{9,17},{10,... | collective-permute-start | bytes 98312 | tf_op jit(solution)/shard_map/ppermute | solution.py:433
  27.1 2.1 %shard_map.121 = (f32[9,56,128]{2,1,0:T(8,128)S(1)}, f32[4,9,24,128]{3,2,1,0:T(8,128)S(1)}, f32[216,512]{1,0:T(8,128)S(1)}) custom-call(f32[9,56,128]{2,1,0:T(8,128)S(1)} %get-tuple-element.70.own, f32[3,9,9,128]{3,2,1,0:T(8,128)S(1)} %copy.18.jac, f32[4,9,9,128]{3,2,1,0:T(8,128)S(1)} %copy.15.flux_local, bf16[552,176]{1,0:T(8,128)(2,1)S(1)} %get-tuple-element.60.matrices, ...), custom_call_target="tpu_custom_call" | custom-call | flops 134217728 | bytes 1048576 | tf_op jit(solution)/shard_map/pallas_call | solution.py:397
  29.3 0.5 collective-permute-done.6.in_2
  29.7 4.5 %shard_map.122 = (f32[9,56,128]{2,1,0:T(8,128)S(1)}, f32[9,56,128]{2,1,0:T(8,128)S(1)}, f32[9,56,128]{2,1,0:T(8,128)S(1)}, f32[64,128]{1,0:T(8,128)S(1)}, f32[64...) custom-call(f32[9,56,128]{2,1,0:T(8,128)S(1)} %copy-done.1, ...), custom_call_target="tpu_custom_call" | custom-call | flops 134217728 | bytes 1048576 | tf_op jit(solution)/shard_map/pallas_call | solution.py:397
  34.4 2.1 %collective-permute-start.9 = (f32[64,128]{1,0:T(8,128)S(1)}, f32[64,128]{1,0:T(8,128)S(1)}, u32[]{:S(2)}, u32[]{:S(2)}) collective-permute-start(f32[64,128]{1,0:T(8,128)S(1)} %get-tuple-element.78), channel_id=1, source_target_pairs={{0,8},{1,2},{2,1},{3,4},{4,3},{5,6},{6,5},{7,15},{8,0},{9,10},{10,... | collective-permute-start | bytes 98312 | tf_op jit(solution)/shard_map/ppermute | solution.py:433
  36.4 0.1 collective-permute-start.10
  36.5 0.1 collective-permute-start.11
  36.6 2.0 %shard_map.123 = (f32[9,56,128]{2,1,0:T(8,128)S(1)}, f32[4,9,24,128]{3,2,1,0:T(8,128)S(1)}, f32[216,512]{1,0:T(8,128)S(1)}) custom-call(f32[9,56,128]{2,1,0:T(8,128)S(1)} %get-tuple-element.81.own, f32[3,9,9,128]{3,2,1,0:T(8,128)S(1)} %copy.18.jac, f32[4,9,9,128]{3,2,1,0:T(8,128)S(1)} %copy.15.flux_local, bf16[552,176]{1,0:T(8,128)(2,1)S(1)} %get-tuple-element.60.matrices, ...), custom_call_target="tpu_custom_call" | custom-call | flops 134217728 | bytes 1048576 | tf_op jit(solution)/shard_map/pallas_call | solution.py:397
  38.6 1.7 %collective-permute-done.10.in_2 = f32[64,128]{1,0:T(8,128)S(1)} collective-permute-done((f32[64,128]{1,0:T(8,128)S(1)}, f32[64,128]{1,0:T(8,128)S(1)}, u32[]{:S(2)}, u32[]{:S(2)}) %collective-permute-start.10) | collective-permute-done | bytes 32800 | tf_op jit(solution)/shard_map/ppermute | solution.py:433
  40.4 4.5 %shard_map.124 = (f32[9,56,128]{2,1,0:T(8,128)S(1)}, f32[9,56,128]{2,1,0:T(8,128)S(1)}, f32[9,56,128]{2,1,0:T(8,128)S(1)}, f32[64,128]{1,0:T(8,128)S(1)}, f32[64...) custom-call(f32[9,56,128]{2,1,0:T(8,128)S(1)} %copy-done.1, ...), custom_call_target="tpu_custom_call" | custom-call | flops 134217728 | bytes 1048576 | tf_op jit(solution)/shard_map/pallas_call | solution.py:397
  45.0 2.1 %collective-permute-start.13 = (f32[64,128]{1,0:T(8,128)S(1)}, f32[64,128]{1,0:T(8,128)S(1)}, u32[]{:S(2)}, u32[]{:S(2)}) collective-permute-start(f32[64,128]{1,0:T(8,128)S(1)} %get-tuple-element.88), channel_id=1, source_target_pairs={{0,8},{1,2},{2,1},{3,4},{4,3},{5,6},{6,5},{7,15},{8,0},{9,10},{10,... | collective-permute-start | bytes 98312 | tf_op jit(solution)/shard_map/ppermute | solution.py:433
  47.1 0.1 collective-permute-start.14
  47.2 1.9 %shard_map.125 = (f32[9,56,128]{2,1,0:T(8,128)S(1)}, f32[4,9,24,128]{3,2,1,0:T(8,128)S(1)}, f32[216,512]{1,0:T(8,128)S(1)}) custom-call(f32[9,56,128]{2,1,0:T(8,128)S(1)} %get-tuple-element.91.own, f32[3,9,9,128]{3,2,1,0:T(8,128)S(1)} %copy.18.jac, f32[4,9,9,128]{3,2,1,0:T(8,128)S(1)} %copy.15.flux_local, bf16[552,176]{1,0:T(8,128)(2,1)S(1)} %get-tuple-element.60.matrices, ...), custom_call_target="tpu_custom_call" | custom-call | flops 134217728 | bytes 1048576 | tf_op jit(solution)/shard_map/pallas_call | solution.py:397
  49.2 1.8 %collective-permute-done.14.in_2 = f32[64,128]{1,0:T(8,128)S(1)} collective-permute-done((f32[64,128]{1,0:T(8,128)S(1)}, f32[64,128]{1,0:T(8,128)S(1)}, u32[]{:S(2)}, u32[]{:S(2)}) %collective-permute-start.14) | collective-permute-done | bytes 32800 | tf_op jit(solution)/shard_map/ppermute | solution.py:433
  51.0 1.8 %shard_map.126 = f32[9,56,128]{2,1,0:T(8,128)} custom-call(f32[9,56,128]{2,1,0:T(8,128)S(1)} %get-tuple-element.85.applied_in, f32[9,56,128]{2,1,0:T(8,128)S(1)} %get-tuple-element.86.pending_in, f32[64,128]{1,0:T(8,128)S(1)} %collective-permute-done.12.in_0, f32[64,128]{1,0:T(8,128)S(1)} %collective-permute-done.13.in_1, ...), custom_call_target="tpu_custom_call" | custom-call | flops 134217728 | bytes 1048576 | tf_op jit(solution)/shard_map/pallas_call | solution.py:397
  (34 shorter events, 0.4 us)
Async XLA Ops:
  0.0 18.3 %copy-start.1 = (f32[9,56,128]{2,1,0:T(8,128)S(1)}, f32[9,56,128]{2,1,0:T(8,128)}, u32[]{:S(2)}) copy-start(f32[9,56,128]{2,1,0:T(8,128)} %coefficients.7) | copy-start | bytes 774148
  0.0 16.0 %copy-start.3 = (f32[3,56,56]{2,1,0:T(8,128)S(1)}, f32[3,56,56]{2,1,0:T(8,128)}, u32[]{:S(2)}) copy-start(f32[3,56,56]{2,1,0:T(8,128)} %stiffness.3) | copy-start | bytes 112900
  0.0 18.3 %copy-start.6 = (s32[128]{0:T(128)S(1)}, s32[128]{0:T(128)}, u32[]{:S(2)}) copy-start(s32[128]{0:T(128)} %param.20) | copy-start | bytes 1540
  0.0 16.0 %copy-start.8 = (s32[4,128]{1,0:T(4,128)S(1)}, s32[4,128]{1,0:T(4,128)}, u32[]{:S(2)}) copy-start(s32[4,128]{1,0:T(4,128)} %orientation.1) | copy-start | bytes 6148
  0.0 16.0 %copy-start.7 = (s32[4,128]{1,0:T(4,128)S(1)}, s32[4,128]{1,0:T(4,128)}, u32[]{:S(2)}) copy-start(s32[4,128]{1,0:T(4,128)} %slots.1) | copy-start | bytes 6148
  1.0 1.0 %copy-start = (f32[9,56,128]{2,1,0:T(8,128)S(1)}, f32[9,56,128]{2,1,0:T(8,128)}, u32[]{:S(2)}) copy-start(f32[9,56,128]{2,1,0:T(8,128)} %coefficients.7) | copy-start | bytes 774148
  2.0 0.9 %copy-start.2 = (f32[3,56,56]{2,1,0:T(8,128)S(1)}, f32[3,56,56]{2,1,0:T(8,128)}, u32[]{:S(2)}) copy-start(f32[3,56,56]{2,1,0:T(8,128)} %stiffness.3) | copy-start | bytes 112900
  2.8 0.7 %copy-start.5 = (s32[128]{0:T(128)S(1)}, s32[128]{0:T(128)}, u32[]{:S(2)}) copy-start(s32[128]{0:T(128)} %param.20) | copy-start | bytes 1540
  3.5 0.7 %copy-start.9 = (s32[4,16]{1,0:T(4,128)S(1)}, s32[4,16]{1,0:T(4,128)}, u32[]{:S(2)}) copy-start(s32[4,16]{1,0:T(4,128)} %sends.1) | copy-start | bytes 772
  4.2 11.9 %copy-start.4 = (f32[12,21,56]{2,1,0:T(8,128)S(1)}, f32[12,21,56]{2,1,0:T(8,128)}, u32[]{:S(2)}) copy-start(f32[12,21,56]{2,1,0:T(8,128)} %neigh_proj.1) | copy-start | bytes 169348
  7.9 10.4 %collective-permute-start = (f32[64,128]{1,0:T(8,128)S(1)}, f32[64,128]{1,0:T(8,128)S(1)}, u32[]{:S(2)}, u32[]{:S(2)}) collective-permute-start(f32[64,128]{1,0:T(8,128)S(1)} %get-tuple-element.52), channel_id=1, source_target_pairs={{0,1},{1,0},{2,3},{3,2},{4,5},{5,4},{6,7},{7,6},{8,9},{9,8},{10,11... | collective-permute-start | bytes 98312 | tf_op jit(solution)/shard_map/ppermute | solution.py:433
  8.4 9.8 %collective-permute-start.1 = (f32[64,128]{1,0:T(8,128)S(1)}, f32[64,128]{1,0:T(8,128)S(1)}, u32[]{:S(2)}, u32[]{:S(2)}) collective-permute-start(f32[64,128]{1,0:T(8,128)S(1)} %get-tuple-element.53), channel_id=1, source_target_pairs={{0,8},{1,2},{2,1},{3,4},{4,3},{5,6},{6,5},{7,15},{8,0},{9,10},{10,... | collective-permute-start | bytes 98312 | tf_op jit(solution)/shard_map/ppermute | solution.py:433
  11.1 7.2 %collective-permute-start.2 = (f32[64,128]{1,0:T(8,128)S(1)}, f32[64,128]{1,0:T(8,128)S(1)}, u32[]{:S(2)}, u32[]{:S(2)}) collective-permute-start(f32[64,128]{1,0:T(8,128)S(1)} %get-tuple-element.54), channel_id=1, source_target_pairs={{0,8},{1,9},{2,10},{3,11},{4,12},{5,13},{6,14},{7,15},{8,0},{9,1},... | collective-permute-start | bytes 98312 | tf_op jit(solution)/shard_map/ppermute | solution.py:433
  11.2 7.1 %collective-permute-start.3 = (f32[64,128]{1,0:T(8,128)S(1)}, f32[64,128]{1,0:T(8,128)S(1)}, u32[]{:S(2)}, u32[]{:S(2)}) collective-permute-start(f32[64,128]{1,0:T(8,128)S(1)} %get-tuple-element.55), channel_id=1, source_target_pairs={{0,1},{1,0},{2,3},{3,2},{4,5},{5,4},{6,7},{7,6},{8,16},{9,17},{10,... | collective-permute-start | bytes 98312 | tf_op jit(solution)/shard_map/ppermute | solution.py:433
  22.9 6.4 %collective-permute-start.4 = (f32[64,128]{1,0:T(8,128)S(1)}, f32[64,128]{1,0:T(8,128)S(1)}, u32[]{:S(2)}, u32[]{:S(2)}) collective-permute-start(f32[64,128]{1,0:T(8,128)S(1)} %get-tuple-element.66), channel_id=1, source_target_pairs={{0,1},{1,0},{2,3},{3,2},{4,5},{5,4},{6,7},{7,6},{8,9},{9,8},{10,11... | collective-permute-start | bytes 98312 | tf_op jit(solution)/shard_map/ppermute | solution.py:433
  23.0 6.3 %collective-permute-start.5 = (f32[64,128]{1,0:T(8,128)S(1)}, f32[64,128]{1,0:T(8,128)S(1)}, u32[]{:S(2)}, u32[]{:S(2)}) collective-permute-start(f32[64,128]{1,0:T(8,128)S(1)} %get-tuple-element.67), channel_id=1, source_target_pairs={{0,8},{1,2},{2,1},{3,4},{4,3},{5,6},{6,5},{7,15},{8,0},{9,10},{10,... | collective-permute-start | bytes 98312 | tf_op jit(solution)/shard_map/ppermute | solution.py:433
  25.8 3.9 %collective-permute-start.6 = (f32[64,128]{1,0:T(8,128)S(1)}, f32[64,128]{1,0:T(8,128)S(1)}, u32[]{:S(2)}, u32[]{:S(2)}) collective-permute-start(f32[64,128]{1,0:T(8,128)S(1)} %get-tuple-element.68), channel_id=1, source_target_pairs={{0,8},{1,9},{2,10},{3,11},{4,12},{5,13},{6,14},{7,15},{8,0},{9,1},... | collective-permute-start | bytes 98312 | tf_op jit(solution)/shard_map/ppermute | solution.py:433
  25.9 3.9 %collective-permute-start.7 = (f32[64,128]{1,0:T(8,128)S(1)}, f32[64,128]{1,0:T(8,128)S(1)}, u32[]{:S(2)}, u32[]{:S(2)}) collective-permute-start(f32[64,128]{1,0:T(8,128)S(1)} %get-tuple-element.69), channel_id=1, source_target_pairs={{0,1},{1,0},{2,3},{3,2},{4,5},{5,4},{6,7},{7,6},{8,16},{9,17},{10,... | collective-permute-start | bytes 98312 | tf_op jit(solution)/shard_map/ppermute | solution.py:433
  34.3 4.3 %collective-permute-start.8 = (f32[64,128]{1,0:T(8,128)S(1)}, f32[64,128]{1,0:T(8,128)S(1)}, u32[]{:S(2)}, u32[]{:S(2)}) collective-permute-start(f32[64,128]{1,0:T(8,128)S(1)} %get-tuple-element.77), channel_id=1, source_target_pairs={{0,1},{1,0},{2,3},{3,2},{4,5},{5,4},{6,7},{7,6},{8,9},{9,8},{10,11... | collective-permute-start | bytes 98312 | tf_op jit(solution)/shard_map/ppermute | solution.py:433
  34.4 4.2 %collective-permute-start.9 = (f32[64,128]{1,0:T(8,128)S(1)}, f32[64,128]{1,0:T(8,128)S(1)}, u32[]{:S(2)}, u32[]{:S(2)}) collective-permute-start(f32[64,128]{1,0:T(8,128)S(1)} %get-tuple-element.78), channel_id=1, source_target_pairs={{0,8},{1,2},{2,1},{3,4},{4,3},{5,6},{6,5},{7,15},{8,0},{9,10},{10,... | collective-permute-start | bytes 98312 | tf_op jit(solution)/shard_map/ppermute | solution.py:433
  36.4 3.9 %collective-permute-start.10 = (f32[64,128]{1,0:T(8,128)S(1)}, f32[64,128]{1,0:T(8,128)S(1)}, u32[]{:S(2)}, u32[]{:S(2)}) collective-permute-start(f32[64,128]{1,0:T(8,128)S(1)} %get-tuple-element.79), channel_id=1, source_target_pairs={{0,8},{1,9},{2,10},{3,11},{4,12},{5,13},{6,14},{7,15},{8,0},{9,1},... | collective-permute-start | bytes 98312 | tf_op jit(solution)/shard_map/ppermute | solution.py:433
  36.5 3.8 %collective-permute-start.11 = (f32[64,128]{1,0:T(8,128)S(1)}, f32[64,128]{1,0:T(8,128)S(1)}, u32[]{:S(2)}, u32[]{:S(2)}) collective-permute-start(f32[64,128]{1,0:T(8,128)S(1)} %get-tuple-element.80), channel_id=1, source_target_pairs={{0,1},{1,0},{2,3},{3,2},{4,5},{5,4},{6,7},{7,6},{8,16},{9,17},{10,... | collective-permute-start | bytes 98312 | tf_op jit(solution)/shard_map/ppermute | solution.py:433
  44.9 4.3 %collective-permute-start.12 = (f32[64,128]{1,0:T(8,128)S(1)}, f32[64,128]{1,0:T(8,128)S(1)}, u32[]{:S(2)}, u32[]{:S(2)}) collective-permute-start(f32[64,128]{1,0:T(8,128)S(1)} %get-tuple-element.87), channel_id=1, source_target_pairs={{0,1},{1,0},{2,3},{3,2},{4,5},{5,4},{6,7},{7,6},{8,9},{9,8},{10,11... | collective-permute-start | bytes 98312 | tf_op jit(solution)/shard_map/ppermute | solution.py:433
  45.0 4.2 %collective-permute-start.13 = (f32[64,128]{1,0:T(8,128)S(1)}, f32[64,128]{1,0:T(8,128)S(1)}, u32[]{:S(2)}, u32[]{:S(2)}) collective-permute-start(f32[64,128]{1,0:T(8,128)S(1)} %get-tuple-element.88), channel_id=1, source_target_pairs={{0,8},{1,2},{2,1},{3,4},{4,3},{5,6},{6,5},{7,15},{8,0},{9,10},{10,... | collective-permute-start | bytes 98312 | tf_op jit(solution)/shard_map/ppermute | solution.py:433
  47.1 3.9 %collective-permute-start.14 = (f32[64,128]{1,0:T(8,128)S(1)}, f32[64,128]{1,0:T(8,128)S(1)}, u32[]{:S(2)}, u32[]{:S(2)}) collective-permute-start(f32[64,128]{1,0:T(8,128)S(1)} %get-tuple-element.89), channel_id=1, source_target_pairs={{0,8},{1,9},{2,10},{3,11},{4,12},{5,13},{6,14},{7,15},{8,0},{9,1},... | collective-permute-start | bytes 98312 | tf_op jit(solution)/shard_map/ppermute | solution.py:433
  47.2 3.8 %collective-permute-start.15 = (f32[64,128]{1,0:T(8,128)S(1)}, f32[64,128]{1,0:T(8,128)S(1)}, u32[]{:S(2)}, u32[]{:S(2)}) collective-permute-start(f32[64,128]{1,0:T(8,128)S(1)} %get-tuple-element.90), channel_id=1, source_target_pairs={{0,1},{1,0},{2,3},{3,2},{4,5},{5,4},{6,7},{7,6},{8,16},{9,17},{10,... | collective-permute-start | bytes 98312 | tf_op jit(solution)/shard_map/ppermute | solution.py:433
where the time goes:
time: 53.2 us; the launch traced here: 52.8 us
  Pallas kernels  27.4 us (52%)
  starting transfers between devices  13.4 us (25%)
  local copies, waits for them, and re-layouts  7.75 us (15%)
  waiting for transfers between devices  4.03 us (8%)
    pallas_call x9, Pallas kernels, call(): pl.pallas_call(kernel, out_shape=outs, in_specs=[block] * len(operands),...  27.4 us
    ppermute x16, starting transfers between devices, exchange(): lax.ppermute(m, AXES, pairs)  13.4 us
    unnamed x25, local copies, waits for them, and re-layouts  7.75 us
    ppermute x16, waiting for transfers between devices, exchange(): lax.ppermute(m, AXES, pairs)  4.03 us
  transfers between devices with their start and end apart: 16, of which 3 were waited for; matrix products, arithmetic and copies ran while one was open for 7% of the time, Pallas kernels for 16%

commit v1 on v0

--- a/solution.py
+++ b/solution.py
@@ -116,7 +116,7 @@
                         inner * cells : (inner + 1) * cells,
                     ]
                     for i in range(size):
-                        term = jac[direction, start + i, pl.ds(inner, 1), :] * value
+                        term = jac[start + i, inner, pl.ds(direction, 1), :] * value
                         total[i] = term if total[i] is None else total[i] + term
             for i in range(size):
                 own[start + i] += total[i] * weights[degree]
@@ -150,12 +150,30 @@
 
 
 def start_kernel(
-    coefficients, jac, stiffness, clusters, sends,
-    own, message_0, message_1, message_2, message_3, stiff, picks,
-    first, second,
+    stiffness_far, sends_far, clusters_far, coefficients_far, jac_far, *rest
 ):
+    far, rest = rest[:7], rest[7:]
+    own, message_0, message_1, message_2, message_3, stiff, picks = rest[:7]
+    clusters, coefficients, jac, stiffness = rest[7:11]
+    near, (first, second, sends, arrived) = rest[11:18], rest[18:]
     fields, basis, cells = own.shape
+    pairs = (
+        (stiffness_far, stiffness),
+        (sends_far, sends),
+        (clusters_far, clusters),
+        (coefficients_far, coefficients),
+        (jac_far, jac),
+        *zip(far, near),
+    )
+    copies = [
+        pltpu.make_async_copy(source, target, arrived.at[i])
+        for i, (source, target) in enumerate(pairs)
+    ]
+    for copy in copies:
+        copy.start()
+    copies[0].wait()
     stiff[...] = widened(-stiffness[...].reshape(3 * basis, basis))
+    copies[1].wait()
     entries = sends.shape[1]
     rows = directions()
     places = []
@@ -167,9 +185,13 @@
     hot = jnp.where(element == place, 1.0, 0.0).astype(jnp.bfloat16)
     picks[0:cells, :] = hot
     picks[cells : 2 * cells, :] = hot
+    for copy in copies[2:5]:
+        copy.wait()
     weights = taylor_weights(clusters[...], 0)
     series(lambda field: coefficients[field], jac, stiff, weights, own, first, second)
     pack(own, picks, (message_0, message_1, message_2, message_3))
+    for copy in copies[5:]:
+        copy.wait()
 
 
 def local_kernel(own, jac, flux_local, matrices, local_hot, volume, local_flux, traces, spatial):
@@ -187,7 +209,7 @@
                     inner * cells : (inner + 1) * cells,
                 ]
                 for i in range(size):
-                    term = jac[direction, start + i, pl.ds(inner, 1), :] * value
+                    term = jac[start + i, inner, pl.ds(direction, 1), :] * value
                     total[i] = term if total[i] is None else total[i] + term
         for i in range(size):
             volume[start + i] = total[i]
@@ -200,7 +222,7 @@
                 base + face * wide : base + (face + 1) * wide, inner * cells : (inner + 1) * cells
             ]
             for outer in range(fields):
-                term = flux_local[face, outer, pl.ds(inner, 1), :] * value
+                term = flux_local[outer, inner, pl.ds(face, 1), :] * value
                 total[outer] = term if total[outer] is None else total[outer] + term
         for outer in range(fields):
             local_flux[face, outer] = total[outer]
@@ -228,24 +250,24 @@
     spatial, plain,
 ):
     fields, basis, cells = own.shape
-    face_basis = face_proj.shape[1]
+    face_basis = face_proj.shape[0]
     wide = traces.shape[0] // fields
     plain[...] = jnp.zeros_like(plain)
     for direction in range(3):
         plain[direction * basis : (direction + 1) * basis, :] = stiffness[direction].T
     row = 3 * basis
     for face in range(FACES):
-        plain[row : row + face_basis, :] = face_proj[face]
+        plain[row : row + face_basis, :] = face_proj[:, face, :]
         row += wide
     for pair in range(ORIENTS):
         plain[row : row + face_basis, :] = neigh_proj[pair]
         row += wide
     matrices[...] = widened(plain[...])
-    empty = jnp.zeros((basis, wide - face_basis), jnp.float32)
+    empty = jnp.zeros((wide - face_basis, basis), jnp.float32)
     parts = []
     for face in range(FACES):
-        parts += [lifting[face], empty]
-    lift_plain = jnp.concatenate(parts, axis=1)
+        parts += [lifting[:, face, :], empty]
+    lift_plain = jnp.concatenate(parts, axis=0).T
     lift_high = rounded(lift_plain)
     lift[...] = jnp.concatenate([lift_high, lift_high, lift_plain - lift_high], axis=1).astype(
         jnp.bfloat16
@@ -344,7 +366,7 @@
             source = main[inner * wide : (inner + 1) * wide] if inner < fields - 1 else tail
             value = source[:, face * cells : (face + 1) * cells]
             for outer in range(fields):
-                total[outer] = total[outer] + flux_neigh[face, outer, pl.ds(inner, 1), :] * value
+                total[outer] = total[outer] + flux_neigh[outer, inner, pl.ds(face, 1), :] * value
         rows.append(jnp.concatenate(total, axis=1))
     flux = jnp.concatenate(rows, axis=0)
     high = rounded(flux)
@@ -392,14 +414,17 @@
         increment[field] = applied_in[field] + (pending_in[field] + updates[field])
 
 
-def call(kernel, outs, scratch, flops, *operands):
+def call(kernel, outs, scratch, flops, *operands, far=False):
     block = pl.BlockSpec(memory_space=pltpu.VMEM)
+    source = pl.BlockSpec(memory_space=pltpu.HBM) if far else block
+    if far:
+        operands = [pltpu.with_memory_space_constraint(x, pltpu.HBM) for x in operands]
     return pl.pallas_call(
         kernel,
         out_shape=outs,
-        in_specs=[block] * len(operands),
+        in_specs=[source] * len(operands),
         out_specs=[block] * len(outs),
-        scratch_shapes=[pltpu.VMEM(shape, jnp.float32) for shape in scratch],
+        scratch_shapes=scratch,
         compiler_params=pltpu.CompilerParams(vmem_limit_bytes=40 << 20),
         cost_estimate=pl.CostEstimate(flops=flops, bytes_accessed=1 << 20, transcendentals=0),
     )(*operands)
@@ -412,6 +437,11 @@
     fields, basis, cells = coefficients.shape
     wide = -(-face_proj.shape[1] // 8) * 8
     clusters = clusters.reshape(1, cells)
+    jacobians = jnp.transpose(jacobians, (1, 2, 0, 3))
+    flux_local = jnp.transpose(flux_local, (1, 2, 0, 3))
+    flux_neigh = jnp.transpose(flux_neigh, (1, 2, 0, 3))
+    face_proj = jnp.transpose(face_proj, (1, 0, 2))
+    lifting = jnp.transpose(lifting, (2, 0, 1))
     exchanges = [
         swaps(doms, subs, axis, phase) for axis in ("sub", "dom") for phase in (0, 1)
     ]
@@ -426,18 +456,28 @@
     message = f32(basis + 8, cells)
     depth = 3 * basis + 8
     rows = 3 * basis + (FACES + ORIENTS) * wide
-    derived = (3 * basis, fields * cells)
+    derived = pltpu.VMEM((3 * basis, fields * cells), jnp.float32)
     faces = FACES * cells
 
     def exchange(messages):
         return [lax.ppermute(m, AXES, pairs) for m, pairs in zip(messages, exchanges)]
 
-    own, *messages, stiff, picks = call(
+    first = [stiffness, send_list, clusters, coefficients, jacobians]
+    later = [flux_local, flux_neigh, face_proj, neigh_proj, lifting, face_slots, orientation]
+    near = [clusters, coefficients, jacobians, stiffness, *later]
+    own, *given = call(
         start_kernel,
-        [state] + [message] * 4 + [bf16(3 * basis, depth), bf16(2 * cells, 4 * cells)],
-        [derived, derived], 1 << 27,
-        coefficients, jacobians, stiffness, clusters, send_list,
-    )
+        [state] + [message] * 4 + [bf16(3 * basis, depth), bf16(2 * cells, 4 * cells)]
+        + [jax.ShapeDtypeStruct(x.shape, x.dtype) for x in near],
+        [
+            derived, derived, pltpu.VMEM(send_list.shape, send_list.dtype),
+            pltpu.SemaphoreType.DMA((len(first) + len(later),)),
+        ],
+        1 << 27, *first, *later, far=True,
+    )
+    messages, (stiff, picks), near = given[:4], given[4:6], given[6:]
+    clusters, coefficients, jacobians, stiffness = near[:4]
+    flux_local, flux_neigh, face_proj, neigh_proj, lifting, face_slots, orientation = near[4:]
     local_outs = [state, f32(FACES, fields, wide, cells), f32(fields * wide, faces)]
     applied = pending = coefficients
     for substep in range(SUBSTEPS):
@@ -450,13 +490,13 @@
                     bf16(rows, depth), bf16(ORIENTS * cells, faces), bf16(5 * cells, faces),
                     f32(8, 5 * cells), bf16(basis, 3 * FACES * wide),
                 ],
-                [(rows, fields * cells), (rows, basis)], 1 << 27,
+                [pltpu.VMEM((rows, fields * cells), jnp.float32), pltpu.VMEM((rows, basis), jnp.float32)], 1 << 27,
                 own, jacobians, flux_local, stiffness, face_proj, neigh_proj, lifting,
                 face_slots, orientation,
             )
         else:
             volume, local_flux, traces = call(
-                local_kernel, local_outs, [(rows, fields * cells)], 1 << 27,
+                local_kernel, local_outs, [pltpu.VMEM((rows, fields * cells), jnp.float32)], 1 << 27,
                 own, jacobians, flux_local, matrices, local_hot,
             )
         rest = (

time: 53.2 us -> 47 us (0.88)
  local copies, waits for them, and re-layouts: 7.75 us -> 0 us
  Pallas kernels: 27.4 us -> 29.2 us
    unnamed x25 -> x0, local copies, waits for them, and re-layouts: 7.75 us -> none
    pallas_call x9, Pallas kernels: 27.4 us -> 29.2 us  [call(): pl.pallas_call(kernel, out_shape=outs, in_specs=[source] * len(operands),...]
  transfers between devices with their start and end apart: 16 -> 16, of which waited for: 3 -> 4; matrix products, arithmetic and copies ran while one was open for 7% -> 0% of each run, Pallas kernels for 16% -> 18%
where the time goes in v1:
time: 47 us; the launch traced here: 46.8 us
  Pallas kernels  29.2 us (62%)
  starting transfers between devices  13.7 us (29%)
  waiting for transfers between devices  3.74 us (8%)
    pallas_call x9, Pallas kernels, call(): pl.pallas_call(kernel, out_shape=outs, in_specs=[source] * len(operands),...  29.2 us
    ppermute x16, starting transfers between devices, exchange(): lax.ppermute(m, AXES, pairs)  13.7 us
    ppermute x16, waiting for transfers between devices, exchange(): lax.ppermute(m, AXES, pairs)  3.74 us
  transfers between devices with their start and end apart: 16, of which 4 were waited for; matrix products, arithmetic and copies ran while one was open for 0% of the time, Pallas kernels for 18%

profile of v1, /device:TPU:0, one launch (start us, length us, event | category | flops | bytes accessed | tf_op | source)
XLA Modules:
  0.0 46.8 jit_solution(2495468433639272626)
XLA Ops:
  0.0 4.9 %shard_map.118 = (f32[9,56,128]{2,1,0:T(8,128)S(1)}, f32[64,128]{1,0:T(8,128)S(1)}, f32[64,128]{1,0:T(8,128)S(1)}, f32[64,128]{1,0:T(8,128)S(1)}, f32[64,128]{1,...) custom-call(f32[3,56,56]{2,1,0:T(8,128)} %stiffness_far.1, ...), custom_call_target="tpu_custom_call" | custom-call | flops 134217728 | bytes 1048576 | tf_op jit(solution)/shard_map/pallas_call | solution.py:422
  4.9 0.5 %collective-permute-start = (f32[64,128]{1,0:T(8,128)S(1)}, f32[64,128]{1,0:T(8,128)S(1)}, u32[]{:S(2)}, u32[]{:S(2)}) collective-permute-start(f32[64,128]{1,0:T(8,128)S(1)} %get-tuple-element.66), channel_id=1, source_target_pairs={{0,1},{1,0},{2,3},{3,2},{4,5},{5,4},{6,7},{7,6},{8,9},{9,8},{10,11... | collective-permute-start | bytes 98312 | tf_op jit(solution)/shard_map/ppermute | solution.py:463
  5.5 2.6 %collective-permute-start.1 = (f32[64,128]{1,0:T(8,128)S(1)}, f32[64,128]{1,0:T(8,128)S(1)}, u32[]{:S(2)}, u32[]{:S(2)}) collective-permute-start(f32[64,128]{1,0:T(8,128)S(1)} %get-tuple-element.67), channel_id=1, source_target_pairs={{0,8},{1,2},{2,1},{3,4},{4,3},{5,6},{6,5},{7,15},{8,0},{9,10},{10,... | collective-permute-start | bytes 98312 | tf_op jit(solution)/shard_map/ppermute | solution.py:463
  8.1 0.1 collective-permute-start.2
  8.2 1.2 %collective-permute-start.3 = (f32[64,128]{1,0:T(8,128)S(1)}, f32[64,128]{1,0:T(8,128)S(1)}, u32[]{:S(2)}, u32[]{:S(2)}) collective-permute-start(f32[64,128]{1,0:T(8,128)S(1)} %get-tuple-element.69), channel_id=1, source_target_pairs={{0,1},{1,0},{2,3},{3,2},{4,5},{5,4},{6,7},{7,6},{8,16},{9,17},{10,... | collective-permute-start | bytes 98312 | tf_op jit(solution)/shard_map/ppermute | solution.py:463
  9.4 2.3 %shard_map.119 = (f32[9,56,128]{2,1,0:T(8,128)S(1)}, f32[4,9,24,128]{3,2,1,0:T(8,128)S(1)}, f32[216,512]{1,0:T(8,128)S(1)}, bf16[552,176]{1,0:T(8,128)(2,1)S(1)}...) custom-call(f32[9,56,128]{2,1,0:T(8,128)S(1)} %get-tuple-element.70., ...), custom_call_target="tpu_custom_call" | custom-call | flops 134217728 | bytes 1048576 | tf_op jit(solution)/shard_map/pallas_call | solution.py:422
  11.7 0.0 collective-permute-done.in_0
  11.7 0.0 collective-permute-done.1.in_1
  11.7 0.3 collective-permute-done.2.in_2
  12.0 0.0 collective-permute-done.3.in_3
  12.0 4.7 %shard_map.120 = (f32[9,56,128]{2,1,0:T(8,128)S(1)}, f32[9,56,128]{2,1,0:T(8,128)S(1)}, f32[9,56,128]{2,1,0:T(8,128)S(1)}, f32[64,128]{1,0:T(8,128)S(1)}, f32[64...) custom-call(f32[9,56,128]{2,1,0:T(8,128)S(1)} %get-tuple-element.61.coefficients.applied_in.pending_in, ...), custom_call_target="tpu_custom_call" | custom-call | flops 134217728 | bytes 1048576 | tf_op jit(solution)/shard_map/pallas_call | solution.py:422
  16.7 0.1 collective-permute-start.4
  16.8 2.6 %collective-permute-start.5 = (f32[64,128]{1,0:T(8,128)S(1)}, f32[64,128]{1,0:T(8,128)S(1)}, u32[]{:S(2)}, u32[]{:S(2)}) collective-permute-start(f32[64,128]{1,0:T(8,128)S(1)} %get-tuple-element.89), channel_id=1, source_target_pairs={{0,8},{1,2},{2,1},{3,4},{4,3},{5,6},{6,5},{7,15},{8,0},{9,10},{10,... | collective-permute-start | bytes 98312 | tf_op jit(solution)/shard_map/ppermute | solution.py:463
  19.4 0.0 collective-permute-start.6
  19.4 1.3 %collective-permute-start.7 = (f32[64,128]{1,0:T(8,128)S(1)}, f32[64,128]{1,0:T(8,128)S(1)}, u32[]{:S(2)}, u32[]{:S(2)}) collective-permute-start(f32[64,128]{1,0:T(8,128)S(1)} %get-tuple-element.91), channel_id=1, source_target_pairs={{0,1},{1,0},{2,3},{3,2},{4,5},{5,4},{6,7},{7,6},{8,16},{9,17},{10,... | collective-permute-start | bytes 98312 | tf_op jit(solution)/shard_map/ppermute | solution.py:463
  20.7 2.0 %shard_map.121 = (f32[9,56,128]{2,1,0:T(8,128)S(1)}, f32[4,9,24,128]{3,2,1,0:T(8,128)S(1)}, f32[216,512]{1,0:T(8,128)S(1)}) custom-call(f32[9,56,128]{2,1,0:T(8,128)S(1)} %get-tuple-element.92.own, f32[9,9,3,128]{3,2,1,0:T(4,128)S(1)} %get-tuple-element.62.jac, f32[9,9,4,128]{3,2,1,0:T(4,128)S(1)} %get-tuple-element.71.flux_local, ...), custom_call_target="tpu_custom_call" | custom-call | flops 134217728 | bytes 1048576 | tf_op jit(solution)/shard_map/pallas_call | solution.py:422
  22.7 0.6 %collective-permute-done.6.in_2 = f32[64,128]{1,0:T(8,128)S(1)} collective-permute-done((f32[64,128]{1,0:T(8,128)S(1)}, f32[64,128]{1,0:T(8,128)S(1)}, u32[]{:S(2)}, u32[]{:S(2)}) %collective-permute-start.6) | collective-permute-done | bytes 32800 | tf_op jit(solution)/shard_map/ppermute | solution.py:463
  23.3 4.9 %shard_map.122 = (f32[9,56,128]{2,1,0:T(8,128)S(1)}, f32[9,56,128]{2,1,0:T(8,128)S(1)}, f32[9,56,128]{2,1,0:T(8,128)S(1)}, f32[64,128]{1,0:T(8,128)S(1)}, f32[64...) custom-call(f32[9,56,128]{2,1,0:T(8,128)S(1)} %get-tuple-element.61.coefficients.applied_in.pending_in, ...), custom_call_target="tpu_custom_call" | custom-call | flops 134217728 | bytes 1048576 | tf_op jit(solution)/shard_map/pallas_call | solution.py:422
  28.2 0.1 collective-permute-start.8
  28.2 2.1 %collective-permute-start.9 = (f32[64,128]{1,0:T(8,128)S(1)}, f32[64,128]{1,0:T(8,128)S(1)}, u32[]{:S(2)}, u32[]{:S(2)}) collective-permute-start(f32[64,128]{1,0:T(8,128)S(1)} %get-tuple-element.100), channel_id=1, source_target_pairs={{0,8},{1,2},{2,1},{3,4},{4,3},{5,6},{6,5},{7,15},{8,0},{9,10},{10,... | collective-permute-start | bytes 98312 | tf_op jit(solution)/shard_map/ppermute | solution.py:463
  30.3 0.1 collective-permute-start.10
  30.4 0.7 %collective-permute-start.11 = (f32[64,128]{1,0:T(8,128)S(1)}, f32[64,128]{1,0:T(8,128)S(1)}, u32[]{:S(2)}, u32[]{:S(2)}) collective-permute-start(f32[64,128]{1,0:T(8,128)S(1)} %get-tuple-element.102), channel_id=1, source_target_pairs={{0,1},{1,0},{2,3},{3,2},{4,5},{5,4},{6,7},{7,6},{8,16},{9,17},{10,... | collective-permute-start | bytes 98312 | tf_op jit(solution)/shard_map/ppermute | solution.py:463
  31.1 2.0 %shard_map.123 = (f32[9,56,128]{2,1,0:T(8,128)S(1)}, f32[4,9,24,128]{3,2,1,0:T(8,128)S(1)}, f32[216,512]{1,0:T(8,128)S(1)}) custom-call(f32[9,56,128]{2,1,0:T(8,128)S(1)} %get-tuple-element.103.own, f32[9,9,3,128]{3,2,1,0:T(4,128)S(1)} %get-tuple-element.62.jac, f32[9,9,4,128]{3,2,1,0:T(4,128)S(1)} %get-tuple-element.71.flux_local, ...), custom_call_target="tpu_custom_call" | custom-call | flops 134217728 | bytes 1048576 | tf_op jit(solution)/shard_map/pallas_call | solution.py:422
  33.1 1.1 %collective-permute-done.10.in_2 = f32[64,128]{1,0:T(8,128)S(1)} collective-permute-done((f32[64,128]{1,0:T(8,128)S(1)}, f32[64,128]{1,0:T(8,128)S(1)}, u32[]{:S(2)}, u32[]{:S(2)}) %collective-permute-start.10) | collective-permute-done | bytes 32800 | tf_op jit(solution)/shard_map/ppermute | solution.py:463
  34.2 4.7 %shard_map.124 = (f32[9,56,128]{2,1,0:T(8,128)S(1)}, f32[9,56,128]{2,1,0:T(8,128)S(1)}, f32[9,56,128]{2,1,0:T(8,128)S(1)}, f32[64,128]{1,0:T(8,128)S(1)}, f32[64...) custom-call(f32[9,56,128]{2,1,0:T(8,128)S(1)} %get-tuple-element.61.coefficients.applied_in.pending_in, ...), custom_call_target="tpu_custom_call" | custom-call | flops 134217728 | bytes 1048576 | tf_op jit(solution)/shard_map/pallas_call | solution.py:422
  38.9 0.1 collective-permute-start.12
  39.0 2.1 %collective-permute-start.13 = (f32[64,128]{1,0:T(8,128)S(1)}, f32[64,128]{1,0:T(8,128)S(1)}, u32[]{:S(2)}, u32[]{:S(2)}) collective-permute-start(f32[64,128]{1,0:T(8,128)S(1)} %get-tuple-element.110), channel_id=1, source_target_pairs={{0,8},{1,2},{2,1},{3,4},{4,3},{5,6},{6,5},{7,15},{8,0},{9,10},{10,... | collective-permute-start | bytes 98312 | tf_op jit(solution)/shard_map/ppermute | solution.py:463
  41.1 0.1 collective-permute-start.14
  41.2 0.1 collective-permute-start.15
  41.3 2.0 %shard_map.125 = (f32[9,56,128]{2,1,0:T(8,128)S(1)}, f32[4,9,24,128]{3,2,1,0:T(8,128)S(1)}, f32[216,512]{1,0:T(8,128)S(1)}) custom-call(f32[9,56,128]{2,1,0:T(8,128)S(1)} %get-tuple-element.113.own, f32[9,9,3,128]{3,2,1,0:T(4,128)S(1)} %get-tuple-element.62.jac, f32[9,9,4,128]{3,2,1,0:T(4,128)S(1)} %get-tuple-element.71.flux_local, ...), custom_call_target="tpu_custom_call" | custom-call | flops 134217728 | bytes 1048576 | tf_op jit(solution)/shard_map/pallas_call | solution.py:422
  43.3 1.7 %collective-permute-done.14.in_2 = f32[64,128]{1,0:T(8,128)S(1)} collective-permute-done((f32[64,128]{1,0:T(8,128)S(1)}, f32[64,128]{1,0:T(8,128)S(1)}, u32[]{:S(2)}, u32[]{:S(2)}) %collective-permute-start.14) | collective-permute-done | bytes 32800 | tf_op jit(solution)/shard_map/ppermute | solution.py:463
  45.0 1.8 %shard_map.126 = f32[9,56,128]{2,1,0:T(8,128)} custom-call(f32[9,56,128]{2,1,0:T(8,128)S(1)} %get-tuple-element.107.applied_in, f32[9,56,128]{2,1,0:T(8,128)S(1)} %get-tuple-element.108.pending_in, f32[64,128]{1,0:T(8,128)S(1)} %collective-permute-done.12.in_0, f32[64,128]{1,0:T(8,128)S(1)} %collective-permute-done.13.in_1, ...), custom_call_target="tpu_custom_call" | custom-call | flops 134217728 | bytes 1048576 | tf_op jit(solution)/shard_map/pallas_call | solution.py:422
  (9 shorter events, 0.0 us)
Async XLA Ops:
  4.9 6.8 %collective-permute-start = (f32[64,128]{1,0:T(8,128)S(1)}, f32[64,128]{1,0:T(8,128)S(1)}, u32[]{:S(2)}, u32[]{:S(2)}) collective-permute-start(f32[64,128]{1,0:T(8,128)S(1)} %get-tuple-element.66), channel_id=1, source_target_pairs={{0,1},{1,0},{2,3},{3,2},{4,5},{5,4},{6,7},{7,6},{8,9},{9,8},{10,11... | collective-permute-start | bytes 98312 | tf_op jit(solution)/shard_map/ppermute | solution.py:463
  5.5 6.3 %collective-permute-start.1 = (f32[64,128]{1,0:T(8,128)S(1)}, f32[64,128]{1,0:T(8,128)S(1)}, u32[]{:S(2)}, u32[]{:S(2)}) collective-permute-start(f32[64,128]{1,0:T(8,128)S(1)} %get-tuple-element.67), channel_id=1, source_target_pairs={{0,8},{1,2},{2,1},{3,4},{4,3},{5,6},{6,5},{7,15},{8,0},{9,10},{10,... | collective-permute-start | bytes 98312 | tf_op jit(solution)/shard_map/ppermute | solution.py:463
  8.1 3.9 %collective-permute-start.2 = (f32[64,128]{1,0:T(8,128)S(1)}, f32[64,128]{1,0:T(8,128)S(1)}, u32[]{:S(2)}, u32[]{:S(2)}) collective-permute-start(f32[64,128]{1,0:T(8,128)S(1)} %get-tuple-element.68), channel_id=1, source_target_pairs={{0,8},{1,9},{2,10},{3,11},{4,12},{5,13},{6,14},{7,15},{8,0},{9,1},... | collective-permute-start | bytes 98312 | tf_op jit(solution)/shard_map/ppermute | solution.py:463
  8.2 3.8 %collective-permute-start.3 = (f32[64,128]{1,0:T(8,128)S(1)}, f32[64,128]{1,0:T(8,128)S(1)}, u32[]{:S(2)}, u32[]{:S(2)}) collective-permute-start(f32[64,128]{1,0:T(8,128)S(1)} %get-tuple-element.69), channel_id=1, source_target_pairs={{0,1},{1,0},{2,3},{3,2},{4,5},{5,4},{6,7},{7,6},{8,16},{9,17},{10,... | collective-permute-start | bytes 98312 | tf_op jit(solution)/shard_map/ppermute | solution.py:463
  16.7 6.0 %collective-permute-start.4 = (f32[64,128]{1,0:T(8,128)S(1)}, f32[64,128]{1,0:T(8,128)S(1)}, u32[]{:S(2)}, u32[]{:S(2)}) collective-permute-start(f32[64,128]{1,0:T(8,128)S(1)} %get-tuple-element.88), channel_id=1, source_target_pairs={{0,1},{1,0},{2,3},{3,2},{4,5},{5,4},{6,7},{7,6},{8,9},{9,8},{10,11... | collective-permute-start | bytes 98312 | tf_op jit(solution)/shard_map/ppermute | solution.py:463
  16.8 5.9 %collective-permute-start.5 = (f32[64,128]{1,0:T(8,128)S(1)}, f32[64,128]{1,0:T(8,128)S(1)}, u32[]{:S(2)}, u32[]{:S(2)}) collective-permute-start(f32[64,128]{1,0:T(8,128)S(1)} %get-tuple-element.89), channel_id=1, source_target_pairs={{0,8},{1,2},{2,1},{3,4},{4,3},{5,6},{6,5},{7,15},{8,0},{9,10},{10,... | collective-permute-start | bytes 98312 | tf_op jit(solution)/shard_map/ppermute | solution.py:463
  19.4 3.9 %collective-permute-start.6 = (f32[64,128]{1,0:T(8,128)S(1)}, f32[64,128]{1,0:T(8,128)S(1)}, u32[]{:S(2)}, u32[]{:S(2)}) collective-permute-start(f32[64,128]{1,0:T(8,128)S(1)} %get-tuple-element.90), channel_id=1, source_target_pairs={{0,8},{1,9},{2,10},{3,11},{4,12},{5,13},{6,14},{7,15},{8,0},{9,1},... | collective-permute-start | bytes 98312 | tf_op jit(solution)/shard_map/ppermute | solution.py:463
  19.4 3.9 %collective-permute-start.7 = (f32[64,128]{1,0:T(8,128)S(1)}, f32[64,128]{1,0:T(8,128)S(1)}, u32[]{:S(2)}, u32[]{:S(2)}) collective-permute-start(f32[64,128]{1,0:T(8,128)S(1)} %get-tuple-element.91), channel_id=1, source_target_pairs={{0,1},{1,0},{2,3},{3,2},{4,5},{5,4},{6,7},{7,6},{8,16},{9,17},{10,... | collective-permute-start | bytes 98312 | tf_op jit(solution)/shard_map/ppermute | solution.py:463
  28.2 5.0 %collective-permute-start.8 = (f32[64,128]{1,0:T(8,128)S(1)}, f32[64,128]{1,0:T(8,128)S(1)}, u32[]{:S(2)}, u32[]{:S(2)}) collective-permute-start(f32[64,128]{1,0:T(8,128)S(1)} %get-tuple-element.99), channel_id=1, source_target_pairs={{0,1},{1,0},{2,3},{3,2},{4,5},{5,4},{6,7},{7,6},{8,9},{9,8},{10,11... | collective-permute-start | bytes 98312 | tf_op jit(solution)/shard_map/ppermute | solution.py:463
  28.2 4.9 %collective-permute-start.9 = (f32[64,128]{1,0:T(8,128)S(1)}, f32[64,128]{1,0:T(8,128)S(1)}, u32[]{:S(2)}, u32[]{:S(2)}) collective-permute-start(f32[64,128]{1,0:T(8,128)S(1)} %get-tuple-element.100), channel_id=1, source_target_pairs={{0,8},{1,2},{2,1},{3,4},{4,3},{5,6},{6,5},{7,15},{8,0},{9,10},{10,... | collective-permute-start | bytes 98312 | tf_op jit(solution)/shard_map/ppermute | solution.py:463
  30.3 3.9 %collective-permute-start.10 = (f32[64,128]{1,0:T(8,128)S(1)}, f32[64,128]{1,0:T(8,128)S(1)}, u32[]{:S(2)}, u32[]{:S(2)}) collective-permute-start(f32[64,128]{1,0:T(8,128)S(1)} %get-tuple-element.101), channel_id=1, source_target_pairs={{0,8},{1,9},{2,10},{3,11},{4,12},{5,13},{6,14},{7,15},{8,0},{9,1},... | collective-permute-start | bytes 98312 | tf_op jit(solution)/shard_map/ppermute | solution.py:463
  30.4 3.8 %collective-permute-start.11 = (f32[64,128]{1,0:T(8,128)S(1)}, f32[64,128]{1,0:T(8,128)S(1)}, u32[]{:S(2)}, u32[]{:S(2)}) collective-permute-start(f32[64,128]{1,0:T(8,128)S(1)} %get-tuple-element.102), channel_id=1, source_target_pairs={{0,1},{1,0},{2,3},{3,2},{4,5},{5,4},{6,7},{7,6},{8,16},{9,17},{10,... | collective-permute-start | bytes 98312 | tf_op jit(solution)/shard_map/ppermute | solution.py:463
  38.9 4.3 %collective-permute-start.12 = (f32[64,128]{1,0:T(8,128)S(1)}, f32[64,128]{1,0:T(8,128)S(1)}, u32[]{:S(2)}, u32[]{:S(2)}) collective-permute-start(f32[64,128]{1,0:T(8,128)S(1)} %get-tuple-element.109), channel_id=1, source_target_pairs={{0,1},{1,0},{2,3},{3,2},{4,5},{5,4},{6,7},{7,6},{8,9},{9,8},{10,11... | collective-permute-start | bytes 98312 | tf_op jit(solution)/shard_map/ppermute | solution.py:463
  39.0 4.3 %collective-permute-start.13 = (f32[64,128]{1,0:T(8,128)S(1)}, f32[64,128]{1,0:T(8,128)S(1)}, u32[]{:S(2)}, u32[]{:S(2)}) collective-permute-start(f32[64,128]{1,0:T(8,128)S(1)} %get-tuple-element.110), channel_id=1, source_target_pairs={{0,8},{1,2},{2,1},{3,4},{4,3},{5,6},{6,5},{7,15},{8,0},{9,10},{10,... | collective-permute-start | bytes 98312 | tf_op jit(solution)/shard_map/ppermute | solution.py:463
  41.1 3.9 %collective-permute-start.14 = (f32[64,128]{1,0:T(8,128)S(1)}, f32[64,128]{1,0:T(8,128)S(1)}, u32[]{:S(2)}, u32[]{:S(2)}) collective-permute-start(f32[64,128]{1,0:T(8,128)S(1)} %get-tuple-element.111), channel_id=1, source_target_pairs={{0,8},{1,9},{2,10},{3,11},{4,12},{5,13},{6,14},{7,15},{8,0},{9,1},... | collective-permute-start | bytes 98312 | tf_op jit(solution)/shard_map/ppermute | solution.py:463
  41.2 3.8 %collective-permute-start.15 = (f32[64,128]{1,0:T(8,128)S(1)}, f32[64,128]{1,0:T(8,128)S(1)}, u32[]{:S(2)}, u32[]{:S(2)}) collective-permute-start(f32[64,128]{1,0:T(8,128)S(1)} %get-tuple-element.112), channel_id=1, source_target_pairs={{0,1},{1,0},{2,3},{3,2},{4,5},{5,4},{6,7},{7,6},{8,16},{9,17},{10,... | collective-permute-start | bytes 98312 | tf_op jit(solution)/shard_map/ppermute | solution.py:463

commit v2 on v1

--- a/solution.py
+++ b/solution.py
@@ -14,6 +14,7 @@
 SUBSTEPS = 4
 STEP_LENGTH = 0.5
 GROUPS = (5, 4)
+PAIR_GROUPS = (3, 2)
 AXES = ("dom", "sub")
 
 
@@ -90,40 +91,108 @@
     return weights
 
 
-def series(current, jac, stiff, weights, own, first, second):
-    fields, basis, cells = own.shape
-
-    def spatial(target, start, values):
-        columns = jnp.concatenate([stacked(value) for value in values], axis=1)
-        target[:, start * cells : (start + len(values)) * cells] = product(stiff[...], columns)
-
+def spatial(stiff, target, start, values):
+    cells = values[0].shape[1]
+    columns = jnp.concatenate([stacked(value) for value in values], axis=1)
+    target[:, start * cells : (start + len(values)) * cells] = product(stiff[...], columns)
+
+
+def mixed(rows, source, starts, basis):
+    cells = rows(0, 0, 0).shape[1]
+    fields = source.shape[1] // cells
+    total = [None] * len(starts)
+    for direction in range(3):
+        for inner in range(fields):
+            value = source[
+                direction * basis : (direction + 1) * basis, inner * cells : (inner + 1) * cells
+            ]
+            for i, outer in enumerate(starts):
+                term = rows(outer, inner, direction) * value
+                total[i] = term if total[i] is None else total[i] + term
+    return total
+
+
+def rows_of(jac):
+    return lambda outer, inner, direction: jac[outer, inner, pl.ds(direction, 1), :]
+
+
+def later_weights_of(clusters, substep):
+    goes_on = clusters > 0
+    return [jnp.where(goes_on, w, 0.0) for w in taylor_weights(clusters, substep + 1)]
+
+
+def series(current, rows, stiff, weights, own, first, second, later=None, later_weights=None):
+    fields, basis, _ = own.shape
     start = 0
     for size in GROUPS:
         values = [current(start + i) for i in range(size)]
         for i in range(size):
             own[start + i] = values[i] * weights[0]
-        spatial(first, start, values)
+            if later is not None:
+                later[start + i] = values[i] * later_weights[0]
+        spatial(stiff, first, start, values)
         start += size
     source, target = first, second
     for degree in range(1, ORDER):
         start = 0
         for size in GROUPS:
-            total = [None] * size
-            for direction in range(3):
-                for inner in range(fields):
-                    value = source[
-                        direction * basis : (direction + 1) * basis,
-                        inner * cells : (inner + 1) * cells,
-                    ]
-                    for i in range(size):
-                        term = jac[start + i, inner, pl.ds(direction, 1), :] * value
-                        total[i] = term if total[i] is None else total[i] + term
+            total = mixed(rows, source, range(start, start + size), basis)
             for i in range(size):
                 own[start + i] += total[i] * weights[degree]
+                if later is not None:
+                    later[start + i] += total[i] * later_weights[degree]
             if degree < ORDER - 1:
-                spatial(target, start, total)
+                spatial(stiff, target, start, total)
             start += size
         source, target = target, source
+
+
+def split_columns(values):
+    high = values.astype(jnp.bfloat16)
+    low = (values - high.astype(jnp.float32)).astype(jnp.bfloat16)
+    return jnp.concatenate([high, low], axis=1)
+
+
+def short_series(current, paired, stiff, gather, scatter, later, own, total, first, second):
+    fields, basis, cells = own.shape
+    pairs = (fields + 1) // 2
+    left = lax.broadcasted_iota(jnp.int32, (1, cells), 1) < cells // 2
+    weights = [STEP_LENGTH ** (k + 1) / math.factorial(k + 1) for k in range(ORDER)]
+
+    def both(value):
+        turned = pltpu.roll(value, cells // 2, 1)
+        return [jnp.where(left, value, turned), jnp.where(left, turned, value)]
+
+    rows = jnp.concatenate([current(field) for field in range(fields)], axis=0)
+    picked = product(split_columns(rows), gather[...])
+    values = [picked[field * basis : (field + 1) * basis] for field in range(fields)]
+    for pair in range(pairs):
+        other = values[min(2 * pair + 1, fields - 1)]
+        total[pair * basis : (pair + 1) * basis, :] = (
+            jnp.where(left, values[2 * pair], other) * weights[0]
+        )
+    for start, size in ((0, 5), (5, 4)):
+        spatial(stiff, first, start, values[start : start + size])
+    source, target = first, second
+    for degree in range(1, ORDER):
+        start = 0
+        for size in PAIR_GROUPS:
+            sums = mixed(rows_of(paired), source, range(start, start + size), basis)
+            spread = []
+            for i in range(size):
+                total[(start + i) * basis : (start + i + 1) * basis, :] += sums[i] * weights[degree]
+                if degree < ORDER - 1:
+                    spread += both(sums[i])
+            if degree < ORDER - 1:
+                spatial(stiff, target, 2 * start, spread[: fields - 2 * start])
+            start += size
+        source, target = target, source
+    back = product(split_columns(total[...]), scatter[...])
+    for field in range(fields):
+        pair, half = divmod(field, 2)
+        own[field] = (
+            later[field] + back[pair * basis : (pair + 1) * basis, half * cells : (half + 1) * cells]
+        )
 
 
 def pack(own, picks, messages):
@@ -153,9 +222,9 @@
     stiffness_far, sends_far, clusters_far, coefficients_far, jac_far, *rest
 ):
     far, rest = rest[:7], rest[7:]
-    own, message_0, message_1, message_2, message_3, stiff, picks = rest[:7]
-    clusters, coefficients, jac, stiffness = rest[7:11]
-    near, (first, second, sends, arrived) = rest[11:18], rest[18:]
+    own, later, message_0, message_1, message_2, message_3, stiff, picks = rest[:8]
+    clusters, coefficients, jac, stiffness = rest[8:12]
+    near, (first, second, sends, arrived) = rest[12:19], rest[19:]
     fields, basis, cells = own.shape
     pairs = (
         (stiffness_far, stiffness),
@@ -188,31 +257,30 @@
     for copy in copies[2:5]:
         copy.wait()
     weights = taylor_weights(clusters[...], 0)
-    series(lambda field: coefficients[field], jac, stiff, weights, own, first, second)
+    series(
+        lambda field: coefficients[field], rows_of(jac), stiff, weights, own, first, second,
+        later, later_weights_of(clusters[...], 0),
+    )
     pack(own, picks, (message_0, message_1, message_2, message_3))
     for copy in copies[5:]:
         copy.wait()
 
 
-def local_kernel(own, jac, flux_local, matrices, local_hot, volume, local_flux, traces, spatial):
+def local_kernel(own, jac, flux_local, matrices, local_hot, volume, local_flux, traces, spatials):
+    local_part(
+        own, rows_of(jac), flux_local, matrices, local_hot, volume, local_flux, traces, spatials
+    )
+
+
+def local_part(own, rows, flux_local, matrices, local_hot, volume, local_flux, traces, spatial):
     fields, basis, cells = own.shape
     wide = traces.shape[0] // fields
     columns = jnp.concatenate([stacked(own[field]) for field in range(fields)], axis=1)
     spatial[...] = product(matrices[...], columns)
     start = 0
     for size in GROUPS:
-        total = [None] * size
-        for direction in range(3):
-            for inner in range(fields):
-                value = spatial[
-                    direction * basis : (direction + 1) * basis,
-                    inner * cells : (inner + 1) * cells,
-                ]
-                for i in range(size):
-                    term = jac[start + i, inner, pl.ds(direction, 1), :] * value
-                    total[i] = term if total[i] is None else total[i] + term
-        for i in range(size):
-            volume[start + i] = total[i]
+        for i, total in enumerate(mixed(rows, spatial, range(start, start + size), basis)):
+            volume[start + i] = total
         start += size
     base = 3 * basis
     for face in range(FACES):
@@ -245,9 +313,10 @@
 
 
 def first_local_kernel(
-    own, jac, flux_local, stiffness, face_proj, neigh_proj, lifting, slots, orientation,
+    own, jac, flux_local, stiffness, face_proj, neigh_proj, lifting, slots, orientation, clusters,
     volume, local_flux, traces, matrices, local_hot, halo_hot, halo_pairs, lift,
-    spatial, plain,
+    paired, gather, scatter,
+    spatial, plain, dense,
 ):
     fields, basis, cells = own.shape
     face_basis = face_proj.shape[0]
@@ -300,7 +369,49 @@
         (((1,), (1,)), ((), ())),
         preferred_element_type=jnp.float32,
     )
-    local_kernel(own, jac, flux_local, matrices, local_hot, volume, local_flux, traces, spatial)
+    compaction(clusters, jac, dense, paired, gather, scatter)
+    local_part(
+        own, rows_of(jac), flux_local, matrices, local_hot, volume, local_flux, traces, spatial
+    )
+
+
+def compaction(clusters, jac, dense, paired, gather, scatter):
+    fields, depth, cells = dense.shape
+    half = cells // 2
+    short = jnp.where(clusters[...] == 0, 1.0, 0.0)
+    before = jnp.where(
+        lax.broadcasted_iota(jnp.int32, (cells, cells), 0)
+        < lax.broadcasted_iota(jnp.int32, (cells, cells), 1),
+        1.0,
+        0.0,
+    ).astype(jnp.bfloat16)
+    rank = product(jnp.broadcast_to(short, (8, cells)).astype(jnp.bfloat16), before)[0:1, :]
+    place = jnp.where(short > 0.5, rank, -1.0)
+    row = lax.broadcasted_iota(jnp.int32, (cells, cells), 0)
+    hot = jnp.where(place == (row % half).astype(jnp.float32), 1.0, 0.0)
+    turned = hot.T.astype(jnp.bfloat16)
+    gather[0:cells, :] = turned
+    gather[cells : 2 * cells, :] = turned
+    sides = jnp.concatenate(
+        [jnp.where(row < half, hot, 0.0), jnp.where(row < half, 0.0, hot)], axis=1
+    ).astype(jnp.bfloat16)
+    scatter[0:cells, :] = sides
+    scatter[cells : 2 * cells, :] = sides
+    for outer in range(fields):
+        for inner in range(fields):
+            dense[outer, inner * 3 : inner * 3 + 3, :] = jac[outer, inner]
+        dense[outer, 3 * fields :, :] = jnp.zeros((depth - 3 * fields, cells), jnp.float32)
+    left = lax.broadcasted_iota(jnp.int32, (1, cells), 1) < half
+    picked = product(split_columns(dense[...].reshape(fields * depth, cells)), gather[...])
+    for pair in range(paired.shape[0]):
+        one = picked[2 * pair * depth : (2 * pair + 1) * depth]
+        if 2 * pair + 1 < fields:
+            two = picked[(2 * pair + 1) * depth : (2 * pair + 2) * depth]
+        else:
+            two = jnp.zeros_like(one)
+        both = jnp.where(left, one, two)
+        for inner in range(fields):
+            paired[pair, inner] = both[inner * 3 : inner * 3 + 3]
 
 
 def remote_part(messages, matrices, halo_hot, halo_pairs, traces):
@@ -377,13 +488,15 @@
 
 def step_kernel(
     substep,
-    coefficients, applied_in, pending_in, jac, stiff, clusters, picks,
-    in_0, in_1, in_2, in_3,
-    volume, local_flux, traces, flux_neigh, matrices, halo_hot, halo_pairs, lift,
-    applied, pending, own, message_0, message_1, message_2, message_3,
-    first, second,
+    coefficients, applied_in, pending_in, jac, stiff, clusters, picks, in_0, in_1, in_2, in_3,
+    volume, local_flux, traces, flux_neigh, matrices, halo_hot, halo_pairs, lift, *rest
 ):
-    fields = volume.shape[0]
+    if substep % 2 == 0:
+        (paired, gather, scatter, later, applied, pending, own, *messages), rest = rest[:11], rest[11:]
+        total, first, second = rest
+    else:
+        (applied, pending, own, later, *messages), (first, second) = rest[:8], rest[8:]
+    fields, _, cells = volume.shape
     remote = remote_part((in_0, in_1, in_2, in_3), matrices, halo_hot, halo_pairs, traces)
     updates = change(remote, volume, local_flux, flux_neigh, lift)
     _, done = time_phase(clusters[...], substep)
@@ -396,10 +509,26 @@
         applied[field] = passed + applied_in[field] if substep > 0 else passed
         pending[field] = jnp.where(finished, 0.0, waiting)
     weights = taylor_weights(clusters[...], substep + 1)
-    series(
-        lambda field: coefficients[field] + applied[field], jac, stiff, weights, own, first, second
-    )
-    pack(own, picks, (message_0, message_1, message_2, message_3))
+
+    def current(field):
+        return coefficients[field] + applied[field]
+
+    if substep % 2 == 0:
+        fits = jnp.sum(jnp.where(clusters[...] == 0, 1.0, 0.0)) <= cells // 2
+
+        @pl.when(fits)
+        def _():
+            short_series(current, paired, stiff, gather, scatter, later, own, total, first, second)
+
+        @pl.when(jnp.logical_not(fits))
+        def _():
+            series(current, rows_of(jac), stiff, weights, own, first, second)
+    else:
+        series(
+            current, rows_of(jac), stiff, weights, own, first, second,
+            later, later_weights_of(clusters[...], substep + 1),
+        )
+    pack(own, picks, messages)
 
 
 def last_kernel(
@@ -465,9 +594,9 @@
     first = [stiffness, send_list, clusters, coefficients, jacobians]
     later = [flux_local, flux_neigh, face_proj, neigh_proj, lifting, face_slots, orientation]
     near = [clusters, coefficients, jacobians, stiffness, *later]
-    own, *given = call(
+    own, later, *given = call(
         start_kernel,
-        [state] + [message] * 4 + [bf16(3 * basis, depth), bf16(2 * cells, 4 * cells)]
+        [state] * 2 + [message] * 4 + [bf16(3 * basis, depth), bf16(2 * cells, 4 * cells)]
         + [jax.ShapeDtypeStruct(x.shape, x.dtype) for x in near],
         [
             derived, derived, pltpu.VMEM(send_list.shape, send_list.dtype),
@@ -479,38 +608,54 @@
     clusters, coefficients, jacobians, stiffness = near[:4]
     flux_local, flux_neigh, face_proj, neigh_proj, lifting, face_slots, orientation = near[4:]
     local_outs = [state, f32(FACES, fields, wide, cells), f32(fields * wide, faces)]
+    spatials = pltpu.VMEM((rows, fields * cells), jnp.float32)
+    pairs = (fields + 1) // 2
+    depth = -(-3 * fields // 8) * 8
     applied = pending = coefficients
     for substep in range(SUBSTEPS):
         received = exchange(messages)
         if substep == 0:
-            volume, local_flux, traces, matrices, local_hot, halo_hot, halo_pairs, lift = call(
+            volume, local_flux, traces, *given = call(
                 first_local_kernel,
                 local_outs
                 + [
-                    bf16(rows, depth), bf16(ORIENTS * cells, faces), bf16(5 * cells, faces),
+                    bf16(rows, stiff.shape[1]), bf16(ORIENTS * cells, faces), bf16(5 * cells, faces),
                     f32(8, 5 * cells), bf16(basis, 3 * FACES * wide),
+                    f32(pairs, fields, 3, cells),
+                    bf16(2 * cells, cells), bf16(2 * cells, 2 * cells),
                 ],
-                [pltpu.VMEM((rows, fields * cells), jnp.float32), pltpu.VMEM((rows, basis), jnp.float32)], 1 << 27,
+                [
+                    spatials, pltpu.VMEM((rows, basis), jnp.float32),
+                    pltpu.VMEM((fields, depth, cells), jnp.float32),
+                ],
+                1 << 27,
                 own, jacobians, flux_local, stiffness, face_proj, neigh_proj, lifting,
-                face_slots, orientation,
+                face_slots, orientation, clusters,
             )
+            matrices, local_hot, halo_hot, halo_pairs, lift, *compact = given
         else:
             volume, local_flux, traces = call(
-                local_kernel, local_outs, [pltpu.VMEM((rows, fields * cells), jnp.float32)], 1 << 27,
+                local_kernel, local_outs, [spatials], 1 << 27,
                 own, jacobians, flux_local, matrices, local_hot,
             )
         rest = (
             *received, volume, local_flux, traces, flux_neigh, matrices, halo_hot, halo_pairs, lift,
         )
-        if substep < SUBSTEPS - 1:
+        if substep == SUBSTEPS - 1:
+            (increment,) = call(last_kernel, [state], [], 1 << 27, applied, pending, *rest)
+            return increment
+        most = (coefficients, applied, pending, jacobians, stiff, clusters, picks, *rest)
+        kernel = functools.partial(step_kernel, substep)
+        if substep % 2 == 0:
+            sums = pltpu.VMEM((pairs * basis, cells), jnp.float32)
             applied, pending, own, *messages = call(
-                functools.partial(step_kernel, substep),
-                [state] * 3 + [message] * 4, [derived, derived], 1 << 27,
-                coefficients, applied, pending, jacobians, stiff, clusters, picks, *rest,
+                kernel, [state] * 3 + [message] * 4, [sums, derived, derived], 1 << 27,
+                *most, *compact, later,
             )
         else:
-            (increment,) = call(last_kernel, [state], [], 1 << 27, applied, pending, *rest)
-    return increment
+            applied, pending, own, later, *messages = call(
+                kernel, [state] * 4 + [message] * 4, [derived, derived], 1 << 27, *most
+            )
 
 
 def solution(mesh):

time: 47 us -> 46.5 us (0.989)
  transfers between devices with their start and end apart: 16 -> 16, of which waited for: 4 -> 3; matrix products, arithmetic and copies ran while one was open for 0% -> 0% of each run, Pallas kernels for 18% -> 18%
where the time goes in v2:
time: 46.5 us; the launch traced here: 46.4 us
  Pallas kernels  28.8 us (62%)
  starting transfers between devices  13.7 us (29%)
  waiting for transfers between devices  3.76 us (8%)
    pallas_call x9, Pallas kernels, call(): pl.pallas_call(kernel, out_shape=outs, in_specs=[source] * len(operands),...  28.8 us
    ppermute x16, starting transfers between devices, exchange(): lax.ppermute(m, AXES, pairs)  13.7 us
    ppermute x16, waiting for transfers between devices, exchange(): lax.ppermute(m, AXES, pairs)  3.76 us
  transfers between devices with their start and end apart: 16, of which 3 were waited for; matrix products, arithmetic and copies ran while one was open for 0% of the time, Pallas kernels for 18%

profile of v2, /device:TPU:0, one launch (start us, length us, event | category | flops | bytes accessed | tf_op | source)
XLA Modules:
  0.0 46.4 jit_solution(10402146591978151433)
XLA Ops:
  0.0 5.0 %shard_map.118 = (f32[9,56,128]{2,1,0:T(8,128)S(1)}, f32[9,56,128]{2,1,0:T(8,128)S(1)}, f32[64,128]{1,0:T(8,128)S(1)}, f32[64,128]{1,0:T(8,128)S(1)}, f32[64,128...) custom-call(f32[3,56,56]{2,1,0:T(8,128)} %stiffness_far.1, ...), custom_call_target="tpu_custom_call" | custom-call | flops 134217728 | bytes 1048576 | tf_op jit(solution)/shard_map/pallas_call | solution.py:551
  5.1 0.5 %collective-permute-start = (f32[64,128]{1,0:T(8,128)S(1)}, f32[64,128]{1,0:T(8,128)S(1)}, u32[]{:S(2)}, u32[]{:S(2)}) collective-permute-start(f32[64,128]{1,0:T(8,128)S(1)} %get-tuple-element.71), channel_id=1, source_target_pairs={{0,1},{1,0},{2,3},{3,2},{4,5},{5,4},{6,7},{7,6},{8,9},{9,8},{10,11... | collective-permute-start | bytes 98312 | tf_op jit(solution)/shard_map/ppermute | solution.py:592
  5.6 2.6 %collective-permute-start.1 = (f32[64,128]{1,0:T(8,128)S(1)}, f32[64,128]{1,0:T(8,128)S(1)}, u32[]{:S(2)}, u32[]{:S(2)}) collective-permute-start(f32[64,128]{1,0:T(8,128)S(1)} %get-tuple-element.72), channel_id=1, source_target_pairs={{0,8},{1,2},{2,1},{3,4},{4,3},{5,6},{6,5},{7,15},{8,0},{9,10},{10,... | collective-permute-start | bytes 98312 | tf_op jit(solution)/shard_map/ppermute | solution.py:592
  8.2 0.1 collective-permute-start.2
  8.3 1.3 %collective-permute-start.3 = (f32[64,128]{1,0:T(8,128)S(1)}, f32[64,128]{1,0:T(8,128)S(1)}, u32[]{:S(2)}, u32[]{:S(2)}) collective-permute-start(f32[64,128]{1,0:T(8,128)S(1)} %get-tuple-element.74), channel_id=1, source_target_pairs={{0,1},{1,0},{2,3},{3,2},{4,5},{5,4},{6,7},{7,6},{8,16},{9,17},{10,... | collective-permute-start | bytes 98312 | tf_op jit(solution)/shard_map/ppermute | solution.py:592
  9.6 2.6 %shard_map.119 = (f32[9,56,128]{2,1,0:T(8,128)S(1)}, f32[4,9,24,128]{3,2,1,0:T(8,128)S(1)}, f32[216,512]{1,0:T(8,128)S(1)}, bf16[552,176]{1,0:T(8,128)(2,1)S(1)}...) custom-call(f32[9,56,128]{2,1,0:T(8,128)S(1)} %get-tuple-element.75., ...), custom_call_target="tpu_custom_call" | custom-call | flops 134217728 | bytes 1048576 | tf_op jit(solution)/shard_map/pallas_call | solution.py:551
  12.1 0.0 collective-permute-done.in_0
  12.1 0.0 collective-permute-done.3.in_3
  12.2 4.3 %shard_map.120 = (f32[9,56,128]{2,1,0:T(8,128)S(1)}, f32[9,56,128]{2,1,0:T(8,128)S(1)}, f32[9,56,128]{2,1,0:T(8,128)S(1)}, f32[64,128]{1,0:T(8,128)S(1)}, f32[64...) custom-call(f32[9,56,128]{2,1,0:T(8,128)S(1)} %get-tuple-element.66.coefficients.applied_in.pending_in, ...), custom_call_target="tpu_custom_call" | custom-call | flops 134217728 | bytes 1048576 | tf_op jit(solution)/shard_map/pallas_call | solution.py:551
  16.5 0.1 collective-permute-start.4
  16.5 2.8 %collective-permute-start.5 = (f32[64,128]{1,0:T(8,128)S(1)}, f32[64,128]{1,0:T(8,128)S(1)}, u32[]{:S(2)}, u32[]{:S(2)}) collective-permute-start(f32[64,128]{1,0:T(8,128)S(1)} %get-tuple-element.98), channel_id=1, source_target_pairs={{0,8},{1,2},{2,1},{3,4},{4,3},{5,6},{6,5},{7,15},{8,0},{9,10},{10,... | collective-permute-start | bytes 98312 | tf_op jit(solution)/shard_map/ppermute | solution.py:592
  19.4 0.0 collective-permute-start.6
  19.4 1.3 %collective-permute-start.7 = (f32[64,128]{1,0:T(8,128)S(1)}, f32[64,128]{1,0:T(8,128)S(1)}, u32[]{:S(2)}, u32[]{:S(2)}) collective-permute-start(f32[64,128]{1,0:T(8,128)S(1)} %get-tuple-element.100), channel_id=1, source_target_pairs={{0,1},{1,0},{2,3},{3,2},{4,5},{5,4},{6,7},{7,6},{8,16},{9,17},{10,... | collective-permute-start | bytes 98312 | tf_op jit(solution)/shard_map/ppermute | solution.py:592
  20.7 2.0 %shard_map.121 = (f32[9,56,128]{2,1,0:T(8,128)S(1)}, f32[4,9,24,128]{3,2,1,0:T(8,128)S(1)}, f32[216,512]{1,0:T(8,128)S(1)}) custom-call(f32[9,56,128]{2,1,0:T(8,128)S(1)} %get-tuple-element.101.own, f32[9,9,3,128]{3,2,1,0:T(4,128)S(1)} %get-tuple-element.67.jac, f32[9,9,4,128]{3,2,1,0:T(4,128)S(1)} %get-tuple-element.76.flux_local, ...), custom_call_target="tpu_custom_call" | custom-call | flops 134217728 | bytes 1048576 | tf_op jit(solution)/shard_map/pallas_call | solution.py:551
  22.7 0.0 collective-permute-done.4.in_0
  22.7 0.0 collective-permute-done.5.in_1
  22.7 0.6 %collective-permute-done.6.in_2 = f32[64,128]{1,0:T(8,128)S(1)} collective-permute-done((f32[64,128]{1,0:T(8,128)S(1)}, f32[64,128]{1,0:T(8,128)S(1)}, u32[]{:S(2)}, u32[]{:S(2)}) %collective-permute-start.6) | collective-permute-done | bytes 32800 | tf_op jit(solution)/shard_map/ppermute | solution.py:592
  23.3 4.8 %shard_map.122 = (f32[9,56,128]{2,1,0:T(8,128)S(1)}, f32[9,56,128]{2,1,0:T(8,128)S(1)}, f32[9,56,128]{2,1,0:T(8,128)S(1)}, f32[9,56,128]{2,1,0:T(8,128)S(1)}, f3...) custom-call(f32[9,56,128]{2,1,0:T(8,128)S(1)} %get-tuple-element.66.coefficients.app, ...), custom_call_target="tpu_custom_call" | custom-call | flops 134217728 | bytes 1048576 | tf_op jit(solution)/shard_map/pallas_call | solution.py:551
  28.1 0.1 collective-permute-start.8
  28.2 2.1 %collective-permute-start.9 = (f32[64,128]{1,0:T(8,128)S(1)}, f32[64,128]{1,0:T(8,128)S(1)}, u32[]{:S(2)}, u32[]{:S(2)}) collective-permute-start(f32[64,128]{1,0:T(8,128)S(1)} %get-tuple-element.109), channel_id=1, source_target_pairs={{0,8},{1,2},{2,1},{3,4},{4,3},{5,6},{6,5},{7,15},{8,0},{9,10},{10,... | collective-permute-start | bytes 98312 | tf_op jit(solution)/shard_map/ppermute | solution.py:592
  30.3 0.1 collective-permute-start.10
  30.4 0.4 collective-permute-start.11
  30.8 2.0 %shard_map.123 = (f32[9,56,128]{2,1,0:T(8,128)S(1)}, f32[4,9,24,128]{3,2,1,0:T(8,128)S(1)}, f32[216,512]{1,0:T(8,128)S(1)}) custom-call(f32[9,56,128]{2,1,0:T(8,128)S(1)} %get-tuple-element.112.own, f32[9,9,3,128]{3,2,1,0:T(4,128)S(1)} %get-tuple-element.67.jac, f32[9,9,4,128]{3,2,1,0:T(4,128)S(1)} %get-tuple-element.76.flux_local, ...), custom_call_target="tpu_custom_call" | custom-call | flops 134217728 | bytes 1048576 | tf_op jit(solution)/shard_map/pallas_call | solution.py:551
  32.8 1.4 %collective-permute-done.10.in_2 = f32[64,128]{1,0:T(8,128)S(1)} collective-permute-done((f32[64,128]{1,0:T(8,128)S(1)}, f32[64,128]{1,0:T(8,128)S(1)}, u32[]{:S(2)}, u32[]{:S(2)}) %collective-permute-start.10) | collective-permute-done | bytes 32800 | tf_op jit(solution)/shard_map/ppermute | solution.py:592
  34.2 4.3 %shard_map.124 = (f32[9,56,128]{2,1,0:T(8,128)S(1)}, f32[9,56,128]{2,1,0:T(8,128)S(1)}, f32[9,56,128]{2,1,0:T(8,128)S(1)}, f32[64,128]{1,0:T(8,128)S(1)}, f32[64...) custom-call(f32[9,56,128]{2,1,0:T(8,128)S(1)} %get-tuple-element.66.coefficients.applied_in.pending_in, ...), custom_call_target="tpu_custom_call" | custom-call | flops 134217728 | bytes 1048576 | tf_op jit(solution)/shard_map/pallas_call | solution.py:551
  38.5 0.1 collective-permute-start.12
  38.6 2.1 %collective-permute-start.13 = (f32[64,128]{1,0:T(8,128)S(1)}, f32[64,128]{1,0:T(8,128)S(1)}, u32[]{:S(2)}, u32[]{:S(2)}) collective-permute-start(f32[64,128]{1,0:T(8,128)S(1)} %get-tuple-element.120), channel_id=1, source_target_pairs={{0,8},{1,2},{2,1},{3,4},{4,3},{5,6},{6,5},{7,15},{8,0},{9,10},{10,... | collective-permute-start | bytes 98312 | tf_op jit(solution)/shard_map/ppermute | solution.py:592
  40.7 0.1 collective-permute-start.14
  40.8 0.1 collective-permute-start.15
  40.8 2.0 %shard_map.125 = (f32[9,56,128]{2,1,0:T(8,128)S(1)}, f32[4,9,24,128]{3,2,1,0:T(8,128)S(1)}, f32[216,512]{1,0:T(8,128)S(1)}) custom-call(f32[9,56,128]{2,1,0:T(8,128)S(1)} %get-tuple-element.123.own, f32[9,9,3,128]{3,2,1,0:T(4,128)S(1)} %get-tuple-element.67.jac, f32[9,9,4,128]{3,2,1,0:T(4,128)S(1)} %get-tuple-element.76.flux_local, ...), custom_call_target="tpu_custom_call" | custom-call | flops 134217728 | bytes 1048576 | tf_op jit(solution)/shard_map/pallas_call | solution.py:551
  42.9 1.7 %collective-permute-done.14.in_2 = f32[64,128]{1,0:T(8,128)S(1)} collective-permute-done((f32[64,128]{1,0:T(8,128)S(1)}, f32[64,128]{1,0:T(8,128)S(1)}, u32[]{:S(2)}, u32[]{:S(2)}) %collective-permute-start.14) | collective-permute-done | bytes 32800 | tf_op jit(solution)/shard_map/ppermute | solution.py:592
  44.6 1.8 %shard_map.126 = f32[9,56,128]{2,1,0:T(8,128)} custom-call(f32[9,56,128]{2,1,0:T(8,128)S(1)} %get-tuple-element.117.applied_in, f32[9,56,128]{2,1,0:T(8,128)S(1)} %get-tuple-element.118.pending_in, f32[64,128]{1,0:T(8,128)S(1)} %collective-permute-done.12.in_0, f32[64,128]{1,0:T(8,128)S(1)} %collective-permute-done.13.in_1, ...), custom_call_target="tpu_custom_call" | custom-call | flops 134217728 | bytes 1048576 | tf_op jit(solution)/shard_map/pallas_call | solution.py:551
  (9 shorter events, 0.0 us)
Async XLA Ops:
  5.1 7.1 %collective-permute-start = (f32[64,128]{1,0:T(8,128)S(1)}, f32[64,128]{1,0:T(8,128)S(1)}, u32[]{:S(2)}, u32[]{:S(2)}) collective-permute-start(f32[64,128]{1,0:T(8,128)S(1)} %get-tuple-element.71), channel_id=1, source_target_pairs={{0,1},{1,0},{2,3},{3,2},{4,5},{5,4},{6,7},{7,6},{8,9},{9,8},{10,11... | collective-permute-start | bytes 98312 | tf_op jit(solution)/shard_map/ppermute | solution.py:592
  5.6 6.6 %collective-permute-start.1 = (f32[64,128]{1,0:T(8,128)S(1)}, f32[64,128]{1,0:T(8,128)S(1)}, u32[]{:S(2)}, u32[]{:S(2)}) collective-permute-start(f32[64,128]{1,0:T(8,128)S(1)} %get-tuple-element.72), channel_id=1, source_target_pairs={{0,8},{1,2},{2,1},{3,4},{4,3},{5,6},{6,5},{7,15},{8,0},{9,10},{10,... | collective-permute-start | bytes 98312 | tf_op jit(solution)/shard_map/ppermute | solution.py:592
  8.2 3.9 %collective-permute-start.2 = (f32[64,128]{1,0:T(8,128)S(1)}, f32[64,128]{1,0:T(8,128)S(1)}, u32[]{:S(2)}, u32[]{:S(2)}) collective-permute-start(f32[64,128]{1,0:T(8,128)S(1)} %get-tuple-element.73), channel_id=1, source_target_pairs={{0,8},{1,9},{2,10},{3,11},{4,12},{5,13},{6,14},{7,15},{8,0},{9,1},... | collective-permute-start | bytes 98312 | tf_op jit(solution)/shard_map/ppermute | solution.py:592
  8.3 3.9 %collective-permute-start.3 = (f32[64,128]{1,0:T(8,128)S(1)}, f32[64,128]{1,0:T(8,128)S(1)}, u32[]{:S(2)}, u32[]{:S(2)}) collective-permute-start(f32[64,128]{1,0:T(8,128)S(1)} %get-tuple-element.74), channel_id=1, source_target_pairs={{0,1},{1,0},{2,3},{3,2},{4,5},{5,4},{6,7},{7,6},{8,16},{9,17},{10,... | collective-permute-start | bytes 98312 | tf_op jit(solution)/shard_map/ppermute | solution.py:592
  16.5 6.3 %collective-permute-start.4 = (f32[64,128]{1,0:T(8,128)S(1)}, f32[64,128]{1,0:T(8,128)S(1)}, u32[]{:S(2)}, u32[]{:S(2)}) collective-permute-start(f32[64,128]{1,0:T(8,128)S(1)} %get-tuple-element.97), channel_id=1, source_target_pairs={{0,1},{1,0},{2,3},{3,2},{4,5},{5,4},{6,7},{7,6},{8,9},{9,8},{10,11... | collective-permute-start | bytes 98312 | tf_op jit(solution)/shard_map/ppermute | solution.py:592
  16.5 6.2 %collective-permute-start.5 = (f32[64,128]{1,0:T(8,128)S(1)}, f32[64,128]{1,0:T(8,128)S(1)}, u32[]{:S(2)}, u32[]{:S(2)}) collective-permute-start(f32[64,128]{1,0:T(8,128)S(1)} %get-tuple-element.98), channel_id=1, source_target_pairs={{0,8},{1,2},{2,1},{3,4},{4,3},{5,6},{6,5},{7,15},{8,0},{9,10},{10,... | collective-permute-start | bytes 98312 | tf_op jit(solution)/shard_map/ppermute | solution.py:592
  19.4 3.9 %collective-permute-start.6 = (f32[64,128]{1,0:T(8,128)S(1)}, f32[64,128]{1,0:T(8,128)S(1)}, u32[]{:S(2)}, u32[]{:S(2)}) collective-permute-start(f32[64,128]{1,0:T(8,128)S(1)} %get-tuple-element.99), channel_id=1, source_target_pairs={{0,8},{1,9},{2,10},{3,11},{4,12},{5,13},{6,14},{7,15},{8,0},{9,1},... | collective-permute-start | bytes 98312 | tf_op jit(solution)/shard_map/ppermute | solution.py:592
  19.4 3.9 %collective-permute-start.7 = (f32[64,128]{1,0:T(8,128)S(1)}, f32[64,128]{1,0:T(8,128)S(1)}, u32[]{:S(2)}, u32[]{:S(2)}) collective-permute-start(f32[64,128]{1,0:T(8,128)S(1)} %get-tuple-element.100), channel_id=1, source_target_pairs={{0,1},{1,0},{2,3},{3,2},{4,5},{5,4},{6,7},{7,6},{8,16},{9,17},{10,... | collective-permute-start | bytes 98312 | tf_op jit(solution)/shard_map/ppermute | solution.py:592
  28.1 4.7 %collective-permute-start.8 = (f32[64,128]{1,0:T(8,128)S(1)}, f32[64,128]{1,0:T(8,128)S(1)}, u32[]{:S(2)}, u32[]{:S(2)}) collective-permute-start(f32[64,128]{1,0:T(8,128)S(1)} %get-tuple-element.108), channel_id=1, source_target_pairs={{0,1},{1,0},{2,3},{3,2},{4,5},{5,4},{6,7},{7,6},{8,9},{9,8},{10,11... | collective-permute-start | bytes 98312 | tf_op jit(solution)/shard_map/ppermute | solution.py:592
  28.2 4.6 %collective-permute-start.9 = (f32[64,128]{1,0:T(8,128)S(1)}, f32[64,128]{1,0:T(8,128)S(1)}, u32[]{:S(2)}, u32[]{:S(2)}) collective-permute-start(f32[64,128]{1,0:T(8,128)S(1)} %get-tuple-element.109), channel_id=1, source_target_pairs={{0,8},{1,2},{2,1},{3,4},{4,3},{5,6},{6,5},{7,15},{8,0},{9,10},{10,... | collective-permute-start | bytes 98312 | tf_op jit(solution)/shard_map/ppermute | solution.py:592
  30.3 3.9 %collective-permute-start.10 = (f32[64,128]{1,0:T(8,128)S(1)}, f32[64,128]{1,0:T(8,128)S(1)}, u32[]{:S(2)}, u32[]{:S(2)}) collective-permute-start(f32[64,128]{1,0:T(8,128)S(1)} %get-tuple-element.110), channel_id=1, source_target_pairs={{0,8},{1,9},{2,10},{3,11},{4,12},{5,13},{6,14},{7,15},{8,0},{9,1},... | collective-permute-start | bytes 98312 | tf_op jit(solution)/shard_map/ppermute | solution.py:592
  30.4 3.8 %collective-permute-start.11 = (f32[64,128]{1,0:T(8,128)S(1)}, f32[64,128]{1,0:T(8,128)S(1)}, u32[]{:S(2)}, u32[]{:S(2)}) collective-permute-start(f32[64,128]{1,0:T(8,128)S(1)} %get-tuple-element.111), channel_id=1, source_target_pairs={{0,1},{1,0},{2,3},{3,2},{4,5},{5,4},{6,7},{7,6},{8,16},{9,17},{10,... | collective-permute-start | bytes 98312 | tf_op jit(solution)/shard_map/ppermute | solution.py:592
  38.5 4.3 %collective-permute-start.12 = (f32[64,128]{1,0:T(8,128)S(1)}, f32[64,128]{1,0:T(8,128)S(1)}, u32[]{:S(2)}, u32[]{:S(2)}) collective-permute-start(f32[64,128]{1,0:T(8,128)S(1)} %get-tuple-element.119), channel_id=1, source_target_pairs={{0,1},{1,0},{2,3},{3,2},{4,5},{5,4},{6,7},{7,6},{8,9},{9,8},{10,11... | collective-permute-start | bytes 98312 | tf_op jit(solution)/shard_map/ppermute | solution.py:592
  38.6 4.2 %collective-permute-start.13 = (f32[64,128]{1,0:T(8,128)S(1)}, f32[64,128]{1,0:T(8,128)S(1)}, u32[]{:S(2)}, u32[]{:S(2)}) collective-permute-start(f32[64,128]{1,0:T(8,128)S(1)} %get-tuple-element.120), channel_id=1, source_target_pairs={{0,8},{1,2},{2,1},{3,4},{4,3},{5,6},{6,5},{7,15},{8,0},{9,10},{10,... | collective-permute-start | bytes 98312 | tf_op jit(solution)/shard_map/ppermute | solution.py:592
  40.7 3.9 %collective-permute-start.14 = (f32[64,128]{1,0:T(8,128)S(1)}, f32[64,128]{1,0:T(8,128)S(1)}, u32[]{:S(2)}, u32[]{:S(2)}) collective-permute-start(f32[64,128]{1,0:T(8,128)S(1)} %get-tuple-element.121), channel_id=1, source_target_pairs={{0,8},{1,9},{2,10},{3,11},{4,12},{5,13},{6,14},{7,15},{8,0},{9,1},... | collective-permute-start | bytes 98312 | tf_op jit(solution)/shard_map/ppermute | solution.py:592
  40.8 3.8 %collective-permute-start.15 = (f32[64,128]{1,0:T(8,128)S(1)}, f32[64,128]{1,0:T(8,128)S(1)}, u32[]{:S(2)}, u32[]{:S(2)}) collective-permute-start(f32[64,128]{1,0:T(8,128)S(1)} %get-tuple-element.122), channel_id=1, source_target_pairs={{0,1},{1,0},{2,3},{3,2},{4,5},{5,4},{6,7},{7,6},{8,16},{9,17},{10,... | collective-permute-start | bytes 98312 | tf_op jit(solution)/shard_map/ppermute | solution.py:592

commit v3 on v2

--- a/solution.py
+++ b/solution.py
@@ -147,13 +147,19 @@
         source, target = target, source
 
 
+def picked_lanes(values, places):
+    return jnp.take_along_axis(
+        values, jnp.broadcast_to(places, values.shape), axis=1, mode="promise_in_bounds"
+    )
+
+
 def split_columns(values):
     high = values.astype(jnp.bfloat16)
     low = (values - high.astype(jnp.float32)).astype(jnp.bfloat16)
     return jnp.concatenate([high, low], axis=1)
 
 
-def short_series(current, paired, stiff, gather, scatter, later, own, total, first, second):
+def short_series(current, paired, stiff, places, scatter, later, own, total, first, second):
     fields, basis, cells = own.shape
     pairs = (fields + 1) // 2
     left = lax.broadcasted_iota(jnp.int32, (1, cells), 1) < cells // 2
@@ -163,9 +169,7 @@
         turned = pltpu.roll(value, cells // 2, 1)
         return [jnp.where(left, value, turned), jnp.where(left, turned, value)]
 
-    rows = jnp.concatenate([current(field) for field in range(fields)], axis=0)
-    picked = product(split_columns(rows), gather[...])
-    values = [picked[field * basis : (field + 1) * basis] for field in range(fields)]
+    values = [picked_lanes(current(field), places[0:1, :]) for field in range(fields)]
     for pair in range(pairs):
         other = values[min(2 * pair + 1, fields - 1)]
         total[pair * basis : (pair + 1) * basis, :] = (
@@ -315,8 +319,8 @@
 def first_local_kernel(
     own, jac, flux_local, stiffness, face_proj, neigh_proj, lifting, slots, orientation, clusters,
     volume, local_flux, traces, matrices, local_hot, halo_hot, halo_pairs, lift,
-    paired, gather, scatter,
-    spatial, plain, dense,
+    paired, places, scatter,
+    spatial, plain,
 ):
     fields, basis, cells = own.shape
     face_basis = face_proj.shape[0]
@@ -369,49 +373,43 @@
         (((1,), (1,)), ((), ())),
         preferred_element_type=jnp.float32,
     )
-    compaction(clusters, jac, dense, paired, gather, scatter)
+    compaction(clusters, jac, paired, places, scatter)
     local_part(
         own, rows_of(jac), flux_local, matrices, local_hot, volume, local_flux, traces, spatial
     )
 
 
-def compaction(clusters, jac, dense, paired, gather, scatter):
-    fields, depth, cells = dense.shape
+def compaction(clusters, jac, paired, places, scatter):
+    fields = jac.shape[0]
+    cells = clusters.shape[1]
     half = cells // 2
     short = jnp.where(clusters[...] == 0, 1.0, 0.0)
-    before = jnp.where(
-        lax.broadcasted_iota(jnp.int32, (cells, cells), 0)
-        < lax.broadcasted_iota(jnp.int32, (cells, cells), 1),
-        1.0,
-        0.0,
-    ).astype(jnp.bfloat16)
+    row = lax.broadcasted_iota(jnp.int32, (cells, cells), 0)
+    column = lax.broadcasted_iota(jnp.int32, (cells, cells), 1)
+    before = jnp.where(row < column, 1.0, 0.0).astype(jnp.bfloat16)
     rank = product(jnp.broadcast_to(short, (8, cells)).astype(jnp.bfloat16), before)[0:1, :]
-    place = jnp.where(short > 0.5, rank, -1.0)
-    row = lax.broadcasted_iota(jnp.int32, (cells, cells), 0)
-    hot = jnp.where(place == (row % half).astype(jnp.float32), 1.0, 0.0)
-    turned = hot.T.astype(jnp.bfloat16)
-    gather[0:cells, :] = turned
-    gather[cells : 2 * cells, :] = turned
+    rank = jnp.where(short > 0.5, rank, -1.0)
+    hot = jnp.where(rank == (row % half).astype(jnp.float32), 1.0, 0.0)
+    element = column[0:8, :].astype(jnp.float32).astype(jnp.bfloat16)
+    place = lax.dot_general(
+        element, hot.astype(jnp.bfloat16), (((1,), (1,)), ((), ())),
+        preferred_element_type=jnp.float32,
+    ).astype(jnp.int32)
+    places[...] = place
     sides = jnp.concatenate(
         [jnp.where(row < half, hot, 0.0), jnp.where(row < half, 0.0, hot)], axis=1
     ).astype(jnp.bfloat16)
     scatter[0:cells, :] = sides
     scatter[cells : 2 * cells, :] = sides
-    for outer in range(fields):
+    left = column[0:1, :] < half
+    for pair in range(paired.shape[0]):
         for inner in range(fields):
-            dense[outer, inner * 3 : inner * 3 + 3, :] = jac[outer, inner]
-        dense[outer, 3 * fields :, :] = jnp.zeros((depth - 3 * fields, cells), jnp.float32)
-    left = lax.broadcasted_iota(jnp.int32, (1, cells), 1) < half
-    picked = product(split_columns(dense[...].reshape(fields * depth, cells)), gather[...])
-    for pair in range(paired.shape[0]):
-        one = picked[2 * pair * depth : (2 * pair + 1) * depth]
-        if 2 * pair + 1 < fields:
-            two = picked[(2 * pair + 1) * depth : (2 * pair + 2) * depth]
-        else:
-            two = jnp.zeros_like(one)
-        both = jnp.where(left, one, two)
-        for inner in range(fields):
-            paired[pair, inner] = both[inner * 3 : inner * 3 + 3]
+            one = picked_lanes(jac[2 * pair, inner], place[0:1, :])
+            if 2 * pair + 1 < fields:
+                two = picked_lanes(jac[2 * pair + 1, inner], place[0:1, :])
+            else:
+                two = jnp.zeros_like(one)
+            paired[pair, inner] = jnp.where(left, one, two)
 
 
 def remote_part(messages, matrices, halo_hot, halo_pairs, traces):
@@ -492,11 +490,13 @@
     volume, local_flux, traces, flux_neigh, matrices, halo_hot, halo_pairs, lift, *rest
 ):
     if substep % 2 == 0:
-        (paired, gather, scatter, later, applied, pending, own, *messages), rest = rest[:11], rest[11:]
+        (paired, places, scatter, later, applied, pending, own, *messages), rest = rest[:11], rest[11:]
         total, first, second = rest
     else:
         (applied, pending, own, later, *messages), (first, second) = rest[:8], rest[8:]
     fields, _, cells = volume.shape
+    if substep % 2 == 0:
+        fits = jnp.sum(jnp.where(clusters[...] == 0, 1.0, 0.0)) <= cells // 2
     remote = remote_part((in_0, in_1, in_2, in_3), matrices, halo_hot, halo_pairs, traces)
     updates = change(remote, volume, local_flux, flux_neigh, lift)
     _, done = time_phase(clusters[...], substep)
@@ -514,11 +514,10 @@
         return coefficients[field] + applied[field]
 
     if substep % 2 == 0:
-        fits = jnp.sum(jnp.where(clusters[...] == 0, 1.0, 0.0)) <= cells // 2
 
         @pl.when(fits)
         def _():
-            short_series(current, paired, stiff, gather, scatter, later, own, total, first, second)
+            short_series(current, paired, stiff, places, scatter, later, own, total, first, second)
 
         @pl.when(jnp.logical_not(fits))
         def _():
@@ -610,7 +609,6 @@
     local_outs = [state, f32(FACES, fields, wide, cells), f32(fields * wide, faces)]
     spatials = pltpu.VMEM((rows, fields * cells), jnp.float32)
     pairs = (fields + 1) // 2
-    depth = -(-3 * fields // 8) * 8
     applied = pending = coefficients
     for substep in range(SUBSTEPS):
         received = exchange(messages)
@@ -622,11 +620,10 @@
                     bf16(rows, stiff.shape[1]), bf16(ORIENTS * cells, faces), bf16(5 * cells, faces),
                     f32(8, 5 * cells), bf16(basis, 3 * FACES * wide),
                     f32(pairs, fields, 3, cells),
-                    bf16(2 * cells, cells), bf16(2 * cells, 2 * cells),
+                    jax.ShapeDtypeStruct((8, cells), jnp.int32), bf16(2 * cells, 2 * cells),
                 ],
                 [
                     spatials, pltpu.VMEM((rows, basis), jnp.float32),
-                    pltpu.VMEM((fields, depth, cells), jnp.float32),
                 ],
                 1 << 27,
                 own, jacobians, flux_local, stiffness, face_proj, neigh_proj, lifting,

time: 46.5 us -> 46 us (0.989)
  Pallas kernels: 28.8 us -> 28.3 us
    pallas_call x9, Pallas kernels: 28.8 us -> 28.3 us  [call(): pl.pallas_call(kernel, out_shape=outs, in_specs=[source] * len(operands),...]
  transfers between devices with their start and end apart: 16 -> 16, of which waited for: 3 -> 4; matrix products, arithmetic and copies ran while one was open for 0% -> 0% of each run, Pallas kernels for 18% -> 18%
where the time goes in v3:
time: 46 us; the launch traced here: 45.9 us
  Pallas kernels  28.3 us (62%)
  starting transfers between devices  13.8 us (30%)
  waiting for transfers between devices  3.7 us (8%)
    pallas_call x9, Pallas kernels, call(): pl.pallas_call(kernel, out_shape=outs, in_specs=[source] * len(operands),...  28.3 us
    ppermute x16, starting transfers between devices, exchange(): lax.ppermute(m, AXES, pairs)  13.8 us
    ppermute x16, waiting for transfers between devices, exchange(): lax.ppermute(m, AXES, pairs)  3.7 us
  transfers between devices with their start and end apart: 16, of which 4 were waited for; matrix products, arithmetic and copies ran while one was open for 0% of the time, Pallas kernels for 18%

profile of v3, /device:TPU:0, one launch (start us, length us, event | category | flops | bytes accessed | tf_op | source)
XLA Modules:
  0.0 45.9 jit_solution(9973973990059313001)
XLA Ops:
  0.0 5.0 %shard_map.118 = (f32[9,56,128]{2,1,0:T(8,128)S(1)}, f32[9,56,128]{2,1,0:T(8,128)S(1)}, f32[64,128]{1,0:T(8,128)S(1)}, f32[64,128]{1,0:T(8,128)S(1)}, f32[64,128...) custom-call(f32[3,56,56]{2,1,0:T(8,128)} %stiffness_far.1, ...), custom_call_target="tpu_custom_call" | custom-call | flops 134217728 | bytes 1048576 | tf_op jit(solution)/shard_map/pallas_call | solution.py:550
  5.0 0.5 %collective-permute-start = (f32[64,128]{1,0:T(8,128)S(1)}, f32[64,128]{1,0:T(8,128)S(1)}, u32[]{:S(2)}, u32[]{:S(2)}) collective-permute-start(f32[64,128]{1,0:T(8,128)S(1)} %get-tuple-element.71), channel_id=1, source_target_pairs={{0,1},{1,0},{2,3},{3,2},{4,5},{5,4},{6,7},{7,6},{8,9},{9,8},{10,11... | collective-permute-start | bytes 98312 | tf_op jit(solution)/shard_map/ppermute | solution.py:591
  5.5 2.6 %collective-permute-start.1 = (f32[64,128]{1,0:T(8,128)S(1)}, f32[64,128]{1,0:T(8,128)S(1)}, u32[]{:S(2)}, u32[]{:S(2)}) collective-permute-start(f32[64,128]{1,0:T(8,128)S(1)} %get-tuple-element.72), channel_id=1, source_target_pairs={{0,8},{1,2},{2,1},{3,4},{4,3},{5,6},{6,5},{7,15},{8,0},{9,10},{10,... | collective-permute-start | bytes 98312 | tf_op jit(solution)/shard_map/ppermute | solution.py:591
  8.2 0.1 collective-permute-start.2
  8.3 1.3 %collective-permute-start.3 = (f32[64,128]{1,0:T(8,128)S(1)}, f32[64,128]{1,0:T(8,128)S(1)}, u32[]{:S(2)}, u32[]{:S(2)}) collective-permute-start(f32[64,128]{1,0:T(8,128)S(1)} %get-tuple-element.74), channel_id=1, source_target_pairs={{0,1},{1,0},{2,3},{3,2},{4,5},{5,4},{6,7},{7,6},{8,16},{9,17},{10,... | collective-permute-start | bytes 98312 | tf_op jit(solution)/shard_map/ppermute | solution.py:591
  9.5 2.3 %shard_map.119 = (f32[9,56,128]{2,1,0:T(8,128)S(1)}, f32[4,9,24,128]{3,2,1,0:T(8,128)S(1)}, f32[216,512]{1,0:T(8,128)S(1)}, bf16[552,176]{1,0:T(8,128)(2,1)S(1)}...) custom-call(f32[9,56,128]{2,1,0:T(8,128)S(1)} %get-tuple-element.75., ...), custom_call_target="tpu_custom_call" | custom-call | flops 134217728 | bytes 1048576 | tf_op jit(solution)/shard_map/pallas_call | solution.py:550
  11.9 0.0 collective-permute-done.1.in_1
  11.9 0.2 collective-permute-done.2.in_2
  12.1 0.0 collective-permute-done.3.in_3
  12.1 4.1 %shard_map.120 = (f32[9,56,128]{2,1,0:T(8,128)S(1)}, f32[9,56,128]{2,1,0:T(8,128)S(1)}, f32[9,56,128]{2,1,0:T(8,128)S(1)}, f32[64,128]{1,0:T(8,128)S(1)}, f32[64...) custom-call(f32[9,56,128]{2,1,0:T(8,128)S(1)} %get-tuple-element.66.coefficients.applied_in.pending_in, ...), custom_call_target="tpu_custom_call" | custom-call | flops 134217728 | bytes 1048576 | tf_op jit(solution)/shard_map/pallas_call | solution.py:550
  16.3 0.1 collective-permute-start.4
  16.3 2.7 %collective-permute-start.5 = (f32[64,128]{1,0:T(8,128)S(1)}, f32[64,128]{1,0:T(8,128)S(1)}, u32[]{:S(2)}, u32[]{:S(2)}) collective-permute-start(f32[64,128]{1,0:T(8,128)S(1)} %get-tuple-element.98), channel_id=1, source_target_pairs={{0,8},{1,2},{2,1},{3,4},{4,3},{5,6},{6,5},{7,15},{8,0},{9,10},{10,... | collective-permute-start | bytes 98312 | tf_op jit(solution)/shard_map/ppermute | solution.py:591
  19.0 0.0 collective-permute-start.6
  19.1 1.3 %collective-permute-start.7 = (f32[64,128]{1,0:T(8,128)S(1)}, f32[64,128]{1,0:T(8,128)S(1)}, u32[]{:S(2)}, u32[]{:S(2)}) collective-permute-start(f32[64,128]{1,0:T(8,128)S(1)} %get-tuple-element.100), channel_id=1, source_target_pairs={{0,1},{1,0},{2,3},{3,2},{4,5},{5,4},{6,7},{7,6},{8,16},{9,17},{10,... | collective-permute-start | bytes 98312 | tf_op jit(solution)/shard_map/ppermute | solution.py:591
  20.4 2.0 %shard_map.121 = (f32[9,56,128]{2,1,0:T(8,128)S(1)}, f32[4,9,24,128]{3,2,1,0:T(8,128)S(1)}, f32[216,512]{1,0:T(8,128)S(1)}) custom-call(f32[9,56,128]{2,1,0:T(8,128)S(1)} %get-tuple-element.101.own, f32[9,9,3,128]{3,2,1,0:T(4,128)S(1)} %get-tuple-element.67.jac, f32[9,9,4,128]{3,2,1,0:T(4,128)S(1)} %get-tuple-element.76.flux_local, ...), custom_call_target="tpu_custom_call" | custom-call | flops 134217728 | bytes 1048576 | tf_op jit(solution)/shard_map/pallas_call | solution.py:550
  22.4 0.0 collective-permute-done.4.in_0
  22.4 0.6 %collective-permute-done.6.in_2 = f32[64,128]{1,0:T(8,128)S(1)} collective-permute-done((f32[64,128]{1,0:T(8,128)S(1)}, f32[64,128]{1,0:T(8,128)S(1)}, u32[]{:S(2)}, u32[]{:S(2)}) %collective-permute-start.6) | collective-permute-done | bytes 32800 | tf_op jit(solution)/shard_map/ppermute | solution.py:591
  23.0 4.8 %shard_map.122 = (f32[9,56,128]{2,1,0:T(8,128)S(1)}, f32[9,56,128]{2,1,0:T(8,128)S(1)}, f32[9,56,128]{2,1,0:T(8,128)S(1)}, f32[9,56,128]{2,1,0:T(8,128)S(1)}, f3...) custom-call(f32[9,56,128]{2,1,0:T(8,128)S(1)} %get-tuple-element.66.coefficients.app, ...), custom_call_target="tpu_custom_call" | custom-call | flops 134217728 | bytes 1048576 | tf_op jit(solution)/shard_map/pallas_call | solution.py:550
  27.7 0.1 collective-permute-start.8
  27.8 2.1 %collective-permute-start.9 = (f32[64,128]{1,0:T(8,128)S(1)}, f32[64,128]{1,0:T(8,128)S(1)}, u32[]{:S(2)}, u32[]{:S(2)}) collective-permute-start(f32[64,128]{1,0:T(8,128)S(1)} %get-tuple-element.109), channel_id=1, source_target_pairs={{0,8},{1,2},{2,1},{3,4},{4,3},{5,6},{6,5},{7,15},{8,0},{9,10},{10,... | collective-permute-start | bytes 98312 | tf_op jit(solution)/shard_map/ppermute | solution.py:591
  29.9 0.1 collective-permute-start.10
  30.0 0.6 %collective-permute-start.11 = (f32[64,128]{1,0:T(8,128)S(1)}, f32[64,128]{1,0:T(8,128)S(1)}, u32[]{:S(2)}, u32[]{:S(2)}) collective-permute-start(f32[64,128]{1,0:T(8,128)S(1)} %get-tuple-element.111), channel_id=1, source_target_pairs={{0,1},{1,0},{2,3},{3,2},{4,5},{5,4},{6,7},{7,6},{8,16},{9,17},{10,... | collective-permute-start | bytes 98312 | tf_op jit(solution)/shard_map/ppermute | solution.py:591
  30.6 2.0 %shard_map.123 = (f32[9,56,128]{2,1,0:T(8,128)S(1)}, f32[4,9,24,128]{3,2,1,0:T(8,128)S(1)}, f32[216,512]{1,0:T(8,128)S(1)}) custom-call(f32[9,56,128]{2,1,0:T(8,128)S(1)} %get-tuple-element.112.own, f32[9,9,3,128]{3,2,1,0:T(4,128)S(1)} %get-tuple-element.67.jac, f32[9,9,4,128]{3,2,1,0:T(4,128)S(1)} %get-tuple-element.76.flux_local, ...), custom_call_target="tpu_custom_call" | custom-call | flops 134217728 | bytes 1048576 | tf_op jit(solution)/shard_map/pallas_call | solution.py:550
  32.7 1.2 %collective-permute-done.10.in_2 = f32[64,128]{1,0:T(8,128)S(1)} collective-permute-done((f32[64,128]{1,0:T(8,128)S(1)}, f32[64,128]{1,0:T(8,128)S(1)}, u32[]{:S(2)}, u32[]{:S(2)}) %collective-permute-start.10) | collective-permute-done | bytes 32800 | tf_op jit(solution)/shard_map/ppermute | solution.py:591
  33.8 4.2 %shard_map.124 = (f32[9,56,128]{2,1,0:T(8,128)S(1)}, f32[9,56,128]{2,1,0:T(8,128)S(1)}, f32[9,56,128]{2,1,0:T(8,128)S(1)}, f32[64,128]{1,0:T(8,128)S(1)}, f32[64...) custom-call(f32[9,56,128]{2,1,0:T(8,128)S(1)} %get-tuple-element.66.coefficients.applied_in.pending_in, ...), custom_call_target="tpu_custom_call" | custom-call | flops 134217728 | bytes 1048576 | tf_op jit(solution)/shard_map/pallas_call | solution.py:550
  38.0 0.1 collective-permute-start.12
  38.1 2.1 %collective-permute-start.13 = (f32[64,128]{1,0:T(8,128)S(1)}, f32[64,128]{1,0:T(8,128)S(1)}, u32[]{:S(2)}, u32[]{:S(2)}) collective-permute-start(f32[64,128]{1,0:T(8,128)S(1)} %get-tuple-element.120), channel_id=1, source_target_pairs={{0,8},{1,2},{2,1},{3,4},{4,3},{5,6},{6,5},{7,15},{8,0},{9,10},{10,... | collective-permute-start | bytes 98312 | tf_op jit(solution)/shard_map/ppermute | solution.py:591
  40.2 0.1 collective-permute-start.14
  40.3 0.1 collective-permute-start.15
  40.3 2.0 %shard_map.125 = (f32[9,56,128]{2,1,0:T(8,128)S(1)}, f32[4,9,24,128]{3,2,1,0:T(8,128)S(1)}, f32[216,512]{1,0:T(8,128)S(1)}) custom-call(f32[9,56,128]{2,1,0:T(8,128)S(1)} %get-tuple-element.123.own, f32[9,9,3,128]{3,2,1,0:T(4,128)S(1)} %get-tuple-element.67.jac, f32[9,9,4,128]{3,2,1,0:T(4,128)S(1)} %get-tuple-element.76.flux_local, ...), custom_call_target="tpu_custom_call" | custom-call | flops 134217728 | bytes 1048576 | tf_op jit(solution)/shard_map/pallas_call | solution.py:550
  42.4 1.7 %collective-permute-done.14.in_2 = f32[64,128]{1,0:T(8,128)S(1)} collective-permute-done((f32[64,128]{1,0:T(8,128)S(1)}, f32[64,128]{1,0:T(8,128)S(1)}, u32[]{:S(2)}, u32[]{:S(2)}) %collective-permute-start.14) | collective-permute-done | bytes 32800 | tf_op jit(solution)/shard_map/ppermute | solution.py:591
  44.1 1.8 %shard_map.126 = f32[9,56,128]{2,1,0:T(8,128)} custom-call(f32[9,56,128]{2,1,0:T(8,128)S(1)} %get-tuple-element.117.applied_in, f32[9,56,128]{2,1,0:T(8,128)S(1)} %get-tuple-element.118.pending_in, f32[64,128]{1,0:T(8,128)S(1)} %collective-permute-done.12.in_0, f32[64,128]{1,0:T(8,128)S(1)} %collective-permute-done.13.in_1, ...), custom_call_target="tpu_custom_call" | custom-call | flops 134217728 | bytes 1048576 | tf_op jit(solution)/shard_map/pallas_call | solution.py:550
  (9 shorter events, 0.0 us)
Async XLA Ops:
  5.0 6.8 %collective-permute-start = (f32[64,128]{1,0:T(8,128)S(1)}, f32[64,128]{1,0:T(8,128)S(1)}, u32[]{:S(2)}, u32[]{:S(2)}) collective-permute-start(f32[64,128]{1,0:T(8,128)S(1)} %get-tuple-element.71), channel_id=1, source_target_pairs={{0,1},{1,0},{2,3},{3,2},{4,5},{5,4},{6,7},{7,6},{8,9},{9,8},{10,11... | collective-permute-start | bytes 98312 | tf_op jit(solution)/shard_map/ppermute | solution.py:591
  5.5 6.3 %collective-permute-start.1 = (f32[64,128]{1,0:T(8,128)S(1)}, f32[64,128]{1,0:T(8,128)S(1)}, u32[]{:S(2)}, u32[]{:S(2)}) collective-permute-start(f32[64,128]{1,0:T(8,128)S(1)} %get-tuple-element.72), channel_id=1, source_target_pairs={{0,8},{1,2},{2,1},{3,4},{4,3},{5,6},{6,5},{7,15},{8,0},{9,10},{10,... | collective-permute-start | bytes 98312 | tf_op jit(solution)/shard_map/ppermute | solution.py:591
  8.2 3.9 %collective-permute-start.2 = (f32[64,128]{1,0:T(8,128)S(1)}, f32[64,128]{1,0:T(8,128)S(1)}, u32[]{:S(2)}, u32[]{:S(2)}) collective-permute-start(f32[64,128]{1,0:T(8,128)S(1)} %get-tuple-element.73), channel_id=1, source_target_pairs={{0,8},{1,9},{2,10},{3,11},{4,12},{5,13},{6,14},{7,15},{8,0},{9,1},... | collective-permute-start | bytes 98312 | tf_op jit(solution)/shard_map/ppermute | solution.py:591
  8.3 3.8 %collective-permute-start.3 = (f32[64,128]{1,0:T(8,128)S(1)}, f32[64,128]{1,0:T(8,128)S(1)}, u32[]{:S(2)}, u32[]{:S(2)}) collective-permute-start(f32[64,128]{1,0:T(8,128)S(1)} %get-tuple-element.74), channel_id=1, source_target_pairs={{0,1},{1,0},{2,3},{3,2},{4,5},{5,4},{6,7},{7,6},{8,16},{9,17},{10,... | collective-permute-start | bytes 98312 | tf_op jit(solution)/shard_map/ppermute | solution.py:591
  16.3 6.1 %collective-permute-start.4 = (f32[64,128]{1,0:T(8,128)S(1)}, f32[64,128]{1,0:T(8,128)S(1)}, u32[]{:S(2)}, u32[]{:S(2)}) collective-permute-start(f32[64,128]{1,0:T(8,128)S(1)} %get-tuple-element.97), channel_id=1, source_target_pairs={{0,1},{1,0},{2,3},{3,2},{4,5},{5,4},{6,7},{7,6},{8,9},{9,8},{10,11... | collective-permute-start | bytes 98312 | tf_op jit(solution)/shard_map/ppermute | solution.py:591
  16.3 6.1 %collective-permute-start.5 = (f32[64,128]{1,0:T(8,128)S(1)}, f32[64,128]{1,0:T(8,128)S(1)}, u32[]{:S(2)}, u32[]{:S(2)}) collective-permute-start(f32[64,128]{1,0:T(8,128)S(1)} %get-tuple-element.98), channel_id=1, source_target_pairs={{0,8},{1,2},{2,1},{3,4},{4,3},{5,6},{6,5},{7,15},{8,0},{9,10},{10,... | collective-permute-start | bytes 98312 | tf_op jit(solution)/shard_map/ppermute | solution.py:591
  19.0 3.9 %collective-permute-start.6 = (f32[64,128]{1,0:T(8,128)S(1)}, f32[64,128]{1,0:T(8,128)S(1)}, u32[]{:S(2)}, u32[]{:S(2)}) collective-permute-start(f32[64,128]{1,0:T(8,128)S(1)} %get-tuple-element.99), channel_id=1, source_target_pairs={{0,8},{1,9},{2,10},{3,11},{4,12},{5,13},{6,14},{7,15},{8,0},{9,1},... | collective-permute-start | bytes 98312 | tf_op jit(solution)/shard_map/ppermute | solution.py:591
  19.1 3.9 %collective-permute-start.7 = (f32[64,128]{1,0:T(8,128)S(1)}, f32[64,128]{1,0:T(8,128)S(1)}, u32[]{:S(2)}, u32[]{:S(2)}) collective-permute-start(f32[64,128]{1,0:T(8,128)S(1)} %get-tuple-element.100), channel_id=1, source_target_pairs={{0,1},{1,0},{2,3},{3,2},{4,5},{5,4},{6,7},{7,6},{8,16},{9,17},{10,... | collective-permute-start | bytes 98312 | tf_op jit(solution)/shard_map/ppermute | solution.py:591
  27.7 4.9 %collective-permute-start.8 = (f32[64,128]{1,0:T(8,128)S(1)}, f32[64,128]{1,0:T(8,128)S(1)}, u32[]{:S(2)}, u32[]{:S(2)}) collective-permute-start(f32[64,128]{1,0:T(8,128)S(1)} %get-tuple-element.108), channel_id=1, source_target_pairs={{0,1},{1,0},{2,3},{3,2},{4,5},{5,4},{6,7},{7,6},{8,9},{9,8},{10,11... | collective-permute-start | bytes 98312 | tf_op jit(solution)/shard_map/ppermute | solution.py:591
  27.8 4.8 %collective-permute-start.9 = (f32[64,128]{1,0:T(8,128)S(1)}, f32[64,128]{1,0:T(8,128)S(1)}, u32[]{:S(2)}, u32[]{:S(2)}) collective-permute-start(f32[64,128]{1,0:T(8,128)S(1)} %get-tuple-element.109), channel_id=1, source_target_pairs={{0,8},{1,2},{2,1},{3,4},{4,3},{5,6},{6,5},{7,15},{8,0},{9,10},{10,... | collective-permute-start | bytes 98312 | tf_op jit(solution)/shard_map/ppermute | solution.py:591
  29.9 3.9 %collective-permute-start.10 = (f32[64,128]{1,0:T(8,128)S(1)}, f32[64,128]{1,0:T(8,128)S(1)}, u32[]{:S(2)}, u32[]{:S(2)}) collective-permute-start(f32[64,128]{1,0:T(8,128)S(1)} %get-tuple-element.110), channel_id=1, source_target_pairs={{0,8},{1,9},{2,10},{3,11},{4,12},{5,13},{6,14},{7,15},{8,0},{9,1},... | collective-permute-start | bytes 98312 | tf_op jit(solution)/shard_map/ppermute | solution.py:591
  30.0 3.8 %collective-permute-start.11 = (f32[64,128]{1,0:T(8,128)S(1)}, f32[64,128]{1,0:T(8,128)S(1)}, u32[]{:S(2)}, u32[]{:S(2)}) collective-permute-start(f32[64,128]{1,0:T(8,128)S(1)} %get-tuple-element.111), channel_id=1, source_target_pairs={{0,1},{1,0},{2,3},{3,2},{4,5},{5,4},{6,7},{7,6},{8,16},{9,17},{10,... | collective-permute-start | bytes 98312 | tf_op jit(solution)/shard_map/ppermute | solution.py:591
  38.0 4.3 %collective-permute-start.12 = (f32[64,128]{1,0:T(8,128)S(1)}, f32[64,128]{1,0:T(8,128)S(1)}, u32[]{:S(2)}, u32[]{:S(2)}) collective-permute-start(f32[64,128]{1,0:T(8,128)S(1)} %get-tuple-element.119), channel_id=1, source_target_pairs={{0,1},{1,0},{2,3},{3,2},{4,5},{5,4},{6,7},{7,6},{8,9},{9,8},{10,11... | collective-permute-start | bytes 98312 | tf_op jit(solution)/shard_map/ppermute | solution.py:591
  38.1 4.3 %collective-permute-start.13 = (f32[64,128]{1,0:T(8,128)S(1)}, f32[64,128]{1,0:T(8,128)S(1)}, u32[]{:S(2)}, u32[]{:S(2)}) collective-permute-start(f32[64,128]{1,0:T(8,128)S(1)} %get-tuple-element.120), channel_id=1, source_target_pairs={{0,8},{1,2},{2,1},{3,4},{4,3},{5,6},{6,5},{7,15},{8,0},{9,10},{10,... | collective-permute-start | bytes 98312 | tf_op jit(solution)/shard_map/ppermute | solution.py:591
  40.2 3.9 %collective-permute-start.14 = (f32[64,128]{1,0:T(8,128)S(1)}, f32[64,128]{1,0:T(8,128)S(1)}, u32[]{:S(2)}, u32[]{:S(2)}) collective-permute-start(f32[64,128]{1,0:T(8,128)S(1)} %get-tuple-element.121), channel_id=1, source_target_pairs={{0,8},{1,9},{2,10},{3,11},{4,12},{5,13},{6,14},{7,15},{8,0},{9,1},... | collective-permute-start | bytes 98312 | tf_op jit(solution)/shard_map/ppermute | solution.py:591
  40.3 3.8 %collective-permute-start.15 = (f32[64,128]{1,0:T(8,128)S(1)}, f32[64,128]{1,0:T(8,128)S(1)}, u32[]{:S(2)}, u32[]{:S(2)}) collective-permute-start(f32[64,128]{1,0:T(8,128)S(1)} %get-tuple-element.122), channel_id=1, source_target_pairs={{0,1},{1,0},{2,3},{3,2},{4,5},{5,4},{6,7},{7,6},{8,16},{9,17},{10,... | collective-permute-start | bytes 98312 | tf_op jit(solution)/shard_map/ppermute | solution.py:591

commit v4 on v3

--- a/solution.py
+++ b/solution.py
@@ -56,6 +56,10 @@
     low = weights - high
     pad = jnp.zeros((weights.shape[0], 8), jnp.float32)
     return jnp.concatenate([high, high, low, pad], axis=1).astype(jnp.bfloat16)
+
+
+def pairs_start(basis, wide):
+    return -(-(3 * basis + FACES * wide) // 16) * 16
 
 
 def product(left, right):
@@ -298,7 +302,7 @@
                 total[outer] = term if total[outer] is None else total[outer] + term
         for outer in range(fields):
             local_flux[face, outer] = total[outer]
-    base += FACES * wide
+    base = pairs_start(basis, wide)
     highs, lows = [], []
     for pair in range(ORIENTS):
         rows = slice(base + pair * wide, base + (pair + 1) * wide)
@@ -332,6 +336,7 @@
     for face in range(FACES):
         plain[row : row + face_basis, :] = face_proj[:, face, :]
         row += wide
+    row = pairs_start(basis, wide)
     for pair in range(ORIENTS):
         plain[row : row + face_basis, :] = neigh_proj[pair]
         row += wide
@@ -432,8 +437,7 @@
         last.append(total)
     parts = [message[0:basis, :] for message in messages] + [jnp.concatenate(last, axis=0)]
     columns = jnp.concatenate([stacked(part) for part in parts], axis=1)
-    base = 3 * basis + FACES * wide
-    projected = product(matrices[base:, :], columns)
+    projected = product(matrices[pairs_start(basis, wide) :, :], columns)
     pair_row = halo_pairs[0:1, :]
     chosen = projected[0:wide, :]
     for pair in range(1, ORIENTS):
@@ -583,7 +587,7 @@
     state = f32(fields, basis, cells)
     message = f32(basis + 8, cells)
     depth = 3 * basis + 8
-    rows = 3 * basis + (FACES + ORIENTS) * wide
+    rows = pairs_start(basis, wide) + ORIENTS * wide
     derived = pltpu.VMEM((3 * basis, fields * cells), jnp.float32)
     faces = FACES * cells
 

time: 46 us -> 45.7 us (level)
  Pallas kernels: 28.3 us -> 27.8 us
    pallas_call x9, Pallas kernels: 28.3 us -> 27.8 us  [call(): pl.pallas_call(kernel, out_shape=outs, in_specs=[source] * len(operands),...]
where the time goes in v4:
time: 45.7 us; the launch traced here: 45.6 us
  Pallas kernels  27.8 us (61%)
  starting transfers between devices  13.7 us (30%)
  waiting for transfers between devices  3.96 us (9%)
    pallas_call x9, Pallas kernels, call(): pl.pallas_call(kernel, out_shape=outs, in_specs=[source] * len(operands),...  27.8 us
    ppermute x16, starting transfers between devices, exchange(): lax.ppermute(m, AXES, pairs)  13.7 us
    ppermute x16, waiting for transfers between devices, exchange(): lax.ppermute(m, AXES, pairs)  3.96 us
  transfers between devices with their start and end apart: 16, of which 4 were waited for; matrix products, arithmetic and copies ran while one was open for 0% of the time, Pallas kernels for 18%

profile of v4, /device:TPU:0, one launch (start us, length us, event | category | flops | bytes accessed | tf_op | source)
XLA Modules:
  0.0 45.6 jit_solution(6616288136389021895)
XLA Ops:
  0.0 4.9 %shard_map.118 = (f32[9,56,128]{2,1,0:T(8,128)S(1)}, f32[9,56,128]{2,1,0:T(8,128)S(1)}, f32[64,128]{1,0:T(8,128)S(1)}, f32[64,128]{1,0:T(8,128)S(1)}, f32[64,128...) custom-call(f32[3,56,56]{2,1,0:T(8,128)} %stiffness_far.1, ...), custom_call_target="tpu_custom_call" | custom-call | flops 134217728 | bytes 1048576 | tf_op jit(solution)/shard_map/pallas_call | solution.py:554
  4.9 0.5 %collective-permute-start = (f32[64,128]{1,0:T(8,128)S(1)}, f32[64,128]{1,0:T(8,128)S(1)}, u32[]{:S(2)}, u32[]{:S(2)}) collective-permute-start(f32[64,128]{1,0:T(8,128)S(1)} %get-tuple-element.71), channel_id=1, source_target_pairs={{0,1},{1,0},{2,3},{3,2},{4,5},{5,4},{6,7},{7,6},{8,9},{9,8},{10,11... | collective-permute-start | bytes 98312 | tf_op jit(solution)/shard_map/ppermute | solution.py:595
  5.4 2.6 %collective-permute-start.1 = (f32[64,128]{1,0:T(8,128)S(1)}, f32[64,128]{1,0:T(8,128)S(1)}, u32[]{:S(2)}, u32[]{:S(2)}) collective-permute-start(f32[64,128]{1,0:T(8,128)S(1)} %get-tuple-element.72), channel_id=1, source_target_pairs={{0,8},{1,2},{2,1},{3,4},{4,3},{5,6},{6,5},{7,15},{8,0},{9,10},{10,... | collective-permute-start | bytes 98312 | tf_op jit(solution)/shard_map/ppermute | solution.py:595
  8.1 0.1 collective-permute-start.2
  8.2 1.2 %collective-permute-start.3 = (f32[64,128]{1,0:T(8,128)S(1)}, f32[64,128]{1,0:T(8,128)S(1)}, u32[]{:S(2)}, u32[]{:S(2)}) collective-permute-start(f32[64,128]{1,0:T(8,128)S(1)} %get-tuple-element.74), channel_id=1, source_target_pairs={{0,1},{1,0},{2,3},{3,2},{4,5},{5,4},{6,7},{7,6},{8,16},{9,17},{10,... | collective-permute-start | bytes 98312 | tf_op jit(solution)/shard_map/ppermute | solution.py:595
  9.4 2.3 %shard_map.119 = (f32[9,56,128]{2,1,0:T(8,128)S(1)}, f32[4,9,24,128]{3,2,1,0:T(8,128)S(1)}, f32[216,512]{1,0:T(8,128)S(1)}, bf16[560,176]{1,0:T(8,128)(2,1)S(1)}...) custom-call(f32[9,56,128]{2,1,0:T(8,128)S(1)} %get-tuple-element.75., ...), custom_call_target="tpu_custom_call" | custom-call | flops 134217728 | bytes 1048576 | tf_op jit(solution)/shard_map/pallas_call | solution.py:554
  11.8 0.0 collective-permute-done.1.in_1
  11.8 0.2 collective-permute-done.2.in_2
  12.0 0.0 collective-permute-done.3.in_3
  12.0 4.1 %shard_map.120 = (f32[9,56,128]{2,1,0:T(8,128)S(1)}, f32[9,56,128]{2,1,0:T(8,128)S(1)}, f32[9,56,128]{2,1,0:T(8,128)S(1)}, f32[64,128]{1,0:T(8,128)S(1)}, f32[64...) custom-call(f32[9,56,128]{2,1,0:T(8,128)S(1)} %get-tuple-element.66.coefficients.applied_in.pending_in, ...), custom_call_target="tpu_custom_call" | custom-call | flops 134217728 | bytes 1048576 | tf_op jit(solution)/shard_map/pallas_call | solution.py:554
  16.1 0.1 collective-permute-start.4
  16.2 2.7 %collective-permute-start.5 = (f32[64,128]{1,0:T(8,128)S(1)}, f32[64,128]{1,0:T(8,128)S(1)}, u32[]{:S(2)}, u32[]{:S(2)}) collective-permute-start(f32[64,128]{1,0:T(8,128)S(1)} %get-tuple-element.98), channel_id=1, source_target_pairs={{0,8},{1,2},{2,1},{3,4},{4,3},{5,6},{6,5},{7,15},{8,0},{9,10},{10,... | collective-permute-start | bytes 98312 | tf_op jit(solution)/shard_map/ppermute | solution.py:595
  18.9 0.0 collective-permute-start.6
  18.9 1.3 %collective-permute-start.7 = (f32[64,128]{1,0:T(8,128)S(1)}, f32[64,128]{1,0:T(8,128)S(1)}, u32[]{:S(2)}, u32[]{:S(2)}) collective-permute-start(f32[64,128]{1,0:T(8,128)S(1)} %get-tuple-element.100), channel_id=1, source_target_pairs={{0,1},{1,0},{2,3},{3,2},{4,5},{5,4},{6,7},{7,6},{8,16},{9,17},{10,... | collective-permute-start | bytes 98312 | tf_op jit(solution)/shard_map/ppermute | solution.py:595
  20.2 1.9 %shard_map.121 = (f32[9,56,128]{2,1,0:T(8,128)S(1)}, f32[4,9,24,128]{3,2,1,0:T(8,128)S(1)}, f32[216,512]{1,0:T(8,128)S(1)}) custom-call(f32[9,56,128]{2,1,0:T(8,128)S(1)} %get-tuple-element.101.own, f32[9,9,3,128]{3,2,1,0:T(4,128)S(1)} %get-tuple-element.67.jac, f32[9,9,4,128]{3,2,1,0:T(4,128)S(1)} %get-tuple-element.76.flux_local, ...), custom_call_target="tpu_custom_call" | custom-call | flops 134217728 | bytes 1048576 | tf_op jit(solution)/shard_map/pallas_call | solution.py:554
  22.2 0.0 collective-permute-done.4.in_0
  22.2 0.6 %collective-permute-done.6.in_2 = f32[64,128]{1,0:T(8,128)S(1)} collective-permute-done((f32[64,128]{1,0:T(8,128)S(1)}, f32[64,128]{1,0:T(8,128)S(1)}, u32[]{:S(2)}, u32[]{:S(2)}) %collective-permute-start.6) | collective-permute-done | bytes 32800 | tf_op jit(solution)/shard_map/ppermute | solution.py:595
  22.8 4.7 %shard_map.122 = (f32[9,56,128]{2,1,0:T(8,128)S(1)}, f32[9,56,128]{2,1,0:T(8,128)S(1)}, f32[9,56,128]{2,1,0:T(8,128)S(1)}, f32[9,56,128]{2,1,0:T(8,128)S(1)}, f3...) custom-call(f32[9,56,128]{2,1,0:T(8,128)S(1)} %get-tuple-element.66.coefficients.app, ...), custom_call_target="tpu_custom_call" | custom-call | flops 134217728 | bytes 1048576 | tf_op jit(solution)/shard_map/pallas_call | solution.py:554
  27.5 0.1 collective-permute-start.8
  27.5 2.1 %collective-permute-start.9 = (f32[64,128]{1,0:T(8,128)S(1)}, f32[64,128]{1,0:T(8,128)S(1)}, u32[]{:S(2)}, u32[]{:S(2)}) collective-permute-start(f32[64,128]{1,0:T(8,128)S(1)} %get-tuple-element.109), channel_id=1, source_target_pairs={{0,8},{1,2},{2,1},{3,4},{4,3},{5,6},{6,5},{7,15},{8,0},{9,10},{10,... | collective-permute-start | bytes 98312 | tf_op jit(solution)/shard_map/ppermute | solution.py:595
  29.6 0.1 collective-permute-start.10
  29.7 0.6 %collective-permute-start.11 = (f32[64,128]{1,0:T(8,128)S(1)}, f32[64,128]{1,0:T(8,128)S(1)}, u32[]{:S(2)}, u32[]{:S(2)}) collective-permute-start(f32[64,128]{1,0:T(8,128)S(1)} %get-tuple-element.111), channel_id=1, source_target_pairs={{0,1},{1,0},{2,3},{3,2},{4,5},{5,4},{6,7},{7,6},{8,16},{9,17},{10,... | collective-permute-start | bytes 98312 | tf_op jit(solution)/shard_map/ppermute | solution.py:595
  30.3 1.9 %shard_map.123 = (f32[9,56,128]{2,1,0:T(8,128)S(1)}, f32[4,9,24,128]{3,2,1,0:T(8,128)S(1)}, f32[216,512]{1,0:T(8,128)S(1)}) custom-call(f32[9,56,128]{2,1,0:T(8,128)S(1)} %get-tuple-element.112.own, f32[9,9,3,128]{3,2,1,0:T(4,128)S(1)} %get-tuple-element.67.jac, f32[9,9,4,128]{3,2,1,0:T(4,128)S(1)} %get-tuple-element.76.flux_local, ...), custom_call_target="tpu_custom_call" | custom-call | flops 134217728 | bytes 1048576 | tf_op jit(solution)/shard_map/pallas_call | solution.py:554
  32.3 1.3 %collective-permute-done.10.in_2 = f32[64,128]{1,0:T(8,128)S(1)} collective-permute-done((f32[64,128]{1,0:T(8,128)S(1)}, f32[64,128]{1,0:T(8,128)S(1)}, u32[]{:S(2)}, u32[]{:S(2)}) %collective-permute-start.10) | collective-permute-done | bytes 32800 | tf_op jit(solution)/shard_map/ppermute | solution.py:595
  33.6 4.2 %shard_map.124 = (f32[9,56,128]{2,1,0:T(8,128)S(1)}, f32[9,56,128]{2,1,0:T(8,128)S(1)}, f32[9,56,128]{2,1,0:T(8,128)S(1)}, f32[64,128]{1,0:T(8,128)S(1)}, f32[64...) custom-call(f32[9,56,128]{2,1,0:T(8,128)S(1)} %get-tuple-element.66.coefficients.applied_in.pending_in, ...), custom_call_target="tpu_custom_call" | custom-call | flops 134217728 | bytes 1048576 | tf_op jit(solution)/shard_map/pallas_call | solution.py:554
  37.7 0.1 collective-permute-start.12
  37.8 2.1 %collective-permute-start.13 = (f32[64,128]{1,0:T(8,128)S(1)}, f32[64,128]{1,0:T(8,128)S(1)}, u32[]{:S(2)}, u32[]{:S(2)}) collective-permute-start(f32[64,128]{1,0:T(8,128)S(1)} %get-tuple-element.120), channel_id=1, source_target_pairs={{0,8},{1,2},{2,1},{3,4},{4,3},{5,6},{6,5},{7,15},{8,0},{9,10},{10,... | collective-permute-start | bytes 98312 | tf_op jit(solution)/shard_map/ppermute | solution.py:595
  39.9 0.1 collective-permute-start.14
  40.0 0.1 collective-permute-start.15
  40.1 1.9 %shard_map.125 = (f32[9,56,128]{2,1,0:T(8,128)S(1)}, f32[4,9,24,128]{3,2,1,0:T(8,128)S(1)}, f32[216,512]{1,0:T(8,128)S(1)}) custom-call(f32[9,56,128]{2,1,0:T(8,128)S(1)} %get-tuple-element.123.own, f32[9,9,3,128]{3,2,1,0:T(4,128)S(1)} %get-tuple-element.67.jac, f32[9,9,4,128]{3,2,1,0:T(4,128)S(1)} %get-tuple-element.76.flux_local, ...), custom_call_target="tpu_custom_call" | custom-call | flops 134217728 | bytes 1048576 | tf_op jit(solution)/shard_map/pallas_call | solution.py:554
  42.0 1.8 %collective-permute-done.14.in_2 = f32[64,128]{1,0:T(8,128)S(1)} collective-permute-done((f32[64,128]{1,0:T(8,128)S(1)}, f32[64,128]{1,0:T(8,128)S(1)}, u32[]{:S(2)}, u32[]{:S(2)}) %collective-permute-start.14) | collective-permute-done | bytes 32800 | tf_op jit(solution)/shard_map/ppermute | solution.py:595
  43.8 1.8 %shard_map.126 = f32[9,56,128]{2,1,0:T(8,128)} custom-call(f32[9,56,128]{2,1,0:T(8,128)S(1)} %get-tuple-element.117.applied_in, f32[9,56,128]{2,1,0:T(8,128)S(1)} %get-tuple-element.118.pending_in, f32[64,128]{1,0:T(8,128)S(1)} %collective-permute-done.12.in_0, f32[64,128]{1,0:T(8,128)S(1)} %collective-permute-done.13.in_1, ...), custom_call_target="tpu_custom_call" | custom-call | flops 134217728 | bytes 1048576 | tf_op jit(solution)/shard_map/pallas_call | solution.py:554
  (9 shorter events, 0.0 us)
Async XLA Ops:
  4.9 6.8 %collective-permute-start = (f32[64,128]{1,0:T(8,128)S(1)}, f32[64,128]{1,0:T(8,128)S(1)}, u32[]{:S(2)}, u32[]{:S(2)}) collective-permute-start(f32[64,128]{1,0:T(8,128)S(1)} %get-tuple-element.71), channel_id=1, source_target_pairs={{0,1},{1,0},{2,3},{3,2},{4,5},{5,4},{6,7},{7,6},{8,9},{9,8},{10,11... | collective-permute-start | bytes 98312 | tf_op jit(solution)/shard_map/ppermute | solution.py:595
  5.4 6.3 %collective-permute-start.1 = (f32[64,128]{1,0:T(8,128)S(1)}, f32[64,128]{1,0:T(8,128)S(1)}, u32[]{:S(2)}, u32[]{:S(2)}) collective-permute-start(f32[64,128]{1,0:T(8,128)S(1)} %get-tuple-element.72), channel_id=1, source_target_pairs={{0,8},{1,2},{2,1},{3,4},{4,3},{5,6},{6,5},{7,15},{8,0},{9,10},{10,... | collective-permute-start | bytes 98312 | tf_op jit(solution)/shard_map/ppermute | solution.py:595
  8.1 3.9 %collective-permute-start.2 = (f32[64,128]{1,0:T(8,128)S(1)}, f32[64,128]{1,0:T(8,128)S(1)}, u32[]{:S(2)}, u32[]{:S(2)}) collective-permute-start(f32[64,128]{1,0:T(8,128)S(1)} %get-tuple-element.73), channel_id=1, source_target_pairs={{0,8},{1,9},{2,10},{3,11},{4,12},{5,13},{6,14},{7,15},{8,0},{9,1},... | collective-permute-start | bytes 98312 | tf_op jit(solution)/shard_map/ppermute | solution.py:595
  8.2 3.8 %collective-permute-start.3 = (f32[64,128]{1,0:T(8,128)S(1)}, f32[64,128]{1,0:T(8,128)S(1)}, u32[]{:S(2)}, u32[]{:S(2)}) collective-permute-start(f32[64,128]{1,0:T(8,128)S(1)} %get-tuple-element.74), channel_id=1, source_target_pairs={{0,1},{1,0},{2,3},{3,2},{4,5},{5,4},{6,7},{7,6},{8,16},{9,17},{10,... | collective-permute-start | bytes 98312 | tf_op jit(solution)/shard_map/ppermute | solution.py:595
  16.1 6.0 %collective-permute-start.4 = (f32[64,128]{1,0:T(8,128)S(1)}, f32[64,128]{1,0:T(8,128)S(1)}, u32[]{:S(2)}, u32[]{:S(2)}) collective-permute-start(f32[64,128]{1,0:T(8,128)S(1)} %get-tuple-element.97), channel_id=1, source_target_pairs={{0,1},{1,0},{2,3},{3,2},{4,5},{5,4},{6,7},{7,6},{8,9},{9,8},{10,11... | collective-permute-start | bytes 98312 | tf_op jit(solution)/shard_map/ppermute | solution.py:595
  16.2 6.0 %collective-permute-start.5 = (f32[64,128]{1,0:T(8,128)S(1)}, f32[64,128]{1,0:T(8,128)S(1)}, u32[]{:S(2)}, u32[]{:S(2)}) collective-permute-start(f32[64,128]{1,0:T(8,128)S(1)} %get-tuple-element.98), channel_id=1, source_target_pairs={{0,8},{1,2},{2,1},{3,4},{4,3},{5,6},{6,5},{7,15},{8,0},{9,10},{10,... | collective-permute-start | bytes 98312 | tf_op jit(solution)/shard_map/ppermute | solution.py:595
  18.9 3.9 %collective-permute-start.6 = (f32[64,128]{1,0:T(8,128)S(1)}, f32[64,128]{1,0:T(8,128)S(1)}, u32[]{:S(2)}, u32[]{:S(2)}) collective-permute-start(f32[64,128]{1,0:T(8,128)S(1)} %get-tuple-element.99), channel_id=1, source_target_pairs={{0,8},{1,9},{2,10},{3,11},{4,12},{5,13},{6,14},{7,15},{8,0},{9,1},... | collective-permute-start | bytes 98312 | tf_op jit(solution)/shard_map/ppermute | solution.py:595
  18.9 3.9 %collective-permute-start.7 = (f32[64,128]{1,0:T(8,128)S(1)}, f32[64,128]{1,0:T(8,128)S(1)}, u32[]{:S(2)}, u32[]{:S(2)}) collective-permute-start(f32[64,128]{1,0:T(8,128)S(1)} %get-tuple-element.100), channel_id=1, source_target_pairs={{0,1},{1,0},{2,3},{3,2},{4,5},{5,4},{6,7},{7,6},{8,16},{9,17},{10,... | collective-permute-start | bytes 98312 | tf_op jit(solution)/shard_map/ppermute | solution.py:595
  27.5 4.8 %collective-permute-start.8 = (f32[64,128]{1,0:T(8,128)S(1)}, f32[64,128]{1,0:T(8,128)S(1)}, u32[]{:S(2)}, u32[]{:S(2)}) collective-permute-start(f32[64,128]{1,0:T(8,128)S(1)} %get-tuple-element.108), channel_id=1, source_target_pairs={{0,1},{1,0},{2,3},{3,2},{4,5},{5,4},{6,7},{7,6},{8,9},{9,8},{10,11... | collective-permute-start | bytes 98312 | tf_op jit(solution)/shard_map/ppermute | solution.py:595
  27.5 4.7 %collective-permute-start.9 = (f32[64,128]{1,0:T(8,128)S(1)}, f32[64,128]{1,0:T(8,128)S(1)}, u32[]{:S(2)}, u32[]{:S(2)}) collective-permute-start(f32[64,128]{1,0:T(8,128)S(1)} %get-tuple-element.109), channel_id=1, source_target_pairs={{0,8},{1,2},{2,1},{3,4},{4,3},{5,6},{6,5},{7,15},{8,0},{9,10},{10,... | collective-permute-start | bytes 98312 | tf_op jit(solution)/shard_map/ppermute | solution.py:595
  29.6 3.9 %collective-permute-start.10 = (f32[64,128]{1,0:T(8,128)S(1)}, f32[64,128]{1,0:T(8,128)S(1)}, u32[]{:S(2)}, u32[]{:S(2)}) collective-permute-start(f32[64,128]{1,0:T(8,128)S(1)} %get-tuple-element.110), channel_id=1, source_target_pairs={{0,8},{1,9},{2,10},{3,11},{4,12},{5,13},{6,14},{7,15},{8,0},{9,1},... | collective-permute-start | bytes 98312 | tf_op jit(solution)/shard_map/ppermute | solution.py:595
  29.7 3.8 %collective-permute-start.11 = (f32[64,128]{1,0:T(8,128)S(1)}, f32[64,128]{1,0:T(8,128)S(1)}, u32[]{:S(2)}, u32[]{:S(2)}) collective-permute-start(f32[64,128]{1,0:T(8,128)S(1)} %get-tuple-element.111), channel_id=1, source_target_pairs={{0,1},{1,0},{2,3},{3,2},{4,5},{5,4},{6,7},{7,6},{8,16},{9,17},{10,... | collective-permute-start | bytes 98312 | tf_op jit(solution)/shard_map/ppermute | solution.py:595
  37.7 4.3 %collective-permute-start.12 = (f32[64,128]{1,0:T(8,128)S(1)}, f32[64,128]{1,0:T(8,128)S(1)}, u32[]{:S(2)}, u32[]{:S(2)}) collective-permute-start(f32[64,128]{1,0:T(8,128)S(1)} %get-tuple-element.119), channel_id=1, source_target_pairs={{0,1},{1,0},{2,3},{3,2},{4,5},{5,4},{6,7},{7,6},{8,9},{9,8},{10,11... | collective-permute-start | bytes 98312 | tf_op jit(solution)/shard_map/ppermute | solution.py:595
  37.8 4.2 %collective-permute-start.13 = (f32[64,128]{1,0:T(8,128)S(1)}, f32[64,128]{1,0:T(8,128)S(1)}, u32[]{:S(2)}, u32[]{:S(2)}) collective-permute-start(f32[64,128]{1,0:T(8,128)S(1)} %get-tuple-element.120), channel_id=1, source_target_pairs={{0,8},{1,2},{2,1},{3,4},{4,3},{5,6},{6,5},{7,15},{8,0},{9,10},{10,... | collective-permute-start | bytes 98312 | tf_op jit(solution)/shard_map/ppermute | solution.py:595
  39.9 3.9 %collective-permute-start.14 = (f32[64,128]{1,0:T(8,128)S(1)}, f32[64,128]{1,0:T(8,128)S(1)}, u32[]{:S(2)}, u32[]{:S(2)}) collective-permute-start(f32[64,128]{1,0:T(8,128)S(1)} %get-tuple-element.121), channel_id=1, source_target_pairs={{0,8},{1,9},{2,10},{3,11},{4,12},{5,13},{6,14},{7,15},{8,0},{9,1},... | collective-permute-start | bytes 98312 | tf_op jit(solution)/shard_map/ppermute | solution.py:595
  40.0 3.8 %collective-permute-start.15 = (f32[64,128]{1,0:T(8,128)S(1)}, f32[64,128]{1,0:T(8,128)S(1)}, u32[]{:S(2)}, u32[]{:S(2)}) collective-permute-start(f32[64,128]{1,0:T(8,128)S(1)} %get-tuple-element.122), channel_id=1, source_target_pairs={{0,1},{1,0},{2,3},{3,2},{4,5},{5,4},{6,7},{7,6},{8,16},{9,17},{10,... | collective-permute-start | bytes 98312 | tf_op jit(solution)/shard_map/ppermute | solution.py:595

commit v5 on v4

--- a/solution.py
+++ b/solution.py
@@ -501,10 +501,13 @@
     fields, _, cells = volume.shape
     if substep % 2 == 0:
         fits = jnp.sum(jnp.where(clusters[...] == 0, 1.0, 0.0)) <= cells // 2
+    else:
+        weights = taylor_weights(clusters[...], substep + 1)
+        next_weights = later_weights_of(clusters[...], substep + 1)
+    _, done = time_phase(clusters[...], substep)
+    finished = done > 0.5
     remote = remote_part((in_0, in_1, in_2, in_3), matrices, halo_hot, halo_pairs, traces)
     updates = change(remote, volume, local_flux, flux_neigh, lift)
-    _, done = time_phase(clusters[...], substep)
-    finished = done > 0.5
     for field in range(fields):
         waiting = updates[field]
         if substep > 0:
@@ -512,8 +515,6 @@
         passed = jnp.where(finished, waiting, 0.0)
         applied[field] = passed + applied_in[field] if substep > 0 else passed
         pending[field] = jnp.where(finished, 0.0, waiting)
-    weights = taylor_weights(clusters[...], substep + 1)
-
     def current(field):
         return coefficients[field] + applied[field]
 
@@ -525,11 +526,12 @@
 
         @pl.when(jnp.logical_not(fits))
         def _():
+            weights = taylor_weights(clusters[...], substep + 1)
             series(current, rows_of(jac), stiff, weights, own, first, second)
     else:
         series(
             current, rows_of(jac), stiff, weights, own, first, second,
-            later, later_weights_of(clusters[...], substep + 1),
+            later, next_weights,
         )
     pack(own, picks, messages)
 

time: 45.7 us -> 45.7 us (level)
  no operation moved by 1% of the time
where the time goes in v5:
time: 45.7 us; the launch traced here: 45.6 us
  Pallas kernels  27.8 us (61%)
  starting transfers between devices  13.7 us (30%)
  waiting for transfers between devices  3.97 us (9%)
    pallas_call x9, Pallas kernels, call(): pl.pallas_call(kernel, out_shape=outs, in_specs=[source] * len(operands),...  27.8 us
    ppermute x16, starting transfers between devices, exchange(): lax.ppermute(m, AXES, pairs)  13.7 us
    ppermute x16, waiting for transfers between devices, exchange(): lax.ppermute(m, AXES, pairs)  3.97 us
  transfers between devices with their start and end apart: 16, of which 4 were waited for; matrix products, arithmetic and copies ran while one was open for 0% of the time, Pallas kernels for 18%

profile of v5, /device:TPU:0, one launch (start us, length us, event | category | flops | bytes accessed | tf_op | source)
XLA Modules:
  0.0 45.6 jit_solution(4700437330786567521)
XLA Ops:
  0.0 4.9 %shard_map.118 = (f32[9,56,128]{2,1,0:T(8,128)S(1)}, f32[9,56,128]{2,1,0:T(8,128)S(1)}, f32[64,128]{1,0:T(8,128)S(1)}, f32[64,128]{1,0:T(8,128)S(1)}, f32[64,128...) custom-call(f32[3,56,56]{2,1,0:T(8,128)} %stiffness_far.1, ...), custom_call_target="tpu_custom_call" | custom-call | flops 134217728 | bytes 1048576 | tf_op jit(solution)/shard_map/pallas_call | solution.py:556
  4.9 0.5 %collective-permute-start = (f32[64,128]{1,0:T(8,128)S(1)}, f32[64,128]{1,0:T(8,128)S(1)}, u32[]{:S(2)}, u32[]{:S(2)}) collective-permute-start(f32[64,128]{1,0:T(8,128)S(1)} %get-tuple-element.71), channel_id=1, source_target_pairs={{0,1},{1,0},{2,3},{3,2},{4,5},{5,4},{6,7},{7,6},{8,9},{9,8},{10,11... | collective-permute-start | bytes 98312 | tf_op jit(solution)/shard_map/ppermute | solution.py:597
  5.4 2.6 %collective-permute-start.1 = (f32[64,128]{1,0:T(8,128)S(1)}, f32[64,128]{1,0:T(8,128)S(1)}, u32[]{:S(2)}, u32[]{:S(2)}) collective-permute-start(f32[64,128]{1,0:T(8,128)S(1)} %get-tuple-element.72), channel_id=1, source_target_pairs={{0,8},{1,2},{2,1},{3,4},{4,3},{5,6},{6,5},{7,15},{8,0},{9,10},{10,... | collective-permute-start | bytes 98312 | tf_op jit(solution)/shard_map/ppermute | solution.py:597
  8.1 0.1 collective-permute-start.2
  8.2 1.2 %collective-permute-start.3 = (f32[64,128]{1,0:T(8,128)S(1)}, f32[64,128]{1,0:T(8,128)S(1)}, u32[]{:S(2)}, u32[]{:S(2)}) collective-permute-start(f32[64,128]{1,0:T(8,128)S(1)} %get-tuple-element.74), channel_id=1, source_target_pairs={{0,1},{1,0},{2,3},{3,2},{4,5},{5,4},{6,7},{7,6},{8,16},{9,17},{10,... | collective-permute-start | bytes 98312 | tf_op jit(solution)/shard_map/ppermute | solution.py:597
  9.4 2.3 %shard_map.119 = (f32[9,56,128]{2,1,0:T(8,128)S(1)}, f32[4,9,24,128]{3,2,1,0:T(8,128)S(1)}, f32[216,512]{1,0:T(8,128)S(1)}, bf16[560,176]{1,0:T(8,128)(2,1)S(1)}...) custom-call(f32[9,56,128]{2,1,0:T(8,128)S(1)} %get-tuple-element.75., ...), custom_call_target="tpu_custom_call" | custom-call | flops 134217728 | bytes 1048576 | tf_op jit(solution)/shard_map/pallas_call | solution.py:556
  11.8 0.0 collective-permute-done.1.in_1
  11.8 0.2 collective-permute-done.2.in_2
  12.0 0.0 collective-permute-done.3.in_3
  12.0 4.1 %shard_map.120 = (f32[9,56,128]{2,1,0:T(8,128)S(1)}, f32[9,56,128]{2,1,0:T(8,128)S(1)}, f32[9,56,128]{2,1,0:T(8,128)S(1)}, f32[64,128]{1,0:T(8,128)S(1)}, f32[64...) custom-call(f32[9,56,128]{2,1,0:T(8,128)S(1)} %get-tuple-element.66.coefficients.applied_in.pending_in, ...), custom_call_target="tpu_custom_call" | custom-call | flops 134217728 | bytes 1048576 | tf_op jit(solution)/shard_map/pallas_call | solution.py:556
  16.1 0.1 collective-permute-start.4
  16.2 2.7 %collective-permute-start.5 = (f32[64,128]{1,0:T(8,128)S(1)}, f32[64,128]{1,0:T(8,128)S(1)}, u32[]{:S(2)}, u32[]{:S(2)}) collective-permute-start(f32[64,128]{1,0:T(8,128)S(1)} %get-tuple-element.98), channel_id=1, source_target_pairs={{0,8},{1,2},{2,1},{3,4},{4,3},{5,6},{6,5},{7,15},{8,0},{9,10},{10,... | collective-permute-start | bytes 98312 | tf_op jit(solution)/shard_map/ppermute | solution.py:597
  18.9 0.0 collective-permute-start.6
  18.9 1.3 %collective-permute-start.7 = (f32[64,128]{1,0:T(8,128)S(1)}, f32[64,128]{1,0:T(8,128)S(1)}, u32[]{:S(2)}, u32[]{:S(2)}) collective-permute-start(f32[64,128]{1,0:T(8,128)S(1)} %get-tuple-element.100), channel_id=1, source_target_pairs={{0,1},{1,0},{2,3},{3,2},{4,5},{5,4},{6,7},{7,6},{8,16},{9,17},{10,... | collective-permute-start | bytes 98312 | tf_op jit(solution)/shard_map/ppermute | solution.py:597
  20.2 1.9 %shard_map.121 = (f32[9,56,128]{2,1,0:T(8,128)S(1)}, f32[4,9,24,128]{3,2,1,0:T(8,128)S(1)}, f32[216,512]{1,0:T(8,128)S(1)}) custom-call(f32[9,56,128]{2,1,0:T(8,128)S(1)} %get-tuple-element.101.own, f32[9,9,3,128]{3,2,1,0:T(4,128)S(1)} %get-tuple-element.67.jac, f32[9,9,4,128]{3,2,1,0:T(4,128)S(1)} %get-tuple-element.76.flux_local, ...), custom_call_target="tpu_custom_call" | custom-call | flops 134217728 | bytes 1048576 | tf_op jit(solution)/shard_map/pallas_call | solution.py:556
  22.2 0.0 collective-permute-done.4.in_0
  22.2 0.6 %collective-permute-done.6.in_2 = f32[64,128]{1,0:T(8,128)S(1)} collective-permute-done((f32[64,128]{1,0:T(8,128)S(1)}, f32[64,128]{1,0:T(8,128)S(1)}, u32[]{:S(2)}, u32[]{:S(2)}) %collective-permute-start.6) | collective-permute-done | bytes 32800 | tf_op jit(solution)/shard_map/ppermute | solution.py:597
  22.8 4.7 %shard_map.122 = (f32[9,56,128]{2,1,0:T(8,128)S(1)}, f32[9,56,128]{2,1,0:T(8,128)S(1)}, f32[9,56,128]{2,1,0:T(8,128)S(1)}, f32[9,56,128]{2,1,0:T(8,128)S(1)}, f3...) custom-call(f32[9,56,128]{2,1,0:T(8,128)S(1)} %get-tuple-element.66.coefficients.app, ...), custom_call_target="tpu_custom_call" | custom-call | flops 134217728 | bytes 1048576 | tf_op jit(solution)/shard_map/pallas_call | solution.py:556
  27.5 0.1 collective-permute-start.8
  27.5 2.1 %collective-permute-start.9 = (f32[64,128]{1,0:T(8,128)S(1)}, f32[64,128]{1,0:T(8,128)S(1)}, u32[]{:S(2)}, u32[]{:S(2)}) collective-permute-start(f32[64,128]{1,0:T(8,128)S(1)} %get-tuple-element.109), channel_id=1, source_target_pairs={{0,8},{1,2},{2,1},{3,4},{4,3},{5,6},{6,5},{7,15},{8,0},{9,10},{10,... | collective-permute-start | bytes 98312 | tf_op jit(solution)/shard_map/ppermute | solution.py:597
  29.6 0.1 collective-permute-start.10
  29.7 0.6 %collective-permute-start.11 = (f32[64,128]{1,0:T(8,128)S(1)}, f32[64,128]{1,0:T(8,128)S(1)}, u32[]{:S(2)}, u32[]{:S(2)}) collective-permute-start(f32[64,128]{1,0:T(8,128)S(1)} %get-tuple-element.111), channel_id=1, source_target_pairs={{0,1},{1,0},{2,3},{3,2},{4,5},{5,4},{6,7},{7,6},{8,16},{9,17},{10,... | collective-permute-start | bytes 98312 | tf_op jit(solution)/shard_map/ppermute | solution.py:597
  30.3 1.9 %shard_map.123 = (f32[9,56,128]{2,1,0:T(8,128)S(1)}, f32[4,9,24,128]{3,2,1,0:T(8,128)S(1)}, f32[216,512]{1,0:T(8,128)S(1)}) custom-call(f32[9,56,128]{2,1,0:T(8,128)S(1)} %get-tuple-element.112.own, f32[9,9,3,128]{3,2,1,0:T(4,128)S(1)} %get-tuple-element.67.jac, f32[9,9,4,128]{3,2,1,0:T(4,128)S(1)} %get-tuple-element.76.flux_local, ...), custom_call_target="tpu_custom_call" | custom-call | flops 134217728 | bytes 1048576 | tf_op jit(solution)/shard_map/pallas_call | solution.py:556
  32.2 1.3 %collective-permute-done.10.in_2 = f32[64,128]{1,0:T(8,128)S(1)} collective-permute-done((f32[64,128]{1,0:T(8,128)S(1)}, f32[64,128]{1,0:T(8,128)S(1)}, u32[]{:S(2)}, u32[]{:S(2)}) %collective-permute-start.10) | collective-permute-done | bytes 32800 | tf_op jit(solution)/shard_map/ppermute | solution.py:597
  33.6 4.2 %shard_map.124 = (f32[9,56,128]{2,1,0:T(8,128)S(1)}, f32[9,56,128]{2,1,0:T(8,128)S(1)}, f32[9,56,128]{2,1,0:T(8,128)S(1)}, f32[64,128]{1,0:T(8,128)S(1)}, f32[64...) custom-call(f32[9,56,128]{2,1,0:T(8,128)S(1)} %get-tuple-element.66.coefficients.applied_in.pending_in, ...), custom_call_target="tpu_custom_call" | custom-call | flops 134217728 | bytes 1048576 | tf_op jit(solution)/shard_map/pallas_call | solution.py:556
  37.7 0.1 collective-permute-start.12
  37.8 2.1 %collective-permute-start.13 = (f32[64,128]{1,0:T(8,128)S(1)}, f32[64,128]{1,0:T(8,128)S(1)}, u32[]{:S(2)}, u32[]{:S(2)}) collective-permute-start(f32[64,128]{1,0:T(8,128)S(1)} %get-tuple-element.120), channel_id=1, source_target_pairs={{0,8},{1,2},{2,1},{3,4},{4,3},{5,6},{6,5},{7,15},{8,0},{9,10},{10,... | collective-permute-start | bytes 98312 | tf_op jit(solution)/shard_map/ppermute | solution.py:597
  39.9 0.1 collective-permute-start.14
  40.0 0.1 collective-permute-start.15
  40.0 1.9 %shard_map.125 = (f32[9,56,128]{2,1,0:T(8,128)S(1)}, f32[4,9,24,128]{3,2,1,0:T(8,128)S(1)}, f32[216,512]{1,0:T(8,128)S(1)}) custom-call(f32[9,56,128]{2,1,0:T(8,128)S(1)} %get-tuple-element.123.own, f32[9,9,3,128]{3,2,1,0:T(4,128)S(1)} %get-tuple-element.67.jac, f32[9,9,4,128]{3,2,1,0:T(4,128)S(1)} %get-tuple-element.76.flux_local, ...), custom_call_target="tpu_custom_call" | custom-call | flops 134217728 | bytes 1048576 | tf_op jit(solution)/shard_map/pallas_call | solution.py:556
  42.0 1.8 %collective-permute-done.14.in_2 = f32[64,128]{1,0:T(8,128)S(1)} collective-permute-done((f32[64,128]{1,0:T(8,128)S(1)}, f32[64,128]{1,0:T(8,128)S(1)}, u32[]{:S(2)}, u32[]{:S(2)}) %collective-permute-start.14) | collective-permute-done | bytes 32800 | tf_op jit(solution)/shard_map/ppermute | solution.py:597
  43.8 1.8 %shard_map.126 = f32[9,56,128]{2,1,0:T(8,128)} custom-call(f32[9,56,128]{2,1,0:T(8,128)S(1)} %get-tuple-element.117.applied_in, f32[9,56,128]{2,1,0:T(8,128)S(1)} %get-tuple-element.118.pending_in, f32[64,128]{1,0:T(8,128)S(1)} %collective-permute-done.12.in_0, f32[64,128]{1,0:T(8,128)S(1)} %collective-permute-done.13.in_1, ...), custom_call_target="tpu_custom_call" | custom-call | flops 134217728 | bytes 1048576 | tf_op jit(solution)/shard_map/pallas_call | solution.py:556
  (9 shorter events, 0.0 us)
Async XLA Ops:
  4.9 6.8 %collective-permute-start = (f32[64,128]{1,0:T(8,128)S(1)}, f32[64,128]{1,0:T(8,128)S(1)}, u32[]{:S(2)}, u32[]{:S(2)}) collective-permute-start(f32[64,128]{1,0:T(8,128)S(1)} %get-tuple-element.71), channel_id=1, source_target_pairs={{0,1},{1,0},{2,3},{3,2},{4,5},{5,4},{6,7},{7,6},{8,9},{9,8},{10,11... | collective-permute-start | bytes 98312 | tf_op jit(solution)/shard_map/ppermute | solution.py:597
  5.4 6.3 %collective-permute-start.1 = (f32[64,128]{1,0:T(8,128)S(1)}, f32[64,128]{1,0:T(8,128)S(1)}, u32[]{:S(2)}, u32[]{:S(2)}) collective-permute-start(f32[64,128]{1,0:T(8,128)S(1)} %get-tuple-element.72), channel_id=1, source_target_pairs={{0,8},{1,2},{2,1},{3,4},{4,3},{5,6},{6,5},{7,15},{8,0},{9,10},{10,... | collective-permute-start | bytes 98312 | tf_op jit(solution)/shard_map/ppermute | solution.py:597
  8.1 3.9 %collective-permute-start.2 = (f32[64,128]{1,0:T(8,128)S(1)}, f32[64,128]{1,0:T(8,128)S(1)}, u32[]{:S(2)}, u32[]{:S(2)}) collective-permute-start(f32[64,128]{1,0:T(8,128)S(1)} %get-tuple-element.73), channel_id=1, source_target_pairs={{0,8},{1,9},{2,10},{3,11},{4,12},{5,13},{6,14},{7,15},{8,0},{9,1},... | collective-permute-start | bytes 98312 | tf_op jit(solution)/shard_map/ppermute | solution.py:597
  8.2 3.8 %collective-permute-start.3 = (f32[64,128]{1,0:T(8,128)S(1)}, f32[64,128]{1,0:T(8,128)S(1)}, u32[]{:S(2)}, u32[]{:S(2)}) collective-permute-start(f32[64,128]{1,0:T(8,128)S(1)} %get-tuple-element.74), channel_id=1, source_target_pairs={{0,1},{1,0},{2,3},{3,2},{4,5},{5,4},{6,7},{7,6},{8,16},{9,17},{10,... | collective-permute-start | bytes 98312 | tf_op jit(solution)/shard_map/ppermute | solution.py:597
  16.1 6.0 %collective-permute-start.4 = (f32[64,128]{1,0:T(8,128)S(1)}, f32[64,128]{1,0:T(8,128)S(1)}, u32[]{:S(2)}, u32[]{:S(2)}) collective-permute-start(f32[64,128]{1,0:T(8,128)S(1)} %get-tuple-element.97), channel_id=1, source_target_pairs={{0,1},{1,0},{2,3},{3,2},{4,5},{5,4},{6,7},{7,6},{8,9},{9,8},{10,11... | collective-permute-start | bytes 98312 | tf_op jit(solution)/shard_map/ppermute | solution.py:597
  16.2 6.0 %collective-permute-start.5 = (f32[64,128]{1,0:T(8,128)S(1)}, f32[64,128]{1,0:T(8,128)S(1)}, u32[]{:S(2)}, u32[]{:S(2)}) collective-permute-start(f32[64,128]{1,0:T(8,128)S(1)} %get-tuple-element.98), channel_id=1, source_target_pairs={{0,8},{1,2},{2,1},{3,4},{4,3},{5,6},{6,5},{7,15},{8,0},{9,10},{10,... | collective-permute-start | bytes 98312 | tf_op jit(solution)/shard_map/ppermute | solution.py:597
  18.9 3.9 %collective-permute-start.6 = (f32[64,128]{1,0:T(8,128)S(1)}, f32[64,128]{1,0:T(8,128)S(1)}, u32[]{:S(2)}, u32[]{:S(2)}) collective-permute-start(f32[64,128]{1,0:T(8,128)S(1)} %get-tuple-element.99), channel_id=1, source_target_pairs={{0,8},{1,9},{2,10},{3,11},{4,12},{5,13},{6,14},{7,15},{8,0},{9,1},... | collective-permute-start | bytes 98312 | tf_op jit(solution)/shard_map/ppermute | solution.py:597
  18.9 3.9 %collective-permute-start.7 = (f32[64,128]{1,0:T(8,128)S(1)}, f32[64,128]{1,0:T(8,128)S(1)}, u32[]{:S(2)}, u32[]{:S(2)}) collective-permute-start(f32[64,128]{1,0:T(8,128)S(1)} %get-tuple-element.100), channel_id=1, source_target_pairs={{0,1},{1,0},{2,3},{3,2},{4,5},{5,4},{6,7},{7,6},{8,16},{9,17},{10,... | collective-permute-start | bytes 98312 | tf_op jit(solution)/shard_map/ppermute | solution.py:597
  27.5 4.8 %collective-permute-start.8 = (f32[64,128]{1,0:T(8,128)S(1)}, f32[64,128]{1,0:T(8,128)S(1)}, u32[]{:S(2)}, u32[]{:S(2)}) collective-permute-start(f32[64,128]{1,0:T(8,128)S(1)} %get-tuple-element.108), channel_id=1, source_target_pairs={{0,1},{1,0},{2,3},{3,2},{4,5},{5,4},{6,7},{7,6},{8,9},{9,8},{10,11... | collective-permute-start | bytes 98312 | tf_op jit(solution)/shard_map/ppermute | solution.py:597
  27.5 4.7 %collective-permute-start.9 = (f32[64,128]{1,0:T(8,128)S(1)}, f32[64,128]{1,0:T(8,128)S(1)}, u32[]{:S(2)}, u32[]{:S(2)}) collective-permute-start(f32[64,128]{1,0:T(8,128)S(1)} %get-tuple-element.109), channel_id=1, source_target_pairs={{0,8},{1,2},{2,1},{3,4},{4,3},{5,6},{6,5},{7,15},{8,0},{9,10},{10,... | collective-permute-start | bytes 98312 | tf_op jit(solution)/shard_map/ppermute | solution.py:597
  29.6 3.9 %collective-permute-start.10 = (f32[64,128]{1,0:T(8,128)S(1)}, f32[64,128]{1,0:T(8,128)S(1)}, u32[]{:S(2)}, u32[]{:S(2)}) collective-permute-start(f32[64,128]{1,0:T(8,128)S(1)} %get-tuple-element.110), channel_id=1, source_target_pairs={{0,8},{1,9},{2,10},{3,11},{4,12},{5,13},{6,14},{7,15},{8,0},{9,1},... | collective-permute-start | bytes 98312 | tf_op jit(solution)/shard_map/ppermute | solution.py:597
  29.7 3.8 %collective-permute-start.11 = (f32[64,128]{1,0:T(8,128)S(1)}, f32[64,128]{1,0:T(8,128)S(1)}, u32[]{:S(2)}, u32[]{:S(2)}) collective-permute-start(f32[64,128]{1,0:T(8,128)S(1)} %get-tuple-element.111), channel_id=1, source_target_pairs={{0,1},{1,0},{2,3},{3,2},{4,5},{5,4},{6,7},{7,6},{8,16},{9,17},{10,... | collective-permute-start | bytes 98312 | tf_op jit(solution)/shard_map/ppermute | solution.py:597
  37.7 4.3 %collective-permute-start.12 = (f32[64,128]{1,0:T(8,128)S(1)}, f32[64,128]{1,0:T(8,128)S(1)}, u32[]{:S(2)}, u32[]{:S(2)}) collective-permute-start(f32[64,128]{1,0:T(8,128)S(1)} %get-tuple-element.119), channel_id=1, source_target_pairs={{0,1},{1,0},{2,3},{3,2},{4,5},{5,4},{6,7},{7,6},{8,9},{9,8},{10,11... | collective-permute-start | bytes 98312 | tf_op jit(solution)/shard_map/ppermute | solution.py:597
  37.8 4.2 %collective-permute-start.13 = (f32[64,128]{1,0:T(8,128)S(1)}, f32[64,128]{1,0:T(8,128)S(1)}, u32[]{:S(2)}, u32[]{:S(2)}) collective-permute-start(f32[64,128]{1,0:T(8,128)S(1)} %get-tuple-element.120), channel_id=1, source_target_pairs={{0,8},{1,2},{2,1},{3,4},{4,3},{5,6},{6,5},{7,15},{8,0},{9,10},{10,... | collective-permute-start | bytes 98312 | tf_op jit(solution)/shard_map/ppermute | solution.py:597
  39.9 3.9 %collective-permute-start.14 = (f32[64,128]{1,0:T(8,128)S(1)}, f32[64,128]{1,0:T(8,128)S(1)}, u32[]{:S(2)}, u32[]{:S(2)}) collective-permute-start(f32[64,128]{1,0:T(8,128)S(1)} %get-tuple-element.121), channel_id=1, source_target_pairs={{0,8},{1,9},{2,10},{3,11},{4,12},{5,13},{6,14},{7,15},{8,0},{9,1},... | collective-permute-start | bytes 98312 | tf_op jit(solution)/shard_map/ppermute | solution.py:597
  40.0 3.8 %collective-permute-start.15 = (f32[64,128]{1,0:T(8,128)S(1)}, f32[64,128]{1,0:T(8,128)S(1)}, u32[]{:S(2)}, u32[]{:S(2)}) collective-permute-start(f32[64,128]{1,0:T(8,128)S(1)} %get-tuple-element.122), channel_id=1, source_target_pairs={{0,1},{1,0},{2,3},{3,2},{4,5},{5,4},{6,7},{7,6},{8,16},{9,17},{10,... | collective-permute-start | bytes 98312 | tf_op jit(solution)/shard_map/ppermute | solution.py:597
